TPU v7x, 32 devices: a whole 2x2x4 slice. The times are simulated.
32 devices in a mesh: groups: 2 (over y), det: 4 (over z), sky: 4 (over x, core).
Axes of the slice: x: 2, y: 2, z: 4, core: 2. Of those that a mesh axis runs over, the one named last changes fastest.
Arguments:
- tod: float32 [64, 6400], P(('groups', 'det', 'sky')), parts along dimension 0, may hold values from -8 to 8, as said below
- angle: float32 [64, 6400], P(('groups', 'det', 'sky')), parts along dimension 0, may hold values from -3.140625 to 3.140625
- pixel: int32 [64, 6400], P(('groups', 'det', 'sky')), parts along dimension 0, may hold values from 0 to 127
- baseline_id: int32 [64, 6400], P(('groups', 'det', 'sky')), parts along dimension 0, may hold values from 0 to 31, never falling along the last dimension, each value on 1 to 400 neighbouring positions
- det_weight: float32 [64], P(('groups', 'det', 'sky')), parts along dimension 0, may hold values from 0.002 to 0.02
- tile_owner: int32 [64, 50, 1], P(('groups', 'det', 'sky')), parts along dimension 0, may hold values from 0 to 15; in each aligned block of 100 rows (0 to 99, 100 to 199, ..., all dimensions but the last counted through in order) at most 8 rows name the same one
- tile_slot: int32 [64, 50], P(('groups', 'det', 'sky')), parts along dimension 0, may hold values from 0 to 47
Outputs:
- offset_levels: float32 [64, 32], P(('groups', 'det', 'sky')), parts along dimension 0
- misfit_vector: float32 [64, 32], P(('groups', 'det', 'sky')), parts along dimension 0
There are 2 independent parts, one for each index of `groups`. A program takes and returns all parts, laid end to end along the dimension named above; each array names one. Nothing has to cross between parts.
Inputs may be any that keep to these rules, and one draw needn't show every extreme that they name: The tod is white noise on top of an offset that is constant over each sample block of 128 samples. `tile_owner`: within the rows of one device, at most 8 sample blocks name one sky region, a bound that some block reaches. `baseline_id`: in each detector's row the ids never fall; each baseline holds 1 to 400 samples and one holds exactly 400.
All inputs are finite; a program needn't handle non-finite values.
Results may differ from a plain program's by a relative error of at most 0.0003.
Values sent between devices are 32-bit elements; how exact they have to be, the bound alone decides.
No kernel may reach another device: no remote copies, remote signals or barrier semaphores. Data moves between devices by JAX's collectives and lax.ppermute only.
A program may use at most 64 MiB of HBM per device.

v0:
```python
import jax
import jax.numpy as jnp
from jax import lax
from jax.sharding import PartitionSpec as P

PB = 128
SB = 128
NBASE = 32
ITERS = 2


PRIOR = 0.02
HIGHEST = lax.Precision.HIGHEST


def cofactors(hit_sums):
    entry_ii = hit_sums[0] + PRIOR
    entry_iq = hit_sums[1]
    entry_iu = hit_sums[2]
    entry_qq = hit_sums[3] + PRIOR
    entry_qu = hit_sums[4]
    matrix_stokes_quad = hit_sums[5] + PRIOR
    minor_ii = entry_qq * matrix_stokes_quad - entry_qu * entry_qu
    minor_iq = entry_iu * entry_qu - entry_iq * matrix_stokes_quad
    minor_iu = entry_iq * entry_qu - entry_iu * entry_qq
    minor_qq = entry_ii * matrix_stokes_quad - entry_iu * entry_iu
    minor_qu = entry_iq * entry_iu - entry_ii * entry_qu
    minor_uu = entry_ii * entry_qq - entry_iq * entry_iq
    determinant = entry_ii * minor_ii + entry_iq * minor_iq + entry_iu * minor_iu
    return [
        minor_ii / determinant,
        minor_iq / determinant,
        minor_iu / determinant,
        minor_qq / determinant,
        minor_qu / determinant,
        minor_uu / determinant,
    ]


def solve_map(inverse, map_sums):
    first = inverse[0] * map_sums[0] + inverse[1] * map_sums[1] + inverse[2] * map_sums[2]
    second = inverse[1] * map_sums[0] + inverse[3] * map_sums[1] + inverse[4] * map_sums[2]
    third = inverse[2] * map_sums[0] + inverse[4] * map_sums[1] + inverse[5] * map_sums[2]
    return [first, second, third]


def pixel_hot(pixels):
    return (
        pixels.reshape(-1, SB)[:, :, None] == jnp.arange(PB, dtype=jnp.int32)[None, None, :]
    ).astype(jnp.float32)


def base_hot(base_ids):
    return (base_ids[:, None] == jnp.arange(NBASE, dtype=jnp.int32)[None, :]).astype(jnp.float32)


def open_routes(sums_rows, hit_rows, slot_rows):
    return (
        lax.all_to_all(sums_rows, ("det", "sky"), split_axis=0, concat_axis=0, tiled=True),
        lax.all_to_all(hit_rows, ("det", "sky"), split_axis=0, concat_axis=0, tiled=True),
        lax.all_to_all(slot_rows, ("det", "sky"), split_axis=0, concat_axis=0, tiled=True),
    )


def route_out(sums_rows):
    return lax.all_to_all(sums_rows, ("det", "sky"), split_axis=0, concat_axis=0, tiled=True)


def route_back(map_rows):
    return lax.all_to_all(map_rows, ("det", "sky"), split_axis=0, concat_axis=0, tiled=True)


def on_device(tod, angle, pixel, baseline_id, det_weight, tile_owner, tile_slot):
    detectors, samples = tod.shape
    blocks = tile_slot.shape[1]
    tile_owner_ranks = lax.axis_size(("det", "sky"))
    block_count = detectors * blocks
    capacity = block_count // tile_owner_ranks + 2
    tiles_own = 6 * capacity
    pieces = blocks // 10
    piece_rows = detectors * pieces
    piece_len = samples // pieces
    owner_flat = tile_owner.reshape(block_count)
    slot_flat = tile_slot.reshape(block_count)
    owner_match = (
        owner_flat[:, None] == jnp.arange(tile_owner_ranks, dtype=jnp.int32)[None, :]
    ).astype(jnp.int32)
    slot_rank = jnp.sum(jnp.cumsum(owner_match, axis=0) * owner_match, axis=1) - 1
    send_index = owner_flat * capacity + slot_rank
    cos_piece = jnp.cos(2.0 * angle).reshape(piece_rows, piece_len)
    sin_piece = jnp.sin(2.0 * angle).reshape(piece_rows, piece_len)
    pix_piece = pixel.reshape(piece_rows, piece_len)
    base_piece = baseline_id.reshape(piece_rows, piece_len)
    tod_piece = tod.reshape(piece_rows, piece_len)
    weight_piece = jnp.repeat(det_weight, pieces)

    def bin_signal(source, expand, with_hits):

        def bin_one_piece(inputs):
            values, pixels, base_ids, cosine, sine, weight = inputs
            signal = jnp.dot(base_hot(base_ids), values, precision=HIGHEST) if expand else values
            unity = jnp.ones_like(cosine)
            detector_channels = [weight * signal, weight * cosine * signal, weight * sine * signal]
            if with_hits:
                detector_channels = detector_channels + [
                    weight * unity,
                    weight * cosine,
                    weight * sine,
                    weight * cosine * cosine,
                    weight * cosine * sine,
                    weight * sine * sine,
                ]
            stacked = jnp.stack(detector_channels).reshape(len(detector_channels), -1, SB)
            return jnp.einsum("cbs,bsp->bcp", stacked, pixel_hot(pixels), precision=HIGHEST)

        binned = lax.map(
            bin_one_piece, (source, pix_piece, base_piece, cos_piece, sin_piece, weight_piece)
        )
        return binned.reshape(block_count, binned.shape[2], PB)

    def unbin(block_maps, source, expand):
        maps_piece = block_maps.reshape(piece_rows, -1, 3, PB)

        def unbin_one_piece(inputs):
            maps_in, values, pixels, base_ids, cosine, sine, weight = inputs
            base_table = base_hot(base_ids)
            signal = jnp.dot(base_table, values, precision=HIGHEST) if expand else values
            projected = jnp.einsum(
                "bsp,bcp->cbs", pixel_hot(pixels), maps_in, precision=HIGHEST
            ).reshape(3, -1)
            noise_weighted_signal = weight * (
                signal - projected[0] - cosine * projected[1] - sine * projected[2]
            )
            return jnp.dot(noise_weighted_signal, base_table, precision=HIGHEST)

        accumulated_totals = lax.map(
            unbin_one_piece,
            (maps_piece, source, pix_piece, base_piece, cos_piece, sin_piece, weight_piece),
        )
        return accumulated_totals.reshape(detectors, pieces, NBASE).sum(axis=1)

    def pack(block_values):
        empty = jnp.zeros((tile_owner_ranks * capacity,) + block_values.shape[1:], jnp.float32)
        return (
            empty.at[send_index]
            .set(block_values)
            .reshape((tile_owner_ranks, capacity) + block_values.shape[1:])
        )

    initial_pixel_maps = bin_signal(tod_piece, False, True)
    slot_send = (
        jnp.full((tile_owner_ranks * capacity,), tiles_own, jnp.int32)
        .at[send_index]
        .set(slot_flat)
        .reshape(tile_owner_ranks, capacity)
    )
    sums_in, hits_in, slots_in = open_routes(
        pack(initial_pixel_maps[:, :3]), pack(initial_pixel_maps[:, 3:]), slot_send
    )
    slots_in = slots_in.reshape(-1)
    safe_slots = jnp.minimum(slots_in, tiles_own - 1)

    def collect(received):
        total = jnp.zeros((tiles_own,) + received.shape[2:], jnp.float32)
        return total.at[slots_in].add(received.reshape((-1,) + received.shape[2:]), mode="drop")

    hit_tiles = collect(hits_in)
    inverse = cofactors([hit_tiles[:, channel] for channel in range(6)])

    def answer(sum_tiles):
        sky_maps = jnp.stack(
            solve_map(inverse, [sum_tiles[:, channel] for channel in range(3)]), axis=1
        )
        returned = route_back(sky_maps[safe_slots].reshape(tile_owner_ranks, capacity, 3, PB))
        return returned.reshape(tile_owner_ranks * capacity, 3, PB)[send_index]

    def operate(vector):
        repeated = jnp.repeat(vector, pieces, axis=0)
        binned = bin_signal(repeated, True, False)
        return unbin(answer(collect(route_out(pack(binned)))), repeated, True)

    system_source_vector = unbin(answer(collect(sums_in)), tod_piece, False)
    offset_levels = jnp.zeros_like(system_source_vector)
    misfit_vector = system_source_vector

    def paired(values, operator_product):
        return lax.psum(
            (jnp.sum(values * values), jnp.sum(values * operator_product)), ("det", "sky")
        )

    image = operate(misfit_vector)
    norm_now, curve = paired(misfit_vector, image)
    update_scale = norm_now / curve
    conjugate_update_vector = misfit_vector
    along = image
    for iteration in range(ITERS):
        offset_levels = offset_levels + update_scale * conjugate_update_vector
        misfit_vector = misfit_vector - update_scale * along
        if iteration + 1 < ITERS:
            image = operate(misfit_vector)
            norm_next, curve = paired(misfit_vector, image)
            ratio = norm_next / norm_now
            update_scale = norm_next / (curve - ratio * norm_next / update_scale)
            conjugate_update_vector = misfit_vector + ratio * conjugate_update_vector
            along = image + ratio * along
            norm_now = norm_next
    return (offset_levels, misfit_vector)


def solution(mesh):
    return jax.shard_map(
        on_device,
        mesh=mesh,
        in_specs=(
            P(("groups", "det", "sky"), None),
            P(("groups", "det", "sky"), None),
            P(("groups", "det", "sky"), None),
            P(("groups", "det", "sky"), None),
            P(("groups", "det", "sky")),
            P(("groups", "det", "sky"), None, None),
            P(("groups", "det", "sky"), None),
        ),
        out_specs=(P(("groups", "det", "sky"), None), P(("groups", "det", "sky"), None)),
        check_vma=False,
    )
```

profile of v0, /device:TPU:0, one launch (start us, length us, event | category | flops | bytes accessed | tf_op | source)
XLA Modules:
  0.0 391.8 jit_solution(1906904552847760112)
XLA Ops:
  3.1 0.9 scatter_custom_fusion
  4.7 7.4 %all-to-all-start = ((s32[16,1,8]{2,1,0:T(1,128)}), s32[16,1,8]{2,1,0:T(1,128)S(1)}, u32[]{:S(2)}, u32[]{:S(2)}) async-start(s32[16,1,8]{2,1,0:T(1,128)} %bitcast.36), calls=%async_computation | async-start | bytes 16384 | tf_op jit(solution)/shard_map/all_to_all | solution.py:61
  12.9 0.8 copy-done
  13.7 0.7 multiply_sine_fusion
  14.5 0.7 copy-done.2
  15.3 24.0 %while.60 = (s32[]{:T(128)}, f32[10,10,9,128]{3,2,1,0:T(8,128)S(1)}, f32[10]{0:T(128)S(1)}, f32[10,1280]{1,0:T(8,128)S(1)}, f32[10,1280]{1,0:T(8,128)S(1)}, /*in...) while((s32[]{:T(128)}, f32[10,10,9,128]{3,2,1,0:T(8,128)S(1)}, f32[10]{0:T(128)S(1)}, ...), condition=%wide.region_4.5_spmd, body=%wide.region_3.4_spmd.sunk | while | flops 17868800 | bytes 335997 | solution.py:116
  39.4 3.9 scatter_fusion.2
  44.0 6.0 %all-to-all-start.2 = ((f32[16,8,3,128]{3,1,2,0:T(8,128)}), f32[16,8,3,128]{3,1,2,0:T(8,128)S(1)}, u32[]{:S(2)}, u32[]{:S(2)}) async-start(f32[16,8,3,128]{3,1,2,0:T(8,128)} %copy.82), calls=%async_computation.2 | async-start | bytes 393216 | tf_op jit(solution)/shard_map/all_to_all | solution.py:59
  50.1 3.9 scatter_fusion
  54.0 0.8 copy.72
  54.8 4.2 %all-to-all-done.2 = f32[16,8,3,128]{3,1,2,0:T(8,128)S(1)} async-done(((f32[16,8,3,128]{3,1,2,0:T(8,128)}), f32[16,8,3,128]{3,1,2,0:T(8,128)S(1)}, u32[]{:S(2)}, u32[]{:S(2)}) %all-to-all-start.2) | async-done | bytes 196640 | tf_op jit(solution)/shard_map/all_to_all | solution.py:59
  59.0 3.6 all-to-all-start.1
  63.6 5.0 %scatter_fusion.3 = f32[48,3,128]{2,1,0:T(4,128)S(1)} fusion(f32[48,3,128]{2,1,0:T(4,128)S(1)} %broadcast.159.clone, s32[128]{0:T(128)S(1)} %get-tuple-element.540, f32[128,3,128]{2,1,0:T(4,128)S(1)} %copy.84), kind=kCustom, calls=%fused_computation.10 | custom fusion | flops 49152 | bytes 590336 | tf_op jit(solution)/shard_map/scatter-add | solution.py:165
  68.6 6.1 %all-to-all-done.1 = f32[16,8,6,128]{3,1,2,0:T(8,128)S(1)} async-done(((f32[16,8,6,128]{3,1,2,0:T(8,128)}), f32[16,8,6,128]{3,1,2,0:T(8,128)S(1)}, u32[]{:S(2)}, u32[]{:S(2)}) %all-to-all-start.1) | async-done | bytes 393248 | tf_op jit(solution)/shard_map/all_to_all | solution.py:60
  75.0 5.0 %scatter_fusion.1 = f32[48,6,128]{2,1,0:T(8,128)S(1)} fusion(f32[48,6,128]{2,1,0:T(8,128)S(1)} %broadcast_in_dim.44, s32[128]{0:T(128)S(1)} %get-tuple-element.540, f32[128,6,128]{2,1,0:T(8,128)S(1)} %copy.74), kind=kCustom, calls=%fused_computation.8 | custom fusion | flops 98304 | bytes 1180160 | tf_op jit(solution)/shard_map/scatter-add | solution.py:165
  80.3 0.7 gather_fusion
  81.7 3.7 all-to-all-start.3
  85.5 8.9 %all-to-all-done.3 = f32[16,8,3,128]{3,1,2,0:T(8,128)S(1)} async-done(((f32[16,8,3,128]{3,1,2,0:T(8,128)}), f32[16,8,3,128]{3,1,2,0:T(8,128)S(1)}, u32[]{:S(2)}, u32[]{:S(2)}) %all-to-all-start.3) | async-done | bytes 196640 | tf_op jit(solution)/shard_map/all_to_all | solution.py:70
  94.5 0.7 gather_fusion.1
  95.3 27.3 %while.61 = (s32[]{:T(128)}, f32[10,32]{1,0:T(8,128)S(1)}, f32[10]{0:T(128)S(1)}, f32[10,1280]{1,0:T(8,128)S(1)}, f32[10,10,3,128]{3,2,1,0:T(4,128)S(1)}, /*inde...) while((s32[]{:T(128)}, f32[10,32]{1,0:T(8,128)S(1)}, ...), condition=%wide.region_10.11_spmd, body=%wide.region_9.10_spmd.sunk | while | flops 6602242 | bytes 182809 | solution.py:136
  96.8 0.7 fusion.105
  99.6 0.7 fusion.105
  102.3 0.7 fusion.105
  105.0 0.7 fusion.105
  107.8 0.7 fusion.105
  110.5 0.7 fusion.105
  113.2 0.7 fusion.105
  116.0 0.7 fusion.105
  118.7 0.7 fusion.105
  121.4 0.7 fusion.105
  122.7 31.1 %while.62 = (s32[]{:T(128)}, f32[10,10,3,128]{3,2,1,0:T(4,128)S(1)}, f32[10]{0:T(128)S(1)}, s32[10,1280]{1,0:T(8,128)S(1)}, f32[10,32]{1,0:T(8,128)S(1)}, /*inde...) while((s32[]{:T(128)}, f32[10,10,3,128]{3,2,1,0:T(4,128)S(1)}, ...), condition=%wide.region_15.16_spmd, body=%wide.region_14.15_spmd.sunk | while | flops 6608642 | bytes 160393 | solution.py:116
  153.9 3.9 scatter_fusion.4
  157.8 11.6 %all_to_all.44 = f32[16,8,3,128]{3,1,2,0:T(8,128)S(1)} all-to-all(f32[16,8,3,128]{3,1,2,0:T(8,128)S(1)} %copy.98), channel_id=1, replica_groups=mesh['groups'=2,'det'=4,'sky'=4] {'det','sky'}, dimensions={0} | all-to-all | bytes 393216 | tf_op jit(solution)/shard_map/all_to_all | solution.py:66
  169.6 5.0 %scatter_fusion.5 = f32[48,3,128]{2,1,0:T(4,128)S(1)} fusion(f32[48,3,128]{2,1,0:T(4,128)S(1)} %broadcast.159.clone.1, s32[128]{0:T(128)S(1)} %get-tuple-element.540, f32[128,3,128]{2,1,0:T(4,128)S(1)} %copy.100), kind=kCustom, calls=%fused_computation.12 | custom fusion | flops 49152 | bytes 590336 | tf_op jit(solution)/shard_map/scatter-add | solution.py:165
  174.7 0.7 gather_fusion.2
  176.2 3.7 all-to-all-start.5
  179.9 8.8 %all-to-all-done.5 = f32[16,8,3,128]{3,1,2,0:T(8,128)S(1)} async-done(((f32[16,8,3,128]{3,1,2,0:T(8,128)}), f32[16,8,3,128]{3,1,2,0:T(8,128)S(1)}, u32[]{:S(2)}, u32[]{:S(2)}) %all-to-all-start.5) | async-done | bytes 196640 | tf_op jit(solution)/shard_map/all_to_all | solution.py:70
  188.8 0.7 gather_fusion.3
  189.6 31.2 %while.63 = (s32[]{:T(128)}, f32[10,32]{1,0:T(8,128)S(1)}, f32[10]{0:T(128)S(1)}, s32[10,1280]{1,0:T(8,128)S(1)}, f32[10,32]{1,0:T(8,128)S(1)}, /*index=5*/f32[1...) while((s32[]{:T(128)}, f32[10,32]{1,0:T(8,128)S(1)}, ...), condition=%wide.region_19.20_spmd, body=%wide.region_18.19_spmd.sunk | while | flops 7134722 | bytes 186393 | solution.py:136
  221.4 31.1 %all-reduce.1 = (f32[]{:T(128)}, f32[]{:T(128)}) all-reduce(f32[]{:T(128)} %get-tuple-element.363, f32[]{:T(128)} %get-tuple-element.362), channel_id=1, replica_groups=mesh['groups'=2,'det'=4,'sky'=4] {'det','sky'}, use_global_device_ids=true, to_apply=%region_13.14 | all-reduce | flops 2 | bytes 16 | tf_op jit(solution)/shard_map/psum | solution.py:187
  253.9 32.8 %while.64 = (s32[]{:T(128)}, f32[10,10,3,128]{3,2,1,0:T(4,128)S(1)}, f32[10]{0:T(128)S(1)}, s32[10,1280]{1,0:T(8,128)S(1)}, f32[10,32]{1,0:T(8,128)S(1)}, /*inde...) while((s32[]{:T(128)}, f32[10,10,3,128]{3,2,1,0:T(4,128)S(1)}, ...), condition=%wide.region_26.27_spmd, body=%wide.region_25.26_spmd.sunk | while | flops 6608642 | bytes 160393 | solution.py:116
  255.2 0.7 multiply_reduce_fusion.12
  258.4 0.7 multiply_reduce_fusion.12
  261.7 0.7 multiply_reduce_fusion.12
  265.0 0.7 multiply_reduce_fusion.12
  268.3 0.7 multiply_reduce_fusion.12
  271.5 0.7 multiply_reduce_fusion.12
  274.8 0.7 multiply_reduce_fusion.12
  278.1 0.7 multiply_reduce_fusion.12
  281.4 0.7 multiply_reduce_fusion.12
  284.7 0.7 multiply_reduce_fusion.12
  286.7 3.9 scatter_fusion.6
  290.6 11.6 %all_to_all.45 = f32[16,8,3,128]{3,1,2,0:T(8,128)S(1)} all-to-all(f32[16,8,3,128]{3,1,2,0:T(8,128)S(1)} %copy.114), channel_id=1, replica_groups=mesh['groups'=2,'det'=4,'sky'=4] {'det','sky'}, dimensions={0} | all-to-all | bytes 393216 | tf_op jit(solution)/shard_map/all_to_all | solution.py:66
  302.4 5.0 %scatter_fusion.7 = f32[48,3,128]{2,1,0:T(4,128)S(1)} fusion(f32[48,3,128]{2,1,0:T(4,128)S(1)} %broadcast.159, s32[128]{0:T(128)S(1)} %get-tuple-element.540, f32[128,3,128]{2,1,0:T(4,128)S(1)} %copy.116), kind=kCustom, calls=%fused_computation.14 | custom fusion | flops 49152 | bytes 590336 | tf_op jit(solution)/shard_map/scatter-add | solution.py:165
  307.6 0.7 gather_fusion.4
  309.0 3.5 all-to-all-start.7
  312.5 9.0 %all-to-all-done.7 = f32[16,8,3,128]{3,1,2,0:T(8,128)S(1)} async-done(((f32[16,8,3,128]{3,1,2,0:T(8,128)}), f32[16,8,3,128]{3,1,2,0:T(8,128)S(1)}, u32[]{:S(2)}, u32[]{:S(2)}) %all-to-all-start.7) | async-done | bytes 196640 | tf_op jit(solution)/shard_map/all_to_all | solution.py:70
  321.7 0.7 gather_fusion.5
  322.4 32.4 %while.65 = (s32[]{:T(128)}, f32[10,32]{1,0:T(8,128)S(1)}, f32[10]{0:T(128)S(1)}, s32[10,1280]{1,0:T(8,128)S(1)}, f32[10,32]{1,0:T(8,128)S(1)}, /*index=5*/f32[1...) while((s32[]{:T(128)}, f32[10,32]{1,0:T(8,128)S(1)}, ...), condition=%wide.region_30.31_spmd, body=%wide.region_29.30_spmd.sunk | while | flops 7134722 | bytes 186393 | solution.py:136
  324.4 0.7 fusion.121
  327.7 0.7 fusion.121
  334.2 0.7 fusion.121
  343.9 0.7 fusion.121
  355.5 31.1 %all-reduce = (f32[]{:T(128)}, f32[]{:T(128)}) all-reduce(f32[]{:T(128)} %get-tuple-element.361, f32[]{:T(128)} %get-tuple-element.360), channel_id=1, replica_groups=mesh['groups'=2,'det'=4,'sky'=4] {'det','sky'}, use_global_device_ids=true, to_apply=%region_24.25 | all-reduce | flops 2 | bytes 16 | tf_op jit(solution)/shard_map/psum | solution.py:187
  (616 shorter events, 170.3 us)
Async XLA Ops:
  0.6 0.7 copy-start.4
  2.4 0.7 copy-start.5
  2.4 10.5 %copy-start.1 = (f32[2,6400]{1,0:T(2,128)S(1)}, f32[2,6400]{1,0:T(2,128)}, u32[]{:S(2)}) copy-start(f32[2,6400]{1,0:T(2,128)} %param.19) | copy-start | bytes 153604
  4.7 39.3 %all-to-all-start = ((s32[16,1,8]{2,1,0:T(1,128)}), s32[16,1,8]{2,1,0:T(1,128)S(1)}, u32[]{:S(2)}, u32[]{:S(2)}) async-start(s32[16,1,8]{2,1,0:T(1,128)} %bitcast.36), calls=%async_computation | async-start | bytes 16384 | tf_op jit(solution)/shard_map/all_to_all | solution.py:61
  12.1 0.7 copy-start.6
  12.9 0.8 copy-start
  14.5 0.8 copy-start.2
  44.0 15.0 %all-to-all-start.2 = ((f32[16,8,3,128]{3,1,2,0:T(8,128)}), f32[16,8,3,128]{3,1,2,0:T(8,128)S(1)}, u32[]{:S(2)}, u32[]{:S(2)}) async-start(f32[16,8,3,128]{3,1,2,0:T(8,128)} %copy.82), calls=%async_computation.2 | async-start | bytes 393216 | tf_op jit(solution)/shard_map/all_to_all | solution.py:59
  59.0 15.7 %all-to-all-start.1 = ((f32[16,8,6,128]{3,1,2,0:T(8,128)}), f32[16,8,6,128]{3,1,2,0:T(8,128)S(1)}, u32[]{:S(2)}, u32[]{:S(2)}) async-start(f32[16,8,6,128]{3,1,2,0:T(8,128)} %copy.72), calls=%async_computation.1 | async-start | bytes 786432 | tf_op jit(solution)/shard_map/all_to_all | solution.py:60
  81.7 3.7 copy-start.3
  81.7 12.7 %all-to-all-start.3 = ((f32[16,8,3,128]{3,1,2,0:T(8,128)}), f32[16,8,3,128]{3,1,2,0:T(8,128)S(1)}, u32[]{:S(2)}, u32[]{:S(2)}) async-start(f32[16,8,3,128]{3,1,2,0:T(8,128)} %copy.90), calls=%async_computation.3 | async-start | bytes 393216 | tf_op jit(solution)/shard_map/all_to_all | solution.py:70
  176.2 12.5 %all-to-all-start.5 = ((f32[16,8,3,128]{3,1,2,0:T(8,128)}), f32[16,8,3,128]{3,1,2,0:T(8,128)S(1)}, u32[]{:S(2)}, u32[]{:S(2)}) async-start(f32[16,8,3,128]{3,1,2,0:T(8,128)} %copy.106), calls=%async_computation.5 | async-start | bytes 393216 | tf_op jit(solution)/shard_map/all_to_all | solution.py:70
  309.0 12.5 %all-to-all-start.7 = ((f32[16,8,3,128]{3,1,2,0:T(8,128)}), f32[16,8,3,128]{3,1,2,0:T(8,128)S(1)}, u32[]{:S(2)}, u32[]{:S(2)}) async-start(f32[16,8,3,128]{3,1,2,0:T(8,128)} %copy.122), calls=%async_computation.7 | async-start | bytes 393216 | tf_op jit(solution)/shard_map/all_to_all | solution.py:70
where the time goes:
time: 394 us; the launch traced here: 392 us
  blocking collectives  85.4 us (22%)
  local copies, waits for them, and re-layouts  83 us (21%)
  other arithmetic  78.3 us (20%)
  matrix products  69.7 us (18%)
  waiting for transfers between devices  37 us (9%)
  starting transfers between devices  27.8 us (7%)
  between operations  7.24 us (2%)
    psum x2, blocking collectives, paired(): lax.psum((jnp.sum(values * values), jnp.sum(values * operator_product)),...  62.2 us
    dynamic_slice x160, local copies, waits for them, and re-layouts, bin_signal(): lax.map(bin_one_piece, (source, pix_piece, base_piece, cos_piece, sin_pie...  41.4 us
    all_to_all x3, waiting for transfers between devices, route_back(): lax.all_to_all(map_rows, ('det', 'sky'), split_axis=0, concat_axis=0, til...  26.7 us
    all_to_all x2, blocking collectives, route_out(): lax.all_to_all(sums_rows, ('det', 'sky'), split_axis=0, concat_axis=0, ti...  23.2 us
    mul x30, other arithmetic, unbin_one_piece(): weight * (signal - projected[0] - cosine * projected[1] - sine * projecte...  20.4 us
    dot_general x30, matrix products, unbin_one_piece(): jnp.einsum('bsp,bcp->cbs', pixel_hot(pixels), maps_in, precision=HIGHEST)  20.1 us
    scatter-add x4, other arithmetic, collect(): total.at[slots_in]  19.9 us
    dot_general x30, matrix products, bin_one_piece(): jnp.einsum('cbs,bsp->bcp', stacked, pixel_hot(pixels), precision=HIGHEST)  15.7 us
  transfers between devices with their start and end apart: 6, of which 5 were waited for; matrix products, arithmetic and copies ran while one was open for 10% of the time, Pallas kernels for 0%

commit v1 on v0

v1 whole, which is shorter than its diff:
```python
import functools

import jax
import jax.numpy as jnp
from jax import lax
from jax.experimental import pallas as pl
from jax.experimental.pallas import tpu as pltpu
from jax.sharding import PartitionSpec as P

PB = 128
SB = 128
NBASE = 32
PRIOR = 0.02
PACK = 128 // NBASE
AXES = ("det", "sky")

LANE_TILE = 32
LANE_WEIGHT = 33
LANE_DET = 34
LANE_RANK = 35

f32 = jnp.float32
bf16 = jnp.bfloat16
i32 = jnp.int32


def iota(shape, axis):
    return lax.broadcasted_iota(i32, shape, axis)


def lanes_at(values, index):
    return jnp.take_along_axis(values, index, axis=1, mode="promise_in_bounds")


def split3(values):
    first = values.astype(bf16)
    rest = values - first.astype(f32)
    second = rest.astype(bf16)
    third = (rest - second.astype(f32)).astype(bf16)
    return first, second, third


def mm(left, right):
    return jnp.dot(left, right, preferred_element_type=f32)


def left_exact(left, right):
    one, two, three = split3(right)
    return (mm(left, three) + mm(left, two)) + mm(left, one)


def right_exact(left, right):
    one, two, three = split3(left)
    return (mm(three, right) + mm(two, right)) + mm(one, right)


def upper():
    return (iota((128, 128), 0) <= iota((128, 128), 1)).astype(f32).astype(bf16)


def sin_cos_double(angle):
    turns = jnp.floor(angle * 1.2732395447351628 + 0.5)
    rest = 2.0 * angle
    rest = rest - turns * 1.5703125
    rest = rest - turns * 4.837512969970703125e-4
    rest = rest - turns * 7.54978995489188216e-8
    square = rest * rest
    sine = ((-1.9515295891e-4 * square + 8.3321608736e-3) * square - 1.6666654611e-1) * square * rest + rest
    cosine = ((2.443315711809948e-5 * square - 1.388731625493765e-3) * square + 4.166664568298827e-2) * square * square - 0.5 * square + 1.0
    quadrant = turns.astype(i32) & 3
    odd = (quadrant & 1) == 1
    sin_out = jnp.where(odd, cosine, sine)
    cos_out = jnp.where(odd, sine, cosine)
    sin_out = jnp.where(quadrant >= 2, -sin_out, sin_out)
    cos_out = jnp.where((quadrant == 1) | (quadrant == 2), -cos_out, cos_out)
    return sin_out, cos_out


def pack_kernel(owners, capacity, tod_ref, angle_ref, pixel_ref, base_ref, owner_ref, tile_ref, weight_ref,
                out_ref, rows, small):
    detectors, samples = tod_ref.shape
    blocks = samples // SB
    count = detectors * blocks
    slots = owners * capacity
    for channel, ref in enumerate((tod_ref, angle_ref, pixel_ref, base_ref)):
        rows[channel, pl.ds(96, 32), :] = jnp.zeros((32, 128), f32)
        for k in range(blocks):
            piece = ref[:, k * SB:(k + 1) * SB]
            rows[channel, detectors * k:detectors * (k + 1), :] = piece.astype(f32)
    small[...] = jnp.zeros((8, 128), i32)
    small[0:detectors, 0:blocks] = owner_ref[...]
    small[detectors:2 * detectors, 0:blocks] = tile_ref[...]
    lane8 = iota((8, 128), 1)
    spread = lanes_at(small[...], lane8 >> 1)
    odd = (iota((1, 128), 1) & 1) == 1
    owner = jnp.where(odd, spread[1:2], spread[0:1])
    tile = jnp.where(odd, spread[3:4], spread[2:3])
    lane = iota((1, 128), 1)
    match = ((iota((owners, 128), 0) == owner) & (lane < count)).astype(f32)
    running = mm(match.astype(bf16), upper())
    rank = jnp.sum(match * running, axis=0, keepdims=True).astype(i32) - 1
    target = jnp.where(lane < count, owner * capacity + rank, -1)
    route = (iota((slots, 128), 0) == target).astype(f32).astype(bf16)

    base = rows[3]
    wide = iota((128, 128), 1)
    level = wide.astype(f32)
    bound = jnp.zeros((128, 128), i32)
    for step in (64, 32, 16, 8, 4, 2, 1):
        below = lanes_at(base, bound + (step - 1)) <= level
        bound = bound + jnp.where(below, step, 0)
    bound = bound + jnp.where(lanes_at(base, bound) <= level, 1, 0)
    parity = iota((128, 128), 0) & 1
    weight = jnp.where(parity == 1, weight_ref[1], weight_ref[0])
    meta = jnp.where(wide < NBASE, bound.astype(f32), 0.0)
    meta = meta + jnp.where(wide == LANE_WEIGHT, weight, 0.0)
    meta = meta + jnp.where(wide == LANE_DET, parity.astype(f32), 0.0)
    turned = jnp.where(iota((128, 128), 0) == LANE_TILE, (tile + 1).astype(f32), 0.0).astype(bf16)
    meta_out = left_exact(route, meta) + lax.dot_general(
        route, turned, (((1,), (1,)), ((), ())), preferred_element_type=f32)
    meta_out = meta_out + jnp.where(
        iota((slots, 128), 1) == LANE_RANK, (iota((slots, 128), 0) // capacity).astype(f32), 0.0)

    outs = (left_exact(route, rows[0]), left_exact(route, rows[1]), mm(route, rows[2].astype(bf16)), meta_out)
    for channel, values in enumerate(outs):
        if capacity % 8 == 0:
            out_ref[:, channel * capacity:(channel + 1) * capacity, :] = values.reshape(owners, capacity, 128)
        else:
            out_ref[channel] = values


def sort_lanes(keys):
    turned = keys.T
    part = [turned[8 * i:8 * i + 8] for i in range(16)]
    sub = iota(part[0].shape, 0)

    def across(values, mask):
        return jnp.take_along_axis(values, sub ^ mask, axis=0, mode="promise_in_bounds")

    def exchange(i, j):
        part[i], part[j] = jnp.minimum(part[i], part[j]), jnp.maximum(part[i], part[j])

    for k in range(1, 8):
        if k <= 4:
            for i in range(16):
                j = i ^ ((1 << k) - 1)
                if i < j:
                    exchange(i, j)
        else:
            mask = (1 << (k - 4)) - 1
            low = (sub & (1 << (k - 5))) == 0
            partner = [across(part[i ^ 15], mask) for i in range(16)]
            part = [jnp.where(low, jnp.minimum(a, b), jnp.maximum(a, b)) for a, b in zip(part, partner)]
        for bit in range(k - 2, -1, -1):
            if bit >= 4:
                mask = 1 << (bit - 4)
                low = (sub & mask) == 0
                partner = [across(a, mask) for a in part]
                part = [jnp.where(low, jnp.minimum(a, b), jnp.maximum(a, b)) for a, b in zip(part, partner)]
            else:
                for i in range(16):
                    if i & (1 << bit) == 0:
                        exchange(i, i | (1 << bit))
    mixed = jnp.concatenate(part, axis=0).T
    lane = iota(mixed.shape, 1)
    return lanes_at(mixed, ((lane & 15) << 3) + (lane >> 4))


def ends_to_sums(prefix, ends):
    filled = ends > 0
    at_end = jnp.where(filled, lanes_at(prefix, jnp.maximum(ends - 1, 0)), 0.0)
    before = jnp.where(iota(ends.shape, 1) == 0, 0.0, pltpu.roll(at_end, 1, 1))
    return jnp.where(filled, at_end - before, 0.0)


def cofactors(hit_sums):
    entry_ii = hit_sums[0] + PRIOR
    entry_iq = hit_sums[1]
    entry_iu = hit_sums[2]
    entry_qq = hit_sums[3] + PRIOR
    entry_qu = hit_sums[4]
    entry_uu = hit_sums[5] + PRIOR
    minor_ii = entry_qq * entry_uu - entry_qu * entry_qu
    minor_iq = entry_iu * entry_qu - entry_iq * entry_uu
    minor_iu = entry_iq * entry_qu - entry_iu * entry_qq
    minor_qq = entry_ii * entry_uu - entry_iu * entry_iu
    minor_qu = entry_iq * entry_iu - entry_ii * entry_qu
    minor_uu = entry_ii * entry_qq - entry_iq * entry_iq
    determinant = entry_ii * minor_ii + entry_iq * minor_iq + entry_iu * minor_iu
    return [minor / determinant for minor in (minor_ii, minor_iq, minor_iu, minor_qq, minor_qu, minor_uu)]


def solve_map(inverse, map_sums):
    first = inverse[0] * map_sums[0] + inverse[1] * map_sums[1] + inverse[2] * map_sums[2]
    second = inverse[1] * map_sums[0] + inverse[3] * map_sums[1] + inverse[4] * map_sums[2]
    third = inverse[2] * map_sums[0] + inverse[4] * map_sums[1] + inverse[5] * map_sums[2]
    return [first, second, third]


def vector_rows(slots, capacity, turned):
    rows = slots * 2 * NBASE // capacity // 128
    per_row = slots // rows
    if turned:
        return (iota((rows, slots), 0) == iota((rows, slots), 1) // per_row).astype(f32).astype(bf16)
    return (iota((slots, rows), 1) == iota((slots, rows), 0) // per_row).astype(f32).astype(bf16)


def map_to_baselines(capacity, map_sums, inverse, signal, slot_tile, pixel, cosine, sine, weight, bounds):
    slots = pixel.shape[0]
    sky = solve_map(inverse, map_sums)
    near = left_exact(slot_tile, jnp.concatenate(sky, axis=1))
    rest = signal - lanes_at(near[:, 0:128], pixel)
    rest = rest - cosine * lanes_at(near[:, 128:256], pixel)
    rest = rest - sine * lanes_at(near[:, 256:384], pixel)
    totals = ends_to_sums(right_exact(rest, upper()), bounds) * weight
    return left_exact(vector_rows(slots, capacity, True), totals)


def setup_kernel(owners, capacity, tiles, recv_ref, part_ref, base_ref, sbase_ref, pixel_ref, cos_ref, sin_ref,
                 wcos_ref, wsin_ref, weight_ref, ends_ref, bounds_ref, tile_slot_ref, slot_tile_ref, inv_ref, rank_ref):
    slots = owners * capacity

    def channel(number):
        if capacity % 8 == 0:
            return recv_ref[:, number * capacity:(number + 1) * capacity, :].reshape(slots, 128)
        return recv_ref[number]

    tod, angle, pixel_f, meta = channel(0), channel(1), channel(2), channel(3)
    lane = iota((slots, 128), 1)
    slot = iota((slots, 128), 0)
    pixel = pixel_f.astype(i32)
    pixel_ref[...] = pixel
    sine, cosine = sin_cos_double(angle)
    sin_ref[...] = sine
    cos_ref[...] = cosine

    def meta_lane(number):
        return lanes_at(meta, jnp.full((slots, 128), number, i32))

    weight = meta_lane(LANE_WEIGHT)
    weight_ref[...] = weight
    tile = meta_lane(LANE_TILE).astype(i32) - 1
    slot_tile = (tile == lane).astype(f32)
    slot_tile_ref[...] = slot_tile
    tile_slot = slot_tile.T
    tile_slot_ref[...] = tile_slot
    rank_ref[...] = meta_lane(LANE_RANK)[0:8]
    group = (((slot // capacity) & 1) << 1) + meta_lane(LANE_DET).astype(i32)
    bounds = jnp.where((lane >> 5) == group, lanes_at(meta, lane & 31).astype(i32), 0)
    bounds_ref[...] = bounds

    meta_i = meta.astype(i32)
    base = jnp.zeros((slots, 128), i32)
    for step in (16, 8, 4, 2, 1):
        base = base + jnp.where(lanes_at(meta_i, base + (step - 1)) <= lane, step, 0)
    base = base + (group << 5)
    base_ref[...] = base

    keys = sort_lanes(pixel_f * 128.0 + lane.astype(f32))
    order = keys.astype(i32) & 127
    limit = (lane.astype(f32) + 1.0) * 128.0
    ends = jnp.zeros((slots, 128), i32)
    for step in (64, 32, 16, 8, 4, 2, 1):
        ends = ends + jnp.where(lanes_at(keys, ends + (step - 1)) < limit, step, 0)
    ends = ends + jnp.where(lanes_at(keys, ends) < limit, 1, 0)
    ends_ref[...] = ends
    sbase_ref[...] = lanes_at(base, order)
    scos = lanes_at(cosine, order)
    ssin = lanes_at(sine, order)
    stod = lanes_at(tod, order)
    wcos_ref[...] = scos
    wsin_ref[...] = ssin

    tri = upper()
    stacked = jnp.concatenate(
        [stod, scos * stod, ssin * stod, scos, ssin, scos * scos, scos * ssin], axis=0)
    prefix = right_exact(stacked, tri)
    binned = [ends_to_sums(prefix[n * slots:(n + 1) * slots], ends) for n in range(7)]
    before = pltpu.roll(ends, 1, 1)
    hits = (ends - jnp.where(lane == 0, 0, before)).astype(f32)
    all_binned = jnp.concatenate([weight * values for values in binned + [hits]], axis=1)
    sums = left_exact(tile_slot.astype(bf16)[0:tiles], all_binned)
    sums = [sums[:, 128 * n:128 * (n + 1)] for n in range(8)]
    inverse = cofactors([sums[7], sums[3], sums[4], sums[5], sums[6], sums[7] - sums[5]])
    for number, values in enumerate(inverse):
        inv_ref[number] = values
    part = map_to_baselines(capacity, sums[0:3], inverse, tod, slot_tile.astype(bf16)[:, 0:tiles], pixel, cosine, sine,
                            weight, bounds)
    part_ref[...] = jnp.broadcast_to(part[None], part_ref.shape)


def apply_kernel(capacity, tiles, recv_ref, base_ref, sbase_ref, pixel_ref, cos_ref, sin_ref, wcos_ref, wsin_ref,
                 weight_ref, ends_ref, bounds_ref, tile_slot_ref, slot_tile_ref, inv_ref, vector_ref, part_ref):
    slots = pixel_ref.shape[0]
    vector = jnp.sum(recv_ref[...], axis=0)
    vector_ref[...] = vector
    levels = left_exact(vector_rows(slots, capacity, False), vector)
    signal = lanes_at(levels, base_ref[...])
    sorted_signal = lanes_at(levels, sbase_ref[...])
    stacked = jnp.concatenate(
        [sorted_signal, wcos_ref[...] * sorted_signal, wsin_ref[...] * sorted_signal], axis=0)
    prefix = right_exact(stacked, upper())
    ends = ends_ref[...]
    weight = weight_ref[...]
    binned = jnp.concatenate(
        [weight * ends_to_sums(prefix[n * slots:(n + 1) * slots], ends) for n in range(3)], axis=1)
    sums = left_exact(tile_slot_ref[0:tiles, :].astype(bf16), binned)
    part = map_to_baselines(
        capacity, [sums[:, 128 * n:128 * (n + 1)] for n in range(3)], [inv_ref[n] for n in range(6)], signal,
        slot_tile_ref[:, 0:tiles].astype(bf16), pixel_ref[...], cos_ref[...], sin_ref[...], weight, bounds_ref[...])
    part_ref[...] = jnp.broadcast_to(part[None], part_ref.shape)


def final_kernel(right_ref, image_ref, recv_ref, rank_ref, levels_ref, misfit_ref):
    right = right_ref[...]
    image = image_ref[...]
    twice = jnp.sum(recv_ref[...], axis=0)

    def total(values):
        return jnp.sum(jnp.sum(values, axis=0, keepdims=True), axis=1, keepdims=True)

    norm_now = total(right * right)
    scale = norm_now / total(right * image)
    misfit = right - scale * image
    norm_next = total(misfit * misfit)
    ratio = norm_next / norm_now
    direction = misfit + ratio * right
    along = (image - scale * twice) + ratio * image
    next_scale = norm_next / total(direction * along)
    levels = scale * right + next_scale * direction
    misfit = misfit - next_scale * along
    rank = rank_ref[0:1, :].astype(i32)
    mine = iota(right.shape, 0) == (rank >> 1)
    for values, ref in ((levels, levels_ref), (misfit, misfit_ref)):
        row = jnp.sum(jnp.where(mine, values, 0.0), axis=0, keepdims=True)
        row = jnp.where((rank & 1) == 1, pltpu.roll(row, 64, 1), row)
        ref[0:1, :] = row[:, 0:NBASE]
        ref[1:2, :] = pltpu.roll(row, 128 - NBASE, 1)[:, 0:NBASE]


def whole(count):
    return [pl.BlockSpec(memory_space=pltpu.VMEM)] * count


PARAMS = pltpu.CompilerParams(vmem_limit_bytes=48 * 1024 * 1024)


def exchange(parts):
    return lax.all_to_all(parts, AXES, split_axis=0, concat_axis=0, tiled=True)


def on_device(tod, angle, pixel, baseline_id, det_weight, tile_owner, tile_slot):
    detectors, samples = tod.shape
    blocks = tile_slot.shape[1]
    owners = lax.axis_size(AXES)
    capacity = detectors * blocks // owners + 2
    tiles_own = 6 * capacity
    tiles = -(-tiles_own // 8) * 8
    slots = owners * capacity
    vec_rows = owners * detectors * NBASE // 128
    direct = capacity % 8 == 0

    packed_shape = (owners, 4 * capacity, 128) if direct else (4, slots, 128)
    send = pl.pallas_call(
        functools.partial(pack_kernel, owners, capacity),
        out_shape=jax.ShapeDtypeStruct(packed_shape, f32),
        in_specs=whole(6) + [pl.BlockSpec(memory_space=pltpu.SMEM)],
        out_specs=whole(1)[0],
        scratch_shapes=[pltpu.VMEM((4, 128, 128), f32), pltpu.VMEM((8, 128), i32)],
        compiler_params=PARAMS,
        name="pack",
    )(tod, angle, pixel, baseline_id, tile_owner.reshape(detectors, blocks), tile_slot, det_weight)
    if not direct:
        send = send.reshape(4, owners, capacity, 128).transpose(1, 0, 2, 3)
    recv = exchange(send)
    if not direct:
        recv = recv.transpose(1, 0, 2, 3).reshape(4, slots, 128)

    def lanes(dtype):
        return jax.ShapeDtypeStruct((slots, 128), dtype)

    parts_shape = jax.ShapeDtypeStruct((owners, vec_rows, 128), f32)
    vector_shape = jax.ShapeDtypeStruct((vec_rows, 128), f32)
    part, *state, rank = pl.pallas_call(
        functools.partial(setup_kernel, owners, capacity, tiles),
        out_shape=(parts_shape, lanes(i32), lanes(i32), lanes(i32), lanes(f32), lanes(f32), lanes(f32), lanes(f32),
                   lanes(f32), lanes(i32), lanes(i32), jax.ShapeDtypeStruct((128, slots), f32), lanes(f32),
                   jax.ShapeDtypeStruct((6, tiles, 128), f32), jax.ShapeDtypeStruct((8, 128), f32)),
        in_specs=whole(1),
        out_specs=tuple(whole(15)),
        compiler_params=PARAMS,
        name="setup",
    )(recv)

    def apply(parts):
        return pl.pallas_call(
            functools.partial(apply_kernel, capacity, tiles),
            out_shape=(vector_shape, parts_shape),
            in_specs=whole(1 + len(state)),
            out_specs=tuple(whole(2)),
            compiler_params=PARAMS,
            name="apply",
        )(parts, *state)

    right, part = apply(exchange(part))
    image, part = apply(exchange(part))
    out = jax.ShapeDtypeStruct((detectors, NBASE), f32)
    return pl.pallas_call(
        final_kernel,
        out_shape=(out, out),
        in_specs=whole(4),
        out_specs=tuple(whole(2)),
        compiler_params=PARAMS,
        name="finish",
    )(right, image, exchange(part), rank)


def solution(mesh):
    rows = ("groups", "det", "sky")
    return jax.shard_map(
        on_device,
        mesh=mesh,
        in_specs=(P(rows, None), P(rows, None), P(rows, None), P(rows, None), P(rows), P(rows, None, None), P(rows, None)),
        out_specs=(P(rows, None), P(rows, None)),
        check_vma=False,
    )
```

time: 394 us -> 60.4 us (0.15)
  local copies, waits for them, and re-layouts: 83 us -> 4.56 us
  other arithmetic: 78.3 us -> 0 us
  matrix products: 69.7 us -> 0 us
  blocking collectives: 85.4 us -> 45.8 us
  waiting for transfers between devices: 37 us -> 0 us
  starting transfers between devices: 27.8 us -> 0 us
  Pallas kernels: 0 us -> 8.79 us
  between operations: 7.24 us -> 0.66 us
    dot_general x130 -> x0, matrix products: 69.7 us -> none  [the longest x30 20.1 us: unbin_one_piece(): jnp.einsum('bsp,bcp->cbs', pixel_hot(pixels), maps_in, precision=HIGHEST)]
    psum x2 -> x0, blocking collectives: 62.2 us -> none  [paired(): lax.psum((jnp.sum(values * values), jnp.sum(values * operator_product)),...]
    mul x70 -> x0, other arithmetic: 48 us -> none  [the longest x30 20.4 us: unbin_one_piece(): weight * (signal - projected[0] - cosine * projected[1] - sine * projecte...]
    dynamic_slice x160 -> x0, local copies, waits for them, and re-layouts: 41.4 us -> none  [bin_signal(): lax.map(bin_one_piece, (source, pix_piece, base_piece, cos_piece, sin_pie...]
    all_to_all x6 -> x0, waiting for transfers between devices: 37 us -> none  [the longest x3 26.7 us: route_back(): lax.all_to_all(map_rows, ('det', 'sky'), split_axis=0, concat_axis=0, til...]
    all_to_all x6 -> x0, starting transfers between devices: 27.8 us -> none  [the longest x3 10.9 us: route_back(): lax.all_to_all(map_rows, ('det', 'sky'), split_axis=0, concat_axis=0, til...]
    all_to_all x2 -> x4, blocking collectives: 23.2 us -> 45.8 us  [exchange(): return lax.all_to_all(parts, AXES, split_axis=0, concat_axis=0, tiled=True)]
    scatter-add x4 -> x0, other arithmetic: 19.9 us -> none  [collect(): total.at[slots_in]]
  transfers between devices with their start and end apart: 6 -> 0, of which waited for: 5 -> 0; matrix products, arithmetic and copies ran while one was open for 10% -> 0% of each run, Pallas kernels for 0% -> 0%
where the time goes in v1:
time: 60.4 us; the launch traced here: 59.8 us
  blocking collectives  45.8 us (76%)
  Pallas kernels  8.79 us (15%)
  local copies, waits for them, and re-layouts  4.56 us (8%)
  between operations  0.66 us (1%)
    all_to_all x4, blocking collectives, exchange(): return lax.all_to_all(parts, AXES, split_axis=0, concat_axis=0, tiled=True)  45.8 us
    unnamed x14, local copies, waits for them, and re-layouts  4.56 us
    pallas_call x2, Pallas kernels, apply(): pl.pallas_call(functools.partial(apply_kernel, capacity, tiles), out_shap...  3.54 us
    pallas_call x1, Pallas kernels, on_device(): pl.pallas_call(functools.partial(setup_kernel, owners, capacity, tiles),...  2.79 us
    pallas_call x1, Pallas kernels, on_device(): pl.pallas_call(functools.partial(pack_kernel, owners, capacity), out_shap...  1.48 us

profile of v1, /device:TPU:0, one launch (start us, length us, event | category | flops | bytes accessed | tf_op | source)
XLA Modules:
  0.0 59.8 jit_solution(16389388092347972019)
XLA Ops:
  0.6 0.0 copy-start.4
  0.6 0.0 copy-start.6
  0.7 0.7 %copy-done.4 = s32[2,50,1]{1,2,0:T(1,128)S(1)} copy-done((s32[2,50,1]{1,2,0:T(1,128)S(1)}, s32[2,50,1]{1,2,0:T(1,128)}, u32[]{:S(2)}) %copy-start.4) | copy-done | bytes 424
  1.3 0.0 copy-done.6
  1.3 0.0 copy-start
  1.3 0.8 %copy-done = f32[2,6400]{1,0:T(2,128)S(1)} copy-done((f32[2,6400]{1,0:T(2,128)S(1)}, f32[2,6400]{1,0:T(2,128)}, u32[]{:S(2)}) %copy-start) | copy-done | bytes 51224
  2.1 0.0 copy-start.1
  2.1 0.8 %copy-done.1 = f32[2,6400]{1,0:T(2,128)S(1)} copy-done((f32[2,6400]{1,0:T(2,128)S(1)}, f32[2,6400]{1,0:T(2,128)}, u32[]{:S(2)}) %copy-start.1) | copy-done | bytes 51224
  2.9 0.0 copy-start.2
  2.9 0.8 %copy-done.2 = s32[2,6400]{1,0:T(2,128)S(1)} copy-done((s32[2,6400]{1,0:T(2,128)S(1)}, s32[2,6400]{1,0:T(2,128)}, u32[]{:S(2)}) %copy-start.2) | copy-done | bytes 51224
  3.7 0.0 copy-start.3
  3.7 0.8 %copy-done.3 = s32[2,6400]{1,0:T(2,128)S(1)} copy-done((s32[2,6400]{1,0:T(2,128)S(1)}, s32[2,6400]{1,0:T(2,128)}, u32[]{:S(2)}) %copy-start.3) | copy-done | bytes 51224
  4.5 0.0 copy-start.5
  4.5 0.7 %copy-done.5 = s32[2,50]{1,0:T(2,128)S(1)} copy-done((s32[2,50]{1,0:T(2,128)S(1)}, s32[2,50]{1,0:T(2,128)}, u32[]{:S(2)}) %copy-start.5) | copy-done | bytes 424
  5.2 1.5 %pack.1 = f32[16,32,128]{2,1,0:T(8,128)S(1)} custom-call(f32[2,6400]{1,0:T(2,128)S(1)} %copy-done, f32[2,6400]{1,0:T(2,128)S(1)} %copy-done.1, s32[2,6400]{1,0:T(2,128)S(1)} %copy-done.2, s32[2,6400]{1,0:T(2,128)S(1)} %copy-done.3, s32[2,50]{1,0:T(2,128)S(1)} %bitcast.1, s32[2,50]{1,0:T(2,128)S(1)} %copy-done.5, f32[2]{0:T(128)S(1)} %copy-done.6), custom_call_target="tpu_custom_call" | custom-call | tf_op jit(solution)/shard_map/pack/pallas_call | solution.py:364
  6.7 17.2 %all_to_all.20.recv_ref = f32[16,32,128]{2,1,0:T(8,128)S(1)} all-to-all(f32[16,32,128]{2,1,0:T(8,128)S(1)} %pack.1), channel_id=1, replica_groups=mesh['groups'=2,'det'=4,'sky'=4] {'det','sky'}, dimensions={0} | all-to-all | bytes 524288 | tf_op jit(solution)/shard_map/all_to_all | solution.py:349
  23.9 2.8 %setup.1 = (f32[16,8,128]{2,1,0:T(8,128)S(1)}, s32[128,128]{1,0:T(8,128)S(1)}, s32[128,128]{1,0:T(8,128)S(1)}, s32[128,128]{1,0:T(8,128)S(1)}, f32[128,128]{1,0:...) custom-call(f32[16,32,128]{2,1,0:T(8,128)S(1)} %all_to_all.20.recv_ref), custom_call_target="tpu_custom_call" | custom-call | tf_op jit(solution)/shard_map/setup/pallas_call | solution.py:384
  26.7 9.7 %all_to_all.21.recv_ref = f32[16,8,128]{2,1,0:T(8,128)S(1)} all-to-all(f32[16,8,128]{2,1,0:T(8,128)S(1)} %get-tuple-element.21), channel_id=1, replica_groups=mesh['groups'=2,'det'=4,'sky'=4] {'det','sky'}, dimensions={0} | all-to-all | bytes 131072 | tf_op jit(solution)/shard_map/all_to_all | solution.py:349
  36.4 1.8 %apply.2 = (f32[8,128]{1,0:T(8,128)S(1)}, f32[16,8,128]{2,1,0:T(8,128)S(1)}) custom-call(f32[16,8,128]{2,1,0:T(8,128)S(1)} %all_to_all.21.recv_ref, s32[128,128]{1,0:T(8,128)S(1)} %get-tuple-element.22.base_ref, s32[128,128]{1,0:T(8,128)S(1)} %get-tuple-element.23.sbase_ref, s32[128,128]{1,0:T(8,128)S(1)} %get-tuple-element.24.pixel_ref, ...), custom_call_target="tpu_custom_call" | custom-call | tf_op jit(solution)/shard_map/apply/pallas_call | solution.py:396
  38.1 9.5 %all_to_all.22.recv_ref = f32[16,8,128]{2,1,0:T(8,128)S(1)} all-to-all(f32[16,8,128]{2,1,0:T(8,128)S(1)} %get-tuple-element.36), channel_id=1, replica_groups=mesh['groups'=2,'det'=4,'sky'=4] {'det','sky'}, dimensions={0} | all-to-all | bytes 131072 | tf_op jit(solution)/shard_map/all_to_all | solution.py:349
  47.6 1.8 %apply.3 = (f32[8,128]{1,0:T(8,128)S(1)}, f32[16,8,128]{2,1,0:T(8,128)S(1)}) custom-call(f32[16,8,128]{2,1,0:T(8,128)S(1)} %all_to_all.22.recv_ref, s32[128,128]{1,0:T(8,128)S(1)} %get-tuple-element.22.base_ref, s32[128,128]{1,0:T(8,128)S(1)} %get-tuple-element.23.sbase_ref, s32[128,128]{1,0:T(8,128)S(1)} %get-tuple-element.24.pixel_ref, ...), custom_call_target="tpu_custom_call" | custom-call | tf_op jit(solution)/shard_map/apply/pallas_call | solution.py:396
  49.4 9.5 %all_to_all.23.recv_ref = f32[16,8,128]{2,1,0:T(8,128)S(1)} all-to-all(f32[16,8,128]{2,1,0:T(8,128)S(1)} %get-tuple-element.38), channel_id=1, replica_groups=mesh['groups'=2,'det'=4,'sky'=4] {'det','sky'}, dimensions={0} | all-to-all | bytes 131072 | tf_op jit(solution)/shard_map/all_to_all | solution.py:349
  58.9 1.0 %finish.1 = (f32[2,32]{1,0:T(2,128)}, f32[2,32]{1,0:T(2,128)}) custom-call(f32[8,128]{1,0:T(8,128)S(1)} %get-tuple-element.35.right_ref, f32[8,128]{1,0:T(8,128)S(1)} %get-tuple-element.37.image_ref, f32[16,8,128]{2,1,0:T(8,128)S(1)} %all_to_all.23.recv_ref, f32[8,128]{1,0:T(8,128)S(1)} %get-tuple-element.39.rank_ref), custom_call_target="tpu_custom_call" | custom-call | tf_op jit(solution)/shard_map/finish/pallas_call | solution.py:408
Async XLA Ops:
  0.6 0.7 %copy-start.4 = (s32[2,50,1]{1,2,0:T(1,128)S(1)}, s32[2,50,1]{1,2,0:T(1,128)}, u32[]{:S(2)}) copy-start(s32[2,50,1]{1,2,0:T(1,128)} %param.12) | copy-start | bytes 1204
  0.6 0.7 %copy-start.6 = (f32[2]{0:T(128)S(1)}, f32[2]{0:T(128)}, u32[]{:S(2)}) copy-start(f32[2]{0:T(128)} %weight_ref.1) | copy-start | bytes 28
  1.3 0.8 %copy-start = (f32[2,6400]{1,0:T(2,128)S(1)}, f32[2,6400]{1,0:T(2,128)}, u32[]{:S(2)}) copy-start(f32[2,6400]{1,0:T(2,128)} %tod_ref.1) | copy-start | bytes 153604
  2.1 0.8 %copy-start.1 = (f32[2,6400]{1,0:T(2,128)S(1)}, f32[2,6400]{1,0:T(2,128)}, u32[]{:S(2)}) copy-start(f32[2,6400]{1,0:T(2,128)} %angle_ref.1) | copy-start | bytes 153604
  2.9 0.8 %copy-start.2 = (s32[2,6400]{1,0:T(2,128)S(1)}, s32[2,6400]{1,0:T(2,128)}, u32[]{:S(2)}) copy-start(s32[2,6400]{1,0:T(2,128)} %pixel_ref.1) | copy-start | bytes 153604
  3.7 0.8 %copy-start.3 = (s32[2,6400]{1,0:T(2,128)S(1)}, s32[2,6400]{1,0:T(2,128)}, u32[]{:S(2)}) copy-start(s32[2,6400]{1,0:T(2,128)} %base_ref.1) | copy-start | bytes 153604
  4.5 0.7 %copy-start.5 = (s32[2,50]{1,0:T(2,128)S(1)}, s32[2,50]{1,0:T(2,128)}, u32[]{:S(2)}) copy-start(s32[2,50]{1,0:T(2,128)} %tile_ref.1) | copy-start | bytes 1204

commit v2 on v1

--- a/solution.py
+++ b/solution.py
@@ -76,8 +76,15 @@
     return sin_out, cos_out
 
 
-def pack_kernel(owners, capacity, tod_ref, angle_ref, pixel_ref, base_ref, owner_ref, tile_ref, weight_ref,
-                out_ref, rows, small):
+def pack_kernel(owners, capacity, tod_hbm, angle_hbm, pixel_hbm, base_hbm, owner_hbm, tile_hbm, weight_hbm,
+                out_ref, tod_ref, angle_ref, pixel_ref, base_ref, owner_ref, tile_ref, weight_ref, rows, small, arrived):
+    pairs = ((base_hbm, base_ref), (owner_hbm, owner_ref), (tile_hbm, tile_ref), (weight_hbm, weight_ref),
+             (tod_hbm, tod_ref), (angle_hbm, angle_ref), (pixel_hbm, pixel_ref))
+    copies = [pltpu.make_async_copy(source, into, arrived.at[n]) for n, (source, into) in enumerate(pairs)]
+    for copy in copies:
+        copy.start()
+    for copy in copies:
+        copy.wait()
     detectors, samples = tod_ref.shape
     blocks = samples // SB
     count = detectors * blocks
@@ -286,13 +293,13 @@
         inv_ref[number] = values
     part = map_to_baselines(capacity, sums[0:3], inverse, tod, slot_tile.astype(bf16)[:, 0:tiles], pixel, cosine, sine,
                             weight, bounds)
-    part_ref[...] = jnp.broadcast_to(part[None], part_ref.shape)
+    part_ref[...] = part
 
 
 def apply_kernel(capacity, tiles, recv_ref, base_ref, sbase_ref, pixel_ref, cos_ref, sin_ref, wcos_ref, wsin_ref,
                  weight_ref, ends_ref, bounds_ref, tile_slot_ref, slot_tile_ref, inv_ref, vector_ref, part_ref):
     slots = pixel_ref.shape[0]
-    vector = jnp.sum(recv_ref[...], axis=0)
+    vector = recv_ref[...]
     vector_ref[...] = vector
     levels = left_exact(vector_rows(slots, capacity, False), vector)
     signal = lanes_at(levels, base_ref[...])
@@ -308,13 +315,13 @@
     part = map_to_baselines(
         capacity, [sums[:, 128 * n:128 * (n + 1)] for n in range(3)], [inv_ref[n] for n in range(6)], signal,
         slot_tile_ref[:, 0:tiles].astype(bf16), pixel_ref[...], cos_ref[...], sin_ref[...], weight, bounds_ref[...])
-    part_ref[...] = jnp.broadcast_to(part[None], part_ref.shape)
+    part_ref[...] = part
 
 
 def final_kernel(right_ref, image_ref, recv_ref, rank_ref, levels_ref, misfit_ref):
     right = right_ref[...]
     image = image_ref[...]
-    twice = jnp.sum(recv_ref[...], axis=0)
+    twice = recv_ref[...]
 
     def total(values):
         return jnp.sum(jnp.sum(values, axis=0, keepdims=True), axis=1, keepdims=True)
@@ -345,8 +352,24 @@
 PARAMS = pltpu.CompilerParams(vmem_limit_bytes=48 * 1024 * 1024)
 
 
-def exchange(parts):
-    return lax.all_to_all(parts, AXES, split_axis=0, concat_axis=0, tiled=True)
+def send_out(rows):
+    return lax.all_to_all(rows, AXES, split_axis=0, concat_axis=0, tiled=True)
+
+
+def sum_over(part, axis):
+    size = lax.axis_size(axis)
+    others = [
+        lax.ppermute(part, axis, [(source, (source + shift) % size) for source in range(size)])
+        for shift in range(1, size)]
+    for other in others:
+        part = part + other
+    return part
+
+
+def exchange(part):
+    for axis in reversed(AXES):
+        part = sum_over(part, axis)
+    return part
 
 
 def on_device(tod, angle, pixel, baseline_id, det_weight, tile_owner, tile_slot):
@@ -364,26 +387,31 @@
     send = pl.pallas_call(
         functools.partial(pack_kernel, owners, capacity),
         out_shape=jax.ShapeDtypeStruct(packed_shape, f32),
-        in_specs=whole(6) + [pl.BlockSpec(memory_space=pltpu.SMEM)],
+        in_specs=[pl.BlockSpec(memory_space=pl.ANY)] * 7,
         out_specs=whole(1)[0],
-        scratch_shapes=[pltpu.VMEM((4, 128, 128), f32), pltpu.VMEM((8, 128), i32)],
+        scratch_shapes=[
+            pltpu.VMEM((detectors, samples), f32), pltpu.VMEM((detectors, samples), f32),
+            pltpu.VMEM((detectors, samples), i32), pltpu.VMEM((detectors, samples), i32),
+            pltpu.VMEM((detectors, blocks), i32), pltpu.VMEM((detectors, blocks), i32),
+            pltpu.SMEM((detectors,), f32),
+            pltpu.VMEM((4, 128, 128), f32), pltpu.VMEM((8, 128), i32), pltpu.SemaphoreType.DMA((7,)),
+        ],
         compiler_params=PARAMS,
         name="pack",
     )(tod, angle, pixel, baseline_id, tile_owner.reshape(detectors, blocks), tile_slot, det_weight)
     if not direct:
         send = send.reshape(4, owners, capacity, 128).transpose(1, 0, 2, 3)
-    recv = exchange(send)
+    recv = send_out(send)
     if not direct:
         recv = recv.transpose(1, 0, 2, 3).reshape(4, slots, 128)
 
     def lanes(dtype):
         return jax.ShapeDtypeStruct((slots, 128), dtype)
 
-    parts_shape = jax.ShapeDtypeStruct((owners, vec_rows, 128), f32)
     vector_shape = jax.ShapeDtypeStruct((vec_rows, 128), f32)
     part, *state, rank = pl.pallas_call(
         functools.partial(setup_kernel, owners, capacity, tiles),
-        out_shape=(parts_shape, lanes(i32), lanes(i32), lanes(i32), lanes(f32), lanes(f32), lanes(f32), lanes(f32),
+        out_shape=(vector_shape, lanes(i32), lanes(i32), lanes(i32), lanes(f32), lanes(f32), lanes(f32), lanes(f32),
                    lanes(f32), lanes(i32), lanes(i32), jax.ShapeDtypeStruct((128, slots), f32), lanes(f32),
                    jax.ShapeDtypeStruct((6, tiles, 128), f32), jax.ShapeDtypeStruct((8, 128), f32)),
         in_specs=whole(1),
@@ -395,7 +423,7 @@
     def apply(parts):
         return pl.pallas_call(
             functools.partial(apply_kernel, capacity, tiles),
-            out_shape=(vector_shape, parts_shape),
+            out_shape=(vector_shape, vector_shape),
             in_specs=whole(1 + len(state)),
             out_specs=tuple(whole(2)),
             compiler_params=PARAMS,

time: 60.4 us -> 65.6 us (1.086)
  blocking collectives: 45.8 us -> 17.2 us
  waiting for transfers between devices: 0 us -> 21.6 us
  starting transfers between devices: 0 us -> 12.2 us
    all_to_all x4 -> x1, blocking collectives: 45.8 us -> 17.2 us  [send_out(): return lax.all_to_all(rows, AXES, split_axis=0, concat_axis=0, tiled=True)]
    ppermute x0 -> x18, waiting for transfers between devices: none -> 21.6 us  [sum_over(): lax.ppermute(part, axis, [(source, (source + shift) % size) for source in...]
    ppermute x0 -> x18, starting transfers between devices: none -> 12.2 us  [sum_over(): lax.ppermute(part, axis, [(source, (source + shift) % size) for source in...]
  transfers between devices with their start and end apart: 0 -> 18, of which waited for: 0 -> 16; matrix products, arithmetic and copies ran while one was open for 0% -> 0% of each run, Pallas kernels for 0% -> 0%
where the time goes in v2:
time: 65.6 us; the launch traced here: 65.2 us
  waiting for transfers between devices  21.6 us (33%)
  blocking collectives  17.2 us (26%)
  starting transfers between devices  12.2 us (19%)
  Pallas kernels  8.9 us (14%)
  local copies, waits for them, and re-layouts  4.56 us (7%)
  between operations  0.69 us (1%)
    ppermute x18, waiting for transfers between devices, sum_over(): lax.ppermute(part, axis, [(source, (source + shift) % size) for source in...  21.6 us
    all_to_all x1, blocking collectives, send_out(): return lax.all_to_all(rows, AXES, split_axis=0, concat_axis=0, tiled=True)  17.2 us
    ppermute x18, starting transfers between devices, sum_over(): lax.ppermute(part, axis, [(source, (source + shift) % size) for source in...  12.2 us
    unnamed x14, local copies, waits for them, and re-layouts  4.56 us
    pallas_call x2, Pallas kernels, apply(): pl.pallas_call(functools.partial(apply_kernel, capacity, tiles), out_shap...  3.51 us
    pallas_call x1, Pallas kernels, on_device(): pl.pallas_call(functools.partial(setup_kernel, owners, capacity, tiles),...  2.8 us
    pallas_call x1, Pallas kernels, on_device(): pl.pallas_call(functools.partial(pack_kernel, owners, capacity), out_shap...  1.61 us
  transfers between devices with their start and end apart: 18, of which 16 were waited for; matrix products, arithmetic and copies ran while one was open for 0% of the time, Pallas kernels for 0%

profile of v2, /device:TPU:0, one launch (start us, length us, event | category | flops | bytes accessed | tf_op | source)
XLA Modules:
  0.0 65.2 jit_solution(12763763879951197981)
XLA Ops:
  0.6 0.0 copy-start.4
  0.6 0.0 copy-start.6
  0.7 0.7 %copy-done.4 = s32[2,50,1]{1,2,0:T(1,128)S(1)} copy-done((s32[2,50,1]{1,2,0:T(1,128)S(1)}, s32[2,50,1]{1,2,0:T(1,128)}, u32[]{:S(2)}) %copy-start.4) | copy-done | bytes 424
  1.3 0.0 copy-done.6
  1.3 0.0 copy-start
  1.3 0.8 %copy-done = f32[2,6400]{1,0:T(2,128)S(1)} copy-done((f32[2,6400]{1,0:T(2,128)S(1)}, f32[2,6400]{1,0:T(2,128)}, u32[]{:S(2)}) %copy-start) | copy-done | bytes 51224
  2.1 0.0 copy-start.1
  2.1 0.8 %copy-done.1 = f32[2,6400]{1,0:T(2,128)S(1)} copy-done((f32[2,6400]{1,0:T(2,128)S(1)}, f32[2,6400]{1,0:T(2,128)}, u32[]{:S(2)}) %copy-start.1) | copy-done | bytes 51224
  2.9 0.0 copy-start.2
  2.9 0.8 %copy-done.2 = s32[2,6400]{1,0:T(2,128)S(1)} copy-done((s32[2,6400]{1,0:T(2,128)S(1)}, s32[2,6400]{1,0:T(2,128)}, u32[]{:S(2)}) %copy-start.2) | copy-done | bytes 51224
  3.7 0.0 copy-start.3
  3.7 0.8 %copy-done.3 = s32[2,6400]{1,0:T(2,128)S(1)} copy-done((s32[2,6400]{1,0:T(2,128)S(1)}, s32[2,6400]{1,0:T(2,128)}, u32[]{:S(2)}) %copy-start.3) | copy-done | bytes 51224
  4.5 0.0 copy-start.5
  4.5 0.7 %copy-done.5 = s32[2,50]{1,0:T(2,128)S(1)} copy-done((s32[2,50]{1,0:T(2,128)S(1)}, s32[2,50]{1,0:T(2,128)}, u32[]{:S(2)}) %copy-start.5) | copy-done | bytes 424
  5.2 1.6 %pack.1 = f32[16,32,128]{2,1,0:T(8,128)S(1)} custom-call(f32[2,6400]{1,0:T(2,128)S(1)} %copy-done, f32[2,6400]{1,0:T(2,128)S(1)} %copy-done.1, s32[2,6400]{1,0:T(2,128)S(1)} %copy-done.2, s32[2,6400]{1,0:T(2,128)S(1)} %copy-done.3, s32[2,50]{1,0:T(2,128)S(1)} %bitcast.1, s32[2,50]{1,0:T(2,128)S(1)} %copy-done.5, f32[2]{0:T(128)S(1)} %copy-done.6), custom_call_target="tpu_custom_call" | custom-call | tf_op jit(solution)/shard_map/pack/pallas_call | solution.py:387
  6.8 17.2 %all_to_all.5.recv_ref = f32[16,32,128]{2,1,0:T(8,128)S(1)} all-to-all(f32[16,32,128]{2,1,0:T(8,128)S(1)} %pack.1), channel_id=1, replica_groups=mesh['groups'=2,'det'=4,'sky'=4] {'det','sky'}, dimensions={0} | all-to-all | bytes 524288 | tf_op jit(solution)/shard_map/all_to_all | solution.py:356
  24.0 2.8 %setup.1 = (f32[8,128]{1,0:T(8,128)S(1)}, s32[128,128]{1,0:T(8,128)S(1)}, s32[128,128]{1,0:T(8,128)S(1)}, s32[128,128]{1,0:T(8,128)S(1)}, f32[128,128]{1,0:T(8,1...) custom-call(f32[16,32,128]{2,1,0:T(8,128)S(1)} %all_to_all.5.recv_ref), custom_call_target="tpu_custom_call" | custom-call | tf_op jit(solution)/shard_map/setup/pallas_call | solution.py:412
  26.8 0.2 collective-permute-start.2
  27.0 1.4 %collective-permute-start.1 = (f32[8,128]{1,0:T(8,128)S(1)}, f32[8,128]{1,0:T(8,128)S(1)}, u32[]{:S(2)}, u32[]{:S(2)}) collective-permute-start(f32[8,128]{1,0:T(8,128)S(1)} %get-tuple-element.21), channel_id=1, source_target_pairs={{0,2},{1,3},{2,0},{3,1},{4,6},{5,7},{6,4},{7,5},{8,10},{9,11},{10,... | collective-permute-start | bytes 12296 | tf_op jit(solution)/shard_map/ppermute | solution.py:362
  28.3 0.0 collective-permute-start
  28.4 0.0 collective-permute-done.2
  28.4 2.3 %collective-permute-done.1 = f32[8,128]{1,0:T(8,128)S(1)} collective-permute-done((f32[8,128]{1,0:T(8,128)S(1)}, f32[8,128]{1,0:T(8,128)S(1)}, u32[]{:S(2)}, u32[]{:S(2)}) %collective-permute-start.1) | collective-permute-done | bytes 4128 | tf_op jit(solution)/shard_map/ppermute | solution.py:362
  30.6 0.8 %collective-permute-done = f32[8,128]{1,0:T(8,128)S(1)} collective-permute-done((f32[8,128]{1,0:T(8,128)S(1)}, f32[8,128]{1,0:T(8,128)S(1)}, u32[]{:S(2)}, u32[]{:S(2)}) %collective-permute-start) | collective-permute-done | bytes 4128 | tf_op jit(solution)/shard_map/ppermute | solution.py:362
  31.4 1.5 %collective-permute-start.5 = (f32[8,128]{1,0:T(8,128)S(1)}, f32[8,128]{1,0:T(8,128)S(1)}, u32[]{:S(2)}, u32[]{:S(2)}) collective-permute-start(f32[8,128]{1,0:T(8,128)S(1)} %add_add_fusion.5), channel_id=1, source_target_pairs={{0,12},{4,0},{8,4},{12,8},{1,13},{5,1},{9,5},{13,9},{2,14},{6,2},{... | collective-permute-start | bytes 12296 | tf_op jit(solution)/shard_map/ppermute | solution.py:362
  32.9 0.8 %collective-permute-start.4 = (f32[8,128]{1,0:T(8,128)S(1)}, f32[8,128]{1,0:T(8,128)S(1)}, u32[]{:S(2)}, u32[]{:S(2)}) collective-permute-start(f32[8,128]{1,0:T(8,128)S(1)} %add_add_fusion.5), channel_id=1, source_target_pairs={{0,8},{4,12},{8,0},{12,4},{1,9},{5,13},{9,1},{13,5},{2,10},{6,14},... | collective-permute-start | bytes 12296 | tf_op jit(solution)/shard_map/ppermute | solution.py:362
  33.7 0.5 collective-permute-start.3
  34.2 0.8 %collective-permute-done.5 = f32[8,128]{1,0:T(8,128)S(1)} collective-permute-done((f32[8,128]{1,0:T(8,128)S(1)}, f32[8,128]{1,0:T(8,128)S(1)}, u32[]{:S(2)}, u32[]{:S(2)}) %collective-permute-start.5) | collective-permute-done | bytes 4128 | tf_op jit(solution)/shard_map/ppermute | solution.py:362
  35.0 2.4 %collective-permute-done.4 = f32[8,128]{1,0:T(8,128)S(1)} collective-permute-done((f32[8,128]{1,0:T(8,128)S(1)}, f32[8,128]{1,0:T(8,128)S(1)}, u32[]{:S(2)}, u32[]{:S(2)}) %collective-permute-start.4) | collective-permute-done | bytes 4128 | tf_op jit(solution)/shard_map/ppermute | solution.py:362
  37.4 1.7 %collective-permute-done.3 = f32[8,128]{1,0:T(8,128)S(1)} collective-permute-done((f32[8,128]{1,0:T(8,128)S(1)}, f32[8,128]{1,0:T(8,128)S(1)}, u32[]{:S(2)}, u32[]{:S(2)}) %collective-permute-start.3) | collective-permute-done | bytes 4128 | tf_op jit(solution)/shard_map/ppermute | solution.py:362
  39.1 1.8 %apply.2 = (f32[8,128]{1,0:T(8,128)S(1)}, f32[8,128]{1,0:T(8,128)S(1)}) custom-call(f32[8,128]{1,0:T(8,128)S(1)} %add_add_fusion.4.recv_ref, s32[128,128]{1,0:T(8,128)S(1)} %get-tuple-element.22.base_ref, s32[128,128]{1,0:T(8,128)S(1)} %get-tuple-element.23.sbase_ref, s32[128,128]{1,0:T(8,128)S(1)} %get-tuple-element.24.pixel_ref, ...), custom_call_target="tpu_custom_call" | custom-call | tf_op jit(solution)/shard_map/apply/pallas_call | solution.py:424
  40.9 0.0 collective-permute-start.8
  40.9 0.8 %collective-permute-start.7 = (f32[8,128]{1,0:T(8,128)S(1)}, f32[8,128]{1,0:T(8,128)S(1)}, u32[]{:S(2)}, u32[]{:S(2)}) collective-permute-start(f32[8,128]{1,0:T(8,128)S(1)} %get-tuple-element.36), channel_id=1, source_target_pairs={{0,2},{1,3},{2,0},{3,1},{4,6},{5,7},{6,4},{7,5},{8,10},{9,11},{10,... | collective-permute-start | bytes 12296 | tf_op jit(solution)/shard_map/ppermute | solution.py:362
  41.6 0.2 collective-permute-start.6
  41.8 0.4 collective-permute-done.8
  42.2 2.3 %collective-permute-done.7 = f32[8,128]{1,0:T(8,128)S(1)} collective-permute-done((f32[8,128]{1,0:T(8,128)S(1)}, f32[8,128]{1,0:T(8,128)S(1)}, u32[]{:S(2)}, u32[]{:S(2)}) %collective-permute-start.7) | collective-permute-done | bytes 4128 | tf_op jit(solution)/shard_map/ppermute | solution.py:362
  44.5 0.2 collective-permute-done.6
  44.7 0.2 collective-permute-start.11
  44.9 0.4 collective-permute-start.10
  45.3 2.0 %collective-permute-start.9 = (f32[8,128]{1,0:T(8,128)S(1)}, f32[8,128]{1,0:T(8,128)S(1)}, u32[]{:S(2)}, u32[]{:S(2)}) collective-permute-start(f32[8,128]{1,0:T(8,128)S(1)} %add_add_fusion.3), channel_id=1, source_target_pairs={{0,4},{4,8},{8,12},{12,0},{1,5},{5,9},{9,13},{13,1},{2,6},{6,10},{... | collective-permute-start | bytes 12296 | tf_op jit(solution)/shard_map/ppermute | solution.py:362
  47.3 1.0 %collective-permute-done.11 = f32[8,128]{1,0:T(8,128)S(1)} collective-permute-done((f32[8,128]{1,0:T(8,128)S(1)}, f32[8,128]{1,0:T(8,128)S(1)}, u32[]{:S(2)}, u32[]{:S(2)}) %collective-permute-start.11) | collective-permute-done | bytes 4128 | tf_op jit(solution)/shard_map/ppermute | solution.py:362
  48.3 1.1 %collective-permute-done.10 = f32[8,128]{1,0:T(8,128)S(1)} collective-permute-done((f32[8,128]{1,0:T(8,128)S(1)}, f32[8,128]{1,0:T(8,128)S(1)}, u32[]{:S(2)}, u32[]{:S(2)}) %collective-permute-start.10) | collective-permute-done | bytes 4128 | tf_op jit(solution)/shard_map/ppermute | solution.py:362
  49.4 1.3 %collective-permute-done.9 = f32[8,128]{1,0:T(8,128)S(1)} collective-permute-done((f32[8,128]{1,0:T(8,128)S(1)}, f32[8,128]{1,0:T(8,128)S(1)}, u32[]{:S(2)}, u32[]{:S(2)}) %collective-permute-start.9) | collective-permute-done | bytes 4128 | tf_op jit(solution)/shard_map/ppermute | solution.py:362
  50.7 1.8 %apply.3 = (f32[8,128]{1,0:T(8,128)S(1)}, f32[8,128]{1,0:T(8,128)S(1)}) custom-call(f32[8,128]{1,0:T(8,128)S(1)} %add_add_fusion.2.recv_ref, s32[128,128]{1,0:T(8,128)S(1)} %get-tuple-element.22.base_ref, s32[128,128]{1,0:T(8,128)S(1)} %get-tuple-element.23.sbase_ref, s32[128,128]{1,0:T(8,128)S(1)} %get-tuple-element.24.pixel_ref, ...), custom_call_target="tpu_custom_call" | custom-call | tf_op jit(solution)/shard_map/apply/pallas_call | solution.py:424
  52.5 0.0 collective-permute-start.14
  52.5 1.3 %collective-permute-start.13 = (f32[8,128]{1,0:T(8,128)S(1)}, f32[8,128]{1,0:T(8,128)S(1)}, u32[]{:S(2)}, u32[]{:S(2)}) collective-permute-start(f32[8,128]{1,0:T(8,128)S(1)} %get-tuple-element.38), channel_id=1, source_target_pairs={{0,2},{1,3},{2,0},{3,1},{4,6},{5,7},{6,4},{7,5},{8,10},{9,11},{10,... | collective-permute-start | bytes 12296 | tf_op jit(solution)/shard_map/ppermute | solution.py:362
  53.8 0.2 collective-permute-start.12
  54.0 0.0 collective-permute-done.14
  54.0 2.1 %collective-permute-done.13 = f32[8,128]{1,0:T(8,128)S(1)} collective-permute-done((f32[8,128]{1,0:T(8,128)S(1)}, f32[8,128]{1,0:T(8,128)S(1)}, u32[]{:S(2)}, u32[]{:S(2)}) %collective-permute-start.13) | collective-permute-done | bytes 4128 | tf_op jit(solution)/shard_map/ppermute | solution.py:362
  56.1 0.7 %collective-permute-done.12 = f32[8,128]{1,0:T(8,128)S(1)} collective-permute-done((f32[8,128]{1,0:T(8,128)S(1)}, f32[8,128]{1,0:T(8,128)S(1)}, u32[]{:S(2)}, u32[]{:S(2)}) %collective-permute-start.12) | collective-permute-done | bytes 4128 | tf_op jit(solution)/shard_map/ppermute | solution.py:362
  56.8 2.0 %collective-permute-start.17 = (f32[8,128]{1,0:T(8,128)S(1)}, f32[8,128]{1,0:T(8,128)S(1)}, u32[]{:S(2)}, u32[]{:S(2)}) collective-permute-start(f32[8,128]{1,0:T(8,128)S(1)} %add_add_fusion.1), channel_id=1, source_target_pairs={{0,12},{4,0},{8,4},{12,8},{1,13},{5,1},{9,5},{13,9},{2,14},{6,2},{... | collective-permute-start | bytes 12296 | tf_op jit(solution)/shard_map/ppermute | solution.py:362
  58.8 0.0 collective-permute-start.16
  58.8 0.8 %collective-permute-start.15 = (f32[8,128]{1,0:T(8,128)S(1)}, f32[8,128]{1,0:T(8,128)S(1)}, u32[]{:S(2)}, u32[]{:S(2)}) collective-permute-start(f32[8,128]{1,0:T(8,128)S(1)} %add_add_fusion.1), channel_id=1, source_target_pairs={{0,4},{4,8},{8,12},{12,0},{1,5},{5,9},{9,13},{13,1},{2,6},{6,10},{... | collective-permute-start | bytes 12296 | tf_op jit(solution)/shard_map/ppermute | solution.py:362
  59.6 0.8 %collective-permute-done.17 = f32[8,128]{1,0:T(8,128)S(1)} collective-permute-done((f32[8,128]{1,0:T(8,128)S(1)}, f32[8,128]{1,0:T(8,128)S(1)}, u32[]{:S(2)}, u32[]{:S(2)}) %collective-permute-start.17) | collective-permute-done | bytes 4128 | tf_op jit(solution)/shard_map/ppermute | solution.py:362
  60.4 2.9 %collective-permute-done.16 = f32[8,128]{1,0:T(8,128)S(1)} collective-permute-done((f32[8,128]{1,0:T(8,128)S(1)}, f32[8,128]{1,0:T(8,128)S(1)}, u32[]{:S(2)}, u32[]{:S(2)}) %collective-permute-start.16) | collective-permute-done | bytes 4128 | tf_op jit(solution)/shard_map/ppermute | solution.py:362
  63.3 0.9 %collective-permute-done.15 = f32[8,128]{1,0:T(8,128)S(1)} collective-permute-done((f32[8,128]{1,0:T(8,128)S(1)}, f32[8,128]{1,0:T(8,128)S(1)}, u32[]{:S(2)}, u32[]{:S(2)}) %collective-permute-start.15) | collective-permute-done | bytes 4128 | tf_op jit(solution)/shard_map/ppermute | solution.py:362
  64.2 1.0 %finish.1 = (f32[2,32]{1,0:T(2,128)}, f32[2,32]{1,0:T(2,128)}) custom-call(f32[8,128]{1,0:T(8,128)S(1)} %get-tuple-element.35.right_ref, f32[8,128]{1,0:T(8,128)S(1)} %get-tuple-element.37.image_ref, f32[8,128]{1,0:T(8,128)S(1)} %add_add_fusion.recv_ref, f32[8,128]{1,0:T(8,128)S(1)} %get-tuple-element.39.rank_ref), custom_call_target="tpu_custom_call" | custom-call | tf_op jit(solution)/shard_map/finish/pallas_call | solution.py:436
  (6 shorter events, 0.0 us)
Async XLA Ops:
  0.6 0.7 %copy-start.4 = (s32[2,50,1]{1,2,0:T(1,128)S(1)}, s32[2,50,1]{1,2,0:T(1,128)}, u32[]{:S(2)}) copy-start(s32[2,50,1]{1,2,0:T(1,128)} %param.12) | copy-start | bytes 1204
  0.6 0.7 %copy-start.6 = (f32[2]{0:T(128)S(1)}, f32[2]{0:T(128)}, u32[]{:S(2)}) copy-start(f32[2]{0:T(128)} %weight_hbm.1) | copy-start | bytes 28
  1.3 0.8 %copy-start = (f32[2,6400]{1,0:T(2,128)S(1)}, f32[2,6400]{1,0:T(2,128)}, u32[]{:S(2)}) copy-start(f32[2,6400]{1,0:T(2,128)} %tod_hbm.1) | copy-start | bytes 153604
  2.1 0.8 %copy-start.1 = (f32[2,6400]{1,0:T(2,128)S(1)}, f32[2,6400]{1,0:T(2,128)}, u32[]{:S(2)}) copy-start(f32[2,6400]{1,0:T(2,128)} %angle_hbm.1) | copy-start | bytes 153604
  2.9 0.8 %copy-start.2 = (s32[2,6400]{1,0:T(2,128)S(1)}, s32[2,6400]{1,0:T(2,128)}, u32[]{:S(2)}) copy-start(s32[2,6400]{1,0:T(2,128)} %pixel_hbm.1) | copy-start | bytes 153604
  3.7 0.8 %copy-start.3 = (s32[2,6400]{1,0:T(2,128)S(1)}, s32[2,6400]{1,0:T(2,128)}, u32[]{:S(2)}) copy-start(s32[2,6400]{1,0:T(2,128)} %base_hbm.1) | copy-start | bytes 153604
  4.5 0.7 %copy-start.5 = (s32[2,50]{1,0:T(2,128)S(1)}, s32[2,50]{1,0:T(2,128)}, u32[]{:S(2)}) copy-start(s32[2,50]{1,0:T(2,128)} %tile_hbm.1) | copy-start | bytes 1204
  26.8 1.5 %collective-permute-start.2 = (f32[8,128]{1,0:T(8,128)S(1)}, f32[8,128]{1,0:T(8,128)S(1)}, u32[]{:S(2)}, u32[]{:S(2)}) collective-permute-start(f32[8,128]{1,0:T(8,128)S(1)} %get-tuple-element.21), channel_id=1, source_target_pairs={{0,3},{1,0},{2,1},{3,2},{4,7},{5,4},{6,5},{7,6},{8,11},{9,8},{10,9... | collective-permute-start | bytes 12296 | tf_op jit(solution)/shard_map/ppermute | solution.py:362
  27.0 3.6 %collective-permute-start.1 = (f32[8,128]{1,0:T(8,128)S(1)}, f32[8,128]{1,0:T(8,128)S(1)}, u32[]{:S(2)}, u32[]{:S(2)}) collective-permute-start(f32[8,128]{1,0:T(8,128)S(1)} %get-tuple-element.21), channel_id=1, source_target_pairs={{0,2},{1,3},{2,0},{3,1},{4,6},{5,7},{6,4},{7,5},{8,10},{9,11},{10,... | collective-permute-start | bytes 12296 | tf_op jit(solution)/shard_map/ppermute | solution.py:362
  28.3 3.0 %collective-permute-start = (f32[8,128]{1,0:T(8,128)S(1)}, f32[8,128]{1,0:T(8,128)S(1)}, u32[]{:S(2)}, u32[]{:S(2)}) collective-permute-start(f32[8,128]{1,0:T(8,128)S(1)} %get-tuple-element.21), channel_id=1, source_target_pairs={{0,1},{1,2},{2,3},{3,0},{4,5},{5,6},{6,7},{7,4},{8,9},{9,10},{10,1... | collective-permute-start | bytes 12296 | tf_op jit(solution)/shard_map/ppermute | solution.py:362
  31.4 3.6 %collective-permute-start.5 = (f32[8,128]{1,0:T(8,128)S(1)}, f32[8,128]{1,0:T(8,128)S(1)}, u32[]{:S(2)}, u32[]{:S(2)}) collective-permute-start(f32[8,128]{1,0:T(8,128)S(1)} %add_add_fusion.5), channel_id=1, source_target_pairs={{0,12},{4,0},{8,4},{12,8},{1,13},{5,1},{9,5},{13,9},{2,14},{6,2},{... | collective-permute-start | bytes 12296 | tf_op jit(solution)/shard_map/ppermute | solution.py:362
  32.9 4.5 %collective-permute-start.4 = (f32[8,128]{1,0:T(8,128)S(1)}, f32[8,128]{1,0:T(8,128)S(1)}, u32[]{:S(2)}, u32[]{:S(2)}) collective-permute-start(f32[8,128]{1,0:T(8,128)S(1)} %add_add_fusion.5), channel_id=1, source_target_pairs={{0,8},{4,12},{8,0},{12,4},{1,9},{5,13},{9,1},{13,5},{2,10},{6,14},... | collective-permute-start | bytes 12296 | tf_op jit(solution)/shard_map/ppermute | solution.py:362
  33.7 5.4 %collective-permute-start.3 = (f32[8,128]{1,0:T(8,128)S(1)}, f32[8,128]{1,0:T(8,128)S(1)}, u32[]{:S(2)}, u32[]{:S(2)}) collective-permute-start(f32[8,128]{1,0:T(8,128)S(1)} %add_add_fusion.5), channel_id=1, source_target_pairs={{0,4},{4,8},{8,12},{12,0},{1,5},{5,9},{9,13},{13,1},{2,6},{6,10},{... | collective-permute-start | bytes 12296 | tf_op jit(solution)/shard_map/ppermute | solution.py:362
  40.9 1.3 %collective-permute-start.8 = (f32[8,128]{1,0:T(8,128)S(1)}, f32[8,128]{1,0:T(8,128)S(1)}, u32[]{:S(2)}, u32[]{:S(2)}) collective-permute-start(f32[8,128]{1,0:T(8,128)S(1)} %get-tuple-element.36), channel_id=1, source_target_pairs={{0,3},{1,0},{2,1},{3,2},{4,7},{5,4},{6,5},{7,6},{8,11},{9,8},{10,9... | collective-permute-start | bytes 12296 | tf_op jit(solution)/shard_map/ppermute | solution.py:362
  40.9 3.6 %collective-permute-start.7 = (f32[8,128]{1,0:T(8,128)S(1)}, f32[8,128]{1,0:T(8,128)S(1)}, u32[]{:S(2)}, u32[]{:S(2)}) collective-permute-start(f32[8,128]{1,0:T(8,128)S(1)} %get-tuple-element.36), channel_id=1, source_target_pairs={{0,2},{1,3},{2,0},{3,1},{4,6},{5,7},{6,4},{7,5},{8,10},{9,11},{10,... | collective-permute-start | bytes 12296 | tf_op jit(solution)/shard_map/ppermute | solution.py:362
  41.6 3.0 %collective-permute-start.6 = (f32[8,128]{1,0:T(8,128)S(1)}, f32[8,128]{1,0:T(8,128)S(1)}, u32[]{:S(2)}, u32[]{:S(2)}) collective-permute-start(f32[8,128]{1,0:T(8,128)S(1)} %get-tuple-element.36), channel_id=1, source_target_pairs={{0,1},{1,2},{2,3},{3,0},{4,5},{5,6},{6,7},{7,4},{8,9},{9,10},{10,1... | collective-permute-start | bytes 12296 | tf_op jit(solution)/shard_map/ppermute | solution.py:362
  44.7 3.6 %collective-permute-start.11 = (f32[8,128]{1,0:T(8,128)S(1)}, f32[8,128]{1,0:T(8,128)S(1)}, u32[]{:S(2)}, u32[]{:S(2)}) collective-permute-start(f32[8,128]{1,0:T(8,128)S(1)} %add_add_fusion.3), channel_id=1, source_target_pairs={{0,12},{4,0},{8,4},{12,8},{1,13},{5,1},{9,5},{13,9},{2,14},{6,2},{... | collective-permute-start | bytes 12296 | tf_op jit(solution)/shard_map/ppermute | solution.py:362
  44.9 4.5 %collective-permute-start.10 = (f32[8,128]{1,0:T(8,128)S(1)}, f32[8,128]{1,0:T(8,128)S(1)}, u32[]{:S(2)}, u32[]{:S(2)}) collective-permute-start(f32[8,128]{1,0:T(8,128)S(1)} %add_add_fusion.3), channel_id=1, source_target_pairs={{0,8},{4,12},{8,0},{12,4},{1,9},{5,13},{9,1},{13,5},{2,10},{6,14},... | collective-permute-start | bytes 12296 | tf_op jit(solution)/shard_map/ppermute | solution.py:362
  45.3 5.4 %collective-permute-start.9 = (f32[8,128]{1,0:T(8,128)S(1)}, f32[8,128]{1,0:T(8,128)S(1)}, u32[]{:S(2)}, u32[]{:S(2)}) collective-permute-start(f32[8,128]{1,0:T(8,128)S(1)} %add_add_fusion.3), channel_id=1, source_target_pairs={{0,4},{4,8},{8,12},{12,0},{1,5},{5,9},{9,13},{13,1},{2,6},{6,10},{... | collective-permute-start | bytes 12296 | tf_op jit(solution)/shard_map/ppermute | solution.py:362
  52.5 1.5 %collective-permute-start.14 = (f32[8,128]{1,0:T(8,128)S(1)}, f32[8,128]{1,0:T(8,128)S(1)}, u32[]{:S(2)}, u32[]{:S(2)}) collective-permute-start(f32[8,128]{1,0:T(8,128)S(1)} %get-tuple-element.38), channel_id=1, source_target_pairs={{0,3},{1,0},{2,1},{3,2},{4,7},{5,4},{6,5},{7,6},{8,11},{9,8},{10,9... | collective-permute-start | bytes 12296 | tf_op jit(solution)/shard_map/ppermute | solution.py:362
  52.5 3.6 %collective-permute-start.13 = (f32[8,128]{1,0:T(8,128)S(1)}, f32[8,128]{1,0:T(8,128)S(1)}, u32[]{:S(2)}, u32[]{:S(2)}) collective-permute-start(f32[8,128]{1,0:T(8,128)S(1)} %get-tuple-element.38), channel_id=1, source_target_pairs={{0,2},{1,3},{2,0},{3,1},{4,6},{5,7},{6,4},{7,5},{8,10},{9,11},{10,... | collective-permute-start | bytes 12296 | tf_op jit(solution)/shard_map/ppermute | solution.py:362
  53.8 3.0 %collective-permute-start.12 = (f32[8,128]{1,0:T(8,128)S(1)}, f32[8,128]{1,0:T(8,128)S(1)}, u32[]{:S(2)}, u32[]{:S(2)}) collective-permute-start(f32[8,128]{1,0:T(8,128)S(1)} %get-tuple-element.38), channel_id=1, source_target_pairs={{0,1},{1,2},{2,3},{3,0},{4,5},{5,6},{6,7},{7,4},{8,9},{9,10},{10,1... | collective-permute-start | bytes 12296 | tf_op jit(solution)/shard_map/ppermute | solution.py:362
  56.8 3.6 %collective-permute-start.17 = (f32[8,128]{1,0:T(8,128)S(1)}, f32[8,128]{1,0:T(8,128)S(1)}, u32[]{:S(2)}, u32[]{:S(2)}) collective-permute-start(f32[8,128]{1,0:T(8,128)S(1)} %add_add_fusion.1), channel_id=1, source_target_pairs={{0,12},{4,0},{8,4},{12,8},{1,13},{5,1},{9,5},{13,9},{2,14},{6,2},{... | collective-permute-start | bytes 12296 | tf_op jit(solution)/shard_map/ppermute | solution.py:362
  58.8 4.5 %collective-permute-start.16 = (f32[8,128]{1,0:T(8,128)S(1)}, f32[8,128]{1,0:T(8,128)S(1)}, u32[]{:S(2)}, u32[]{:S(2)}) collective-permute-start(f32[8,128]{1,0:T(8,128)S(1)} %add_add_fusion.1), channel_id=1, source_target_pairs={{0,8},{4,12},{8,0},{12,4},{1,9},{5,13},{9,1},{13,5},{2,10},{6,14},... | collective-permute-start | bytes 12296 | tf_op jit(solution)/shard_map/ppermute | solution.py:362
  58.8 5.4 %collective-permute-start.15 = (f32[8,128]{1,0:T(8,128)S(1)}, f32[8,128]{1,0:T(8,128)S(1)}, u32[]{:S(2)}, u32[]{:S(2)}) collective-permute-start(f32[8,128]{1,0:T(8,128)S(1)} %add_add_fusion.1), channel_id=1, source_target_pairs={{0,4},{4,8},{8,12},{12,0},{1,5},{5,9},{9,13},{13,1},{2,6},{6,10},{... | collective-permute-start | bytes 12296 | tf_op jit(solution)/shard_map/ppermute | solution.py:362

commit v3 on v2

--- a/solution.py
+++ b/solution.py
@@ -299,7 +299,7 @@
 def apply_kernel(capacity, tiles, recv_ref, base_ref, sbase_ref, pixel_ref, cos_ref, sin_ref, wcos_ref, wsin_ref,
                  weight_ref, ends_ref, bounds_ref, tile_slot_ref, slot_tile_ref, inv_ref, vector_ref, part_ref):
     slots = pixel_ref.shape[0]
-    vector = recv_ref[...]
+    vector = jnp.sum(recv_ref[...], axis=0)
     vector_ref[...] = vector
     levels = left_exact(vector_rows(slots, capacity, False), vector)
     signal = lanes_at(levels, base_ref[...])
@@ -321,7 +321,7 @@
 def final_kernel(right_ref, image_ref, recv_ref, rank_ref, levels_ref, misfit_ref):
     right = right_ref[...]
     image = image_ref[...]
-    twice = recv_ref[...]
+    twice = jnp.sum(recv_ref[...], axis=0)
 
     def total(values):
         return jnp.sum(jnp.sum(values, axis=0, keepdims=True), axis=1, keepdims=True)
@@ -349,6 +349,7 @@
     return [pl.BlockSpec(memory_space=pltpu.VMEM)] * count
 
 
+PACK_VMEM = 64 * 1024 * 1024
 PARAMS = pltpu.CompilerParams(vmem_limit_bytes=48 * 1024 * 1024)
 
 
@@ -356,20 +357,8 @@
     return lax.all_to_all(rows, AXES, split_axis=0, concat_axis=0, tiled=True)
 
 
-def sum_over(part, axis):
-    size = lax.axis_size(axis)
-    others = [
-        lax.ppermute(part, axis, [(source, (source + shift) % size) for source in range(size)])
-        for shift in range(1, size)]
-    for other in others:
-        part = part + other
-    return part
-
-
 def exchange(part):
-    for axis in reversed(AXES):
-        part = sum_over(part, axis)
-    return part
+    return lax.all_gather(part, AXES, axis=0, tiled=False)
 
 
 def on_device(tod, angle, pixel, baseline_id, det_weight, tile_owner, tile_slot):
@@ -387,7 +376,7 @@
     send = pl.pallas_call(
         functools.partial(pack_kernel, owners, capacity),
         out_shape=jax.ShapeDtypeStruct(packed_shape, f32),
-        in_specs=[pl.BlockSpec(memory_space=pl.ANY)] * 7,
+        in_specs=[pl.BlockSpec(memory_space=pltpu.HBM)] * 7,
         out_specs=whole(1)[0],
         scratch_shapes=[
             pltpu.VMEM((detectors, samples), f32), pltpu.VMEM((detectors, samples), f32),
@@ -396,7 +385,7 @@
             pltpu.SMEM((detectors,), f32),
             pltpu.VMEM((4, 128, 128), f32), pltpu.VMEM((8, 128), i32), pltpu.SemaphoreType.DMA((7,)),
         ],
-        compiler_params=PARAMS,
+        compiler_params=pltpu.CompilerParams(vmem_limit_bytes=PACK_VMEM),
         name="pack",
     )(tod, angle, pixel, baseline_id, tile_owner.reshape(detectors, blocks), tile_slot, det_weight)
     if not direct:

time: 65.6 us -> 83.7 us (1.28)
  blocking collectives: 17.2 us -> 72.8 us
  waiting for transfers between devices: 21.6 us -> 0 us
  starting transfers between devices: 12.2 us -> 0 us
  local copies, waits for them, and re-layouts: 4.56 us -> 0 us
  Pallas kernels: 8.9 us -> 9.95 us
    all_gather x0 -> x3, blocking collectives: none -> 55.4 us  [exchange(): return lax.all_gather(part, AXES, axis=0, tiled=False)]
    ppermute x18 -> x0, waiting for transfers between devices: 21.6 us -> none  [sum_over(): lax.ppermute(part, axis, [(source, (source + shift) % size) for source in...]
    ppermute x18 -> x0, starting transfers between devices: 12.2 us -> none  [sum_over(): lax.ppermute(part, axis, [(source, (source + shift) % size) for source in...]
    unnamed x14 -> x0, local copies, waits for them, and re-layouts: 4.56 us -> none
    pallas_call x1, Pallas kernels: 1.61 us -> 2.64 us  [on_device(): pl.pallas_call(functools.partial(pack_kernel, owners, capacity), out_shap...]
  transfers between devices with their start and end apart: 18 -> 0, of which waited for: 16 -> 0; matrix products, arithmetic and copies ran while one was open for 0% -> 0% of each run, Pallas kernels for 0% -> 0%
where the time goes in v3:
time: 83.7 us; the launch traced here: 83.4 us
  blocking collectives  72.8 us (87%)
  Pallas kernels  9.95 us (12%)
    all_gather x3, blocking collectives, exchange(): return lax.all_gather(part, AXES, axis=0, tiled=False)  55.4 us
    all_to_all x1, blocking collectives, send_out(): return lax.all_to_all(rows, AXES, split_axis=0, concat_axis=0, tiled=True)  17.4 us
    pallas_call x2, Pallas kernels, apply(): pl.pallas_call(functools.partial(apply_kernel, capacity, tiles), out_shap...  3.54 us
    pallas_call x1, Pallas kernels, on_device(): pl.pallas_call(functools.partial(setup_kernel, owners, capacity, tiles),...  2.8 us
    pallas_call x1, Pallas kernels, on_device(): pl.pallas_call(functools.partial(pack_kernel, owners, capacity), out_shap...  2.64 us

profile of v3, /device:TPU:0, one launch (start us, length us, event | category | flops | bytes accessed | tf_op | source)
XLA Modules:
  0.0 83.4 jit_solution(10211707813763723771)
XLA Ops:
  0.6 2.6 %pack.1 = f32[16,32,128]{2,1,0:T(8,128)} custom-call(f32[2,6400]{1,0:T(2,128)} %tod_hbm.1, f32[2,6400]{1,0:T(2,128)} %angle_hbm.1, s32[2,6400]{1,0:T(2,128)} %pixel_hbm.1, s32[2,6400]{1,0:T(2,128)} %base_hbm.1, s32[2,50]{1,0:T(2,128)} %bitcast.7, s32[2,50]{1,0:T(2,128)} %tile_hbm.1, f32[2]{0:T(128)} %weight_hbm.1), custom_call_target="tpu_custom_call" | custom-call | tf_op jit(solution)/shard_map/pack/pallas_call | solution.py:376
  3.3 17.4 %all_to_all.5.recv_ref = f32[16,32,128]{2,1,0:T(8,128)S(1)} all-to-all(f32[16,32,128]{2,1,0:T(8,128)} %pack.1), channel_id=1, replica_groups=mesh['groups'=2,'det'=4,'sky'=4] {'det','sky'}, dimensions={0} | all-to-all | bytes 524288 | tf_op jit(solution)/shard_map/all_to_all | solution.py:357
  20.7 2.8 %setup.1 = (f32[8,128]{1,0:T(8,128)S(1)}, s32[128,128]{1,0:T(8,128)S(1)}, s32[128,128]{1,0:T(8,128)S(1)}, s32[128,128]{1,0:T(8,128)S(1)}, f32[128,128]{1,0:T(8,1...) custom-call(f32[16,32,128]{2,1,0:T(8,128)S(1)} %all_to_all.5.recv_ref), custom_call_target="tpu_custom_call" | custom-call | tf_op jit(solution)/shard_map/setup/pallas_call | solution.py:401
  23.5 18.8 %all-gather = f32[128,128]{1,0:T(8,128)S(1)} all-gather(f32[8,128]{1,0:T(8,128)S(1)} %get-tuple-element.21), channel_id=2, replica_groups=mesh['groups'=2,'det'=4,'sky'=4] {'det','sky'}, dimensions={0}, use_global_device_ids=true | all-gather | bytes 69632 | tf_op jit(solution)/shard_map/all_gather | solution.py:361
  42.3 1.8 %apply.2 = (f32[8,128]{1,0:T(8,128)S(1)}, f32[8,128]{1,0:T(8,128)S(1)}) custom-call(f32[16,8,128]{2,1,0:T(8,128)S(1)} %bitcast.6, s32[128,128]{1,0:T(8,128)S(1)} %get-tuple-element.22.base_ref, s32[128,128]{1,0:T(8,128)S(1)} %get-tuple-element.23.sbase_ref, s32[128,128]{1,0:T(8,128)S(1)} %get-tuple-element.24.pixel_ref, ...), custom_call_target="tpu_custom_call" | custom-call | tf_op jit(solution)/shard_map/apply/pallas_call | solution.py:413
  44.1 17.7 %all-gather.1 = f32[128,128]{1,0:T(8,128)S(1)} all-gather(f32[8,128]{1,0:T(8,128)S(1)} %get-tuple-element.36), channel_id=3, replica_groups=mesh['groups'=2,'det'=4,'sky'=4] {'det','sky'}, dimensions={0}, use_global_device_ids=true | all-gather | bytes 69632 | tf_op jit(solution)/shard_map/all_gather | solution.py:361
  61.8 1.8 %apply.3 = (f32[8,128]{1,0:T(8,128)S(1)}, f32[8,128]{1,0:T(8,128)S(1)}) custom-call(f32[16,8,128]{2,1,0:T(8,128)S(1)} %bitcast.5, s32[128,128]{1,0:T(8,128)S(1)} %get-tuple-element.22.base_ref, s32[128,128]{1,0:T(8,128)S(1)} %get-tuple-element.23.sbase_ref, s32[128,128]{1,0:T(8,128)S(1)} %get-tuple-element.24.pixel_ref, ...), custom_call_target="tpu_custom_call" | custom-call | tf_op jit(solution)/shard_map/apply/pallas_call | solution.py:413
  63.6 18.9 %all-gather.2 = f32[128,128]{1,0:T(8,128)S(1)} all-gather(f32[8,128]{1,0:T(8,128)S(1)} %get-tuple-element.38), channel_id=4, replica_groups=mesh['groups'=2,'det'=4,'sky'=4] {'det','sky'}, dimensions={0}, use_global_device_ids=true | all-gather | bytes 69632 | tf_op jit(solution)/shard_map/all_gather | solution.py:361
  82.4 1.0 %finish.1 = (f32[2,32]{1,0:T(2,128)}, f32[2,32]{1,0:T(2,128)}) custom-call(f32[8,128]{1,0:T(8,128)S(1)} %get-tuple-element.35.right_ref, f32[8,128]{1,0:T(8,128)S(1)} %get-tuple-element.37.image_ref, f32[16,8,128]{2,1,0:T(8,128)S(1)} %bitcast.4, f32[8,128]{1,0:T(8,128)S(1)} %get-tuple-element.39.rank_ref), custom_call_target="tpu_custom_call" | custom-call | tf_op jit(solution)/shard_map/finish/pallas_call | solution.py:425

commit v4 on v3

--- a/solution.py
+++ b/solution.py
@@ -293,14 +293,12 @@
         inv_ref[number] = values
     part = map_to_baselines(capacity, sums[0:3], inverse, tod, slot_tile.astype(bf16)[:, 0:tiles], pixel, cosine, sine,
                             weight, bounds)
-    part_ref[...] = part
-
-
-def apply_kernel(capacity, tiles, recv_ref, base_ref, sbase_ref, pixel_ref, cos_ref, sin_ref, wcos_ref, wsin_ref,
-                 weight_ref, ends_ref, bounds_ref, tile_slot_ref, slot_tile_ref, inv_ref, vector_ref, part_ref):
+    part_ref[...] = jnp.broadcast_to(part[None], part_ref.shape)
+
+
+def apply(capacity, tiles, vector, base_ref, sbase_ref, pixel_ref, cos_ref, sin_ref, wcos_ref, wsin_ref,
+          weight_ref, ends_ref, bounds_ref, tile_slot_ref, slot_tile_ref, inv_ref):
     slots = pixel_ref.shape[0]
-    vector = jnp.sum(recv_ref[...], axis=0)
-    vector_ref[...] = vector
     levels = left_exact(vector_rows(slots, capacity, False), vector)
     signal = lanes_at(levels, base_ref[...])
     sorted_signal = lanes_at(levels, sbase_ref[...])
@@ -312,37 +310,55 @@
     binned = jnp.concatenate(
         [weight * ends_to_sums(prefix[n * slots:(n + 1) * slots], ends) for n in range(3)], axis=1)
     sums = left_exact(tile_slot_ref[0:tiles, :].astype(bf16), binned)
-    part = map_to_baselines(
+    return map_to_baselines(
         capacity, [sums[:, 128 * n:128 * (n + 1)] for n in range(3)], [inv_ref[n] for n in range(6)], signal,
         slot_tile_ref[:, 0:tiles].astype(bf16), pixel_ref[...], cos_ref[...], sin_ref[...], weight, bounds_ref[...])
-    part_ref[...] = part
-
-
-def final_kernel(right_ref, image_ref, recv_ref, rank_ref, levels_ref, misfit_ref):
+
+
+def total(values):
+    return jnp.sum(jnp.sum(values, axis=0, keepdims=True), axis=1, keepdims=True)
+
+
+def first_kernel(capacity, tiles, recv_ref, *refs):
+    *state, right_ref, part_ref = refs
+    right = jnp.sum(recv_ref[...], axis=0)
+    right_ref[...] = right
+    part = apply(capacity, tiles, right, *state)
+    part_ref[...] = jnp.broadcast_to(part[None], part_ref.shape)
+
+
+def second_kernel(capacity, tiles, recv_ref, right_ref, rank_ref, *refs):
+    *state, own_ref, out_ref = refs
     right = right_ref[...]
-    image = image_ref[...]
-    twice = jnp.sum(recv_ref[...], axis=0)
-
-    def total(values):
-        return jnp.sum(jnp.sum(values, axis=0, keepdims=True), axis=1, keepdims=True)
-
+    image = jnp.sum(recv_ref[...], axis=0)
     norm_now = total(right * right)
     scale = norm_now / total(right * image)
     misfit = right - scale * image
     norm_next = total(misfit * misfit)
-    ratio = norm_next / norm_now
-    direction = misfit + ratio * right
-    along = (image - scale * twice) + ratio * image
-    next_scale = norm_next / total(direction * along)
-    levels = scale * right + next_scale * direction
-    misfit = misfit - next_scale * along
+    direction = misfit + (norm_next / norm_now) * right
     rank = rank_ref[0:1, :].astype(i32)
     mine = iota(right.shape, 0) == (rank >> 1)
+    for number, values in enumerate((scale * right, direction, misfit)):
+        row = jnp.sum(jnp.where(mine, values, 0.0), axis=0, keepdims=True)
+        own_ref[number:number + 1, :] = jnp.where((rank & 1) == 1, pltpu.roll(row, 64, 1), row)
+    own_ref[3:4, :] = jnp.broadcast_to(norm_next, (1, 128))
+    part = apply(capacity, tiles, direction, *state)
+    curve = total(direction * part)
+    lane = iota((1, 128), 1)
+    turned = pltpu.roll(part, 64, 1)
+    for owner in range(out_ref.shape[0]):
+        source = part if owner % 2 == 0 else turned
+        out_ref[owner] = jnp.where(lane < 64, source[owner // 2:owner // 2 + 1], jnp.where(lane == 64, curve, 0.0))
+
+
+def final_kernel(own_ref, recv_ref, levels_ref, misfit_ref):
+    image = jnp.sum(recv_ref[...], axis=0)
+    scale = own_ref[3:4, :] / lanes_at(jnp.broadcast_to(image, (8, 128)), jnp.full((8, 128), 64, i32))[0:1]
+    levels = own_ref[0:1, :] + scale * own_ref[1:2, :]
+    misfit = own_ref[2:3, :] - scale * image
     for values, ref in ((levels, levels_ref), (misfit, misfit_ref)):
-        row = jnp.sum(jnp.where(mine, values, 0.0), axis=0, keepdims=True)
-        row = jnp.where((rank & 1) == 1, pltpu.roll(row, 64, 1), row)
-        ref[0:1, :] = row[:, 0:NBASE]
-        ref[1:2, :] = pltpu.roll(row, 128 - NBASE, 1)[:, 0:NBASE]
+        ref[0:1, :] = values[:, 0:NBASE]
+        ref[1:2, :] = pltpu.roll(values, 128 - NBASE, 1)[:, 0:NBASE]
 
 
 def whole(count):
@@ -355,10 +371,6 @@
 
 def send_out(rows):
     return lax.all_to_all(rows, AXES, split_axis=0, concat_axis=0, tiled=True)
-
-
-def exchange(part):
-    return lax.all_gather(part, AXES, axis=0, tiled=False)
 
 
 def on_device(tod, angle, pixel, baseline_id, det_weight, tile_owner, tile_slot):
@@ -398,9 +410,10 @@
         return jax.ShapeDtypeStruct((slots, 128), dtype)
 
     vector_shape = jax.ShapeDtypeStruct((vec_rows, 128), f32)
+    parts_shape = jax.ShapeDtypeStruct((owners, vec_rows, 128), f32)
     part, *state, rank = pl.pallas_call(
         functools.partial(setup_kernel, owners, capacity, tiles),
-        out_shape=(vector_shape, lanes(i32), lanes(i32), lanes(i32), lanes(f32), lanes(f32), lanes(f32), lanes(f32),
+        out_shape=(parts_shape, lanes(i32), lanes(i32), lanes(i32), lanes(f32), lanes(f32), lanes(f32), lanes(f32),
                    lanes(f32), lanes(i32), lanes(i32), jax.ShapeDtypeStruct((128, slots), f32), lanes(f32),
                    jax.ShapeDtypeStruct((6, tiles, 128), f32), jax.ShapeDtypeStruct((8, 128), f32)),
         in_specs=whole(1),
@@ -408,28 +421,31 @@
         compiler_params=PARAMS,
         name="setup",
     )(recv)
-
-    def apply(parts):
-        return pl.pallas_call(
-            functools.partial(apply_kernel, capacity, tiles),
-            out_shape=(vector_shape, vector_shape),
-            in_specs=whole(1 + len(state)),
-            out_specs=tuple(whole(2)),
-            compiler_params=PARAMS,
-            name="apply",
-        )(parts, *state)
-
-    right, part = apply(exchange(part))
-    image, part = apply(exchange(part))
+    right, part = pl.pallas_call(
+        functools.partial(first_kernel, capacity, tiles),
+        out_shape=(vector_shape, parts_shape),
+        in_specs=whole(1 + len(state)),
+        out_specs=tuple(whole(2)),
+        compiler_params=PARAMS,
+        name="first",
+    )(send_out(part), *state)
+    own, part = pl.pallas_call(
+        functools.partial(second_kernel, capacity, tiles),
+        out_shape=(jax.ShapeDtypeStruct((8, 128), f32), jax.ShapeDtypeStruct((owners, 1, 128), f32)),
+        in_specs=whole(3 + len(state)),
+        out_specs=tuple(whole(2)),
+        compiler_params=PARAMS,
+        name="second",
+    )(send_out(part), right, rank, *state)
     out = jax.ShapeDtypeStruct((detectors, NBASE), f32)
     return pl.pallas_call(
         final_kernel,
         out_shape=(out, out),
-        in_specs=whole(4),
+        in_specs=whole(2),
         out_specs=tuple(whole(2)),
         compiler_params=PARAMS,
         name="finish",
-    )(right, image, exchange(part), rank)
+    )(own, send_out(part))
 
 
 def solution(mesh):

time: 83.7 us -> 56.5 us (0.68)
  blocking collectives: 72.8 us -> 45.6 us
    all_gather x3 -> x0, blocking collectives: 55.4 us -> none  [exchange(): return lax.all_gather(part, AXES, axis=0, tiled=False)]
    all_to_all x1 -> x4, blocking collectives: 17.4 us -> 45.6 us  [send_out(): return lax.all_to_all(rows, AXES, split_axis=0, concat_axis=0, tiled=True)]
where the time goes in v4:
time: 56.5 us; the launch traced here: 56.2 us
  blocking collectives  45.6 us (81%)
  Pallas kernels  9.95 us (18%)
  between operations  0.64 us (1%)
    all_to_all x4, blocking collectives, send_out(): return lax.all_to_all(rows, AXES, split_axis=0, concat_axis=0, tiled=True)  45.6 us
    pallas_call x1, Pallas kernels, on_device(): pl.pallas_call(functools.partial(setup_kernel, owners, capacity, tiles),...  2.79 us
    pallas_call x1, Pallas kernels, on_device(): pl.pallas_call(functools.partial(pack_kernel, owners, capacity), out_shap...  2.64 us
    pallas_call x1, Pallas kernels, on_device(): pl.pallas_call(functools.partial(second_kernel, capacity, tiles), out_sha...  2.03 us
    pallas_call x1, Pallas kernels, on_device(): pl.pallas_call(functools.partial(first_kernel, capacity, tiles), out_shap...  1.77 us

profile of v4, /device:TPU:0, one launch (start us, length us, event | category | flops | bytes accessed | tf_op | source)
XLA Modules:
  0.0 56.2 jit_solution(18390911711719682032)
XLA Ops:
  0.6 2.6 %pack.1 = f32[16,32,128]{2,1,0:T(8,128)} custom-call(f32[2,6400]{1,0:T(2,128)} %tod_hbm.1, f32[2,6400]{1,0:T(2,128)} %angle_hbm.1, s32[2,6400]{1,0:T(2,128)} %pixel_hbm.1, s32[2,6400]{1,0:T(2,128)} %base_hbm.1, s32[2,50]{1,0:T(2,128)} %bitcast.1, s32[2,50]{1,0:T(2,128)} %tile_hbm.1, f32[2]{0:T(128)} %weight_hbm.1), custom_call_target="tpu_custom_call" | custom-call | tf_op jit(solution)/shard_map/pack/pallas_call | solution.py:388
  3.3 17.4 %all_to_all.20.recv_ref = f32[16,32,128]{2,1,0:T(8,128)S(1)} all-to-all(f32[16,32,128]{2,1,0:T(8,128)} %pack.1), channel_id=1, replica_groups=mesh['groups'=2,'det'=4,'sky'=4] {'det','sky'}, dimensions={0} | all-to-all | bytes 524288 | tf_op jit(solution)/shard_map/all_to_all | solution.py:373
  20.7 2.8 %setup.1 = (f32[16,8,128]{2,1,0:T(8,128)S(1)}, s32[128,128]{1,0:T(8,128)S(1)}, s32[128,128]{1,0:T(8,128)S(1)}, s32[128,128]{1,0:T(8,128)S(1)}, f32[128,128]{1,0:...) custom-call(f32[16,32,128]{2,1,0:T(8,128)S(1)} %all_to_all.20.recv_ref), custom_call_target="tpu_custom_call" | custom-call | tf_op jit(solution)/shard_map/setup/pallas_call | solution.py:414
  23.5 9.7 %all_to_all.21.recv_ref = f32[16,8,128]{2,1,0:T(8,128)S(1)} all-to-all(f32[16,8,128]{2,1,0:T(8,128)S(1)} %get-tuple-element.21), channel_id=1, replica_groups=mesh['groups'=2,'det'=4,'sky'=4] {'det','sky'}, dimensions={0} | all-to-all | bytes 131072 | tf_op jit(solution)/shard_map/all_to_all | solution.py:373
  33.2 1.8 %first.1 = (f32[8,128]{1,0:T(8,128)S(1)}, f32[16,8,128]{2,1,0:T(8,128)S(1)}) custom-call(f32[16,8,128]{2,1,0:T(8,128)S(1)} %all_to_all.21.recv_ref, s32[128,128]{1,0:T(8,128)S(1)} %get-tuple-element.22.refs_0_, s32[128,128]{1,0:T(8,128)S(1)} %get-tuple-element.23.refs_1_, s32[128,128]{1,0:T(8,128)S(1)} %get-tuple-element.24.refs_2_, ...), custom_call_target="tpu_custom_call" | custom-call | tf_op jit(solution)/shard_map/first/pallas_call | solution.py:424
  34.9 9.5 %all_to_all.22.recv_ref = f32[16,8,128]{2,1,0:T(8,128)S(1)} all-to-all(f32[16,8,128]{2,1,0:T(8,128)S(1)} %get-tuple-element.35), channel_id=1, replica_groups=mesh['groups'=2,'det'=4,'sky'=4] {'det','sky'}, dimensions={0} | all-to-all | bytes 131072 | tf_op jit(solution)/shard_map/all_to_all | solution.py:373
  44.4 2.0 %second.1 = (f32[8,128]{1,0:T(8,128)S(1)}, f32[16,1,128]{2,1,0:T(1,128)S(1)}) custom-call(f32[16,8,128]{2,1,0:T(8,128)S(1)} %all_to_all.22.recv_ref, f32[8,128]{1,0:T(8,128)S(1)} %get-tuple-element.36.right_ref, f32[8,128]{1,0:T(8,128)S(1)} %get-tuple-element.37.rank_ref, s32[128,128]{1,0:T(8,128)S(1)} %get-tuple-element.22.refs_0_, ...), custom_call_target="tpu_custom_call" | custom-call | tf_op jit(solution)/shard_map/second/pallas_call | solution.py:432
  46.4 9.0 %all_to_all.23.recv_ref = f32[16,1,128]{2,1,0:T(1,128)S(1)} all-to-all(f32[16,1,128]{2,1,0:T(1,128)S(1)} %get-tuple-element.39), channel_id=1, replica_groups=mesh['groups'=2,'det'=4,'sky'=4] {'det','sky'}, dimensions={0} | all-to-all | bytes 16384 | tf_op jit(solution)/shard_map/all_to_all | solution.py:373
  55.4 0.7 %finish.1 = (f32[2,32]{1,0:T(2,128)}, f32[2,32]{1,0:T(2,128)}) custom-call(f32[8,128]{1,0:T(8,128)S(1)} %get-tuple-element.38.own_ref, f32[16,1,128]{2,1,0:T(1,128)S(1)} %all_to_all.23.recv_ref), custom_call_target="tpu_custom_call" | custom-call | tf_op jit(solution)/shard_map/finish/pallas_call | solution.py:441

commit v5 on v4

--- a/solution.py
+++ b/solution.py
@@ -293,7 +293,7 @@
         inv_ref[number] = values
     part = map_to_baselines(capacity, sums[0:3], inverse, tod, slot_tile.astype(bf16)[:, 0:tiles], pixel, cosine, sine,
                             weight, bounds)
-    part_ref[...] = jnp.broadcast_to(part[None], part_ref.shape)
+    part_ref[...] = part
 
 
 def apply(capacity, tiles, vector, base_ref, sbase_ref, pixel_ref, cos_ref, sin_ref, wcos_ref, wsin_ref,
@@ -321,16 +321,16 @@
 
 def first_kernel(capacity, tiles, recv_ref, *refs):
     *state, right_ref, part_ref = refs
-    right = jnp.sum(recv_ref[...], axis=0)
+    right = recv_ref[...]
     right_ref[...] = right
     part = apply(capacity, tiles, right, *state)
-    part_ref[...] = jnp.broadcast_to(part[None], part_ref.shape)
+    part_ref[...] = part
 
 
 def second_kernel(capacity, tiles, recv_ref, right_ref, rank_ref, *refs):
     *state, own_ref, out_ref = refs
     right = right_ref[...]
-    image = jnp.sum(recv_ref[...], axis=0)
+    image = recv_ref[...]
     norm_now = total(right * right)
     scale = norm_now / total(right * image)
     misfit = right - scale * image
@@ -371,6 +371,23 @@
 
 def send_out(rows):
     return lax.all_to_all(rows, AXES, split_axis=0, concat_axis=0, tiled=True)
+
+
+def by_pairs(part):
+    for axis in reversed(AXES):
+        size = lax.axis_size(axis)
+        bit = 1
+        while bit < size:
+            part = part + lax.ppermute(part, axis, [(source, source ^ bit) for source in range(size)])
+            bit *= 2
+    return part
+
+
+def by_axes(part):
+    for axis in reversed(AXES):
+        copies = jnp.broadcast_to(part[None], (lax.axis_size(axis),) + part.shape)
+        part = jnp.sum(lax.all_to_all(copies, axis, split_axis=0, concat_axis=0, tiled=True), axis=0)
+    return part
 
 
 def on_device(tod, angle, pixel, baseline_id, det_weight, tile_owner, tile_slot):
@@ -410,10 +427,9 @@
         return jax.ShapeDtypeStruct((slots, 128), dtype)
 
     vector_shape = jax.ShapeDtypeStruct((vec_rows, 128), f32)
-    parts_shape = jax.ShapeDtypeStruct((owners, vec_rows, 128), f32)
     part, *state, rank = pl.pallas_call(
         functools.partial(setup_kernel, owners, capacity, tiles),
-        out_shape=(parts_shape, lanes(i32), lanes(i32), lanes(i32), lanes(f32), lanes(f32), lanes(f32), lanes(f32),
+        out_shape=(vector_shape, lanes(i32), lanes(i32), lanes(i32), lanes(f32), lanes(f32), lanes(f32), lanes(f32),
                    lanes(f32), lanes(i32), lanes(i32), jax.ShapeDtypeStruct((128, slots), f32), lanes(f32),
                    jax.ShapeDtypeStruct((6, tiles, 128), f32), jax.ShapeDtypeStruct((8, 128), f32)),
         in_specs=whole(1),
@@ -423,12 +439,12 @@
     )(recv)
     right, part = pl.pallas_call(
         functools.partial(first_kernel, capacity, tiles),
-        out_shape=(vector_shape, parts_shape),
+        out_shape=(vector_shape, vector_shape),
         in_specs=whole(1 + len(state)),
         out_specs=tuple(whole(2)),
         compiler_params=PARAMS,
         name="first",
-    )(send_out(part), *state)
+    )(by_pairs(part), *state)
     own, part = pl.pallas_call(
         functools.partial(second_kernel, capacity, tiles),
         out_shape=(jax.ShapeDtypeStruct((8, 128), f32), jax.ShapeDtypeStruct((owners, 1, 128), f32)),
@@ -436,7 +452,7 @@
         out_specs=tuple(whole(2)),
         compiler_params=PARAMS,
         name="second",
-    )(send_out(part), right, rank, *state)
+    )(by_axes(part), right, rank, *state)
     out = jax.ShapeDtypeStruct((detectors, NBASE), f32)
     return pl.pallas_call(
         final_kernel,

time: 56.5 us -> 64.5 us (1.14)
  waiting for transfers between devices: 0 us -> 11.3 us
  blocking collectives: 45.6 us -> 40.6 us
  starting transfers between devices: 0 us -> 1.66 us
    all_to_all x4 -> x2, blocking collectives: 45.6 us -> 26.4 us  [send_out(): return lax.all_to_all(rows, AXES, split_axis=0, concat_axis=0, tiled=True)]
    all_to_all x0 -> x2, blocking collectives: none -> 14.2 us  [by_axes(): lax.all_to_all(copies, axis, split_axis=0, concat_axis=0, tiled=True)]
    ppermute x0 -> x4, waiting for transfers between devices: none -> 11.3 us  [by_pairs(): lax.ppermute(part, axis, [(source, source ^ bit) for source in range(size)])]
    ppermute x0 -> x4, starting transfers between devices: none -> 1.66 us  [by_pairs(): lax.ppermute(part, axis, [(source, source ^ bit) for source in range(size)])]
  transfers between devices with their start and end apart: 0 -> 4, of which waited for: 0 -> 4; matrix products, arithmetic and copies ran while one was open for 0% -> 0% of each run, Pallas kernels for 0% -> 0%
where the time goes in v5:
time: 64.5 us; the launch traced here: 64.1 us
  blocking collectives  40.6 us (63%)
  waiting for transfers between devices  11.3 us (18%)
  Pallas kernels  9.92 us (15%)
  starting transfers between devices  1.66 us (3%)
  between operations  0.66 us (1%)
    all_to_all x2, blocking collectives, send_out(): return lax.all_to_all(rows, AXES, split_axis=0, concat_axis=0, tiled=True)  26.4 us
    all_to_all x2, blocking collectives, by_axes(): lax.all_to_all(copies, axis, split_axis=0, concat_axis=0, tiled=True)  14.2 us
    ppermute x4, waiting for transfers between devices, by_pairs(): lax.ppermute(part, axis, [(source, source ^ bit) for source in range(size)])  11.3 us
    pallas_call x1, Pallas kernels, on_device(): pl.pallas_call(functools.partial(setup_kernel, owners, capacity, tiles),...  2.79 us
    pallas_call x1, Pallas kernels, on_device(): pl.pallas_call(functools.partial(pack_kernel, owners, capacity), out_shap...  2.64 us
    pallas_call x1, Pallas kernels, on_device(): pl.pallas_call(functools.partial(second_kernel, capacity, tiles), out_sha...  2.02 us
    pallas_call x1, Pallas kernels, on_device(): pl.pallas_call(functools.partial(first_kernel, capacity, tiles), out_shap...  1.75 us
    ppermute x4, starting transfers between devices, by_pairs(): lax.ppermute(part, axis, [(source, source ^ bit) for source in range(size)])  1.66 us
  transfers between devices with their start and end apart: 4, of which 4 were waited for; matrix products, arithmetic and copies ran while one was open for 0% of the time, Pallas kernels for 0%

profile of v5, /device:TPU:0, one launch (start us, length us, event | category | flops | bytes accessed | tf_op | source)
XLA Modules:
  0.0 64.1 jit_solution(4849021256109263788)
XLA Ops:
  0.6 2.6 %pack.1 = f32[16,32,128]{2,1,0:T(8,128)} custom-call(f32[2,6400]{1,0:T(2,128)} %tod_hbm.1, f32[2,6400]{1,0:T(2,128)} %angle_hbm.1, s32[2,6400]{1,0:T(2,128)} %pixel_hbm.1, s32[2,6400]{1,0:T(2,128)} %base_hbm.1, s32[2,50]{1,0:T(2,128)} %bitcast.1, s32[2,50]{1,0:T(2,128)} %tile_hbm.1, f32[2]{0:T(128)} %weight_hbm.1), custom_call_target="tpu_custom_call" | custom-call | tf_op jit(solution)/shard_map/pack/pallas_call | solution.py:405
  3.3 17.4 %all_to_all.20.recv_ref = f32[16,32,128]{2,1,0:T(8,128)S(1)} all-to-all(f32[16,32,128]{2,1,0:T(8,128)} %pack.1), channel_id=1, replica_groups=mesh['groups'=2,'det'=4,'sky'=4] {'det','sky'}, dimensions={0} | all-to-all | bytes 524288 | tf_op jit(solution)/shard_map/all_to_all | solution.py:373
  20.7 2.8 %setup.1 = (f32[8,128]{1,0:T(8,128)S(1)}, s32[128,128]{1,0:T(8,128)S(1)}, s32[128,128]{1,0:T(8,128)S(1)}, s32[128,128]{1,0:T(8,128)S(1)}, f32[128,128]{1,0:T(8,1...) custom-call(f32[16,32,128]{2,1,0:T(8,128)S(1)} %all_to_all.20.recv_ref), custom_call_target="tpu_custom_call" | custom-call | tf_op jit(solution)/shard_map/setup/pallas_call | solution.py:430
  23.5 0.0 collective-permute-start
  23.5 1.2 %collective-permute-done = f32[8,128]{1,0:T(8,128)S(1)} collective-permute-done((f32[8,128]{1,0:T(8,128)S(1)}, f32[8,128]{1,0:T(8,128)S(1)}, u32[]{:S(2)}, u32[]{:S(2)}) %collective-permute-start) | collective-permute-done | bytes 4128 | tf_op jit(solution)/shard_map/ppermute | solution.py:381
  24.7 0.2 collective-permute-start.1
  24.9 3.4 %collective-permute-done.1 = f32[8,128]{1,0:T(8,128)S(1)} collective-permute-done((f32[8,128]{1,0:T(8,128)S(1)}, f32[8,128]{1,0:T(8,128)S(1)}, u32[]{:S(2)}, u32[]{:S(2)}) %collective-permute-start.1) | collective-permute-done | bytes 4128 | tf_op jit(solution)/shard_map/ppermute | solution.py:381
  28.3 0.4 collective-permute-start.2
  28.7 3.2 %collective-permute-done.2 = f32[8,128]{1,0:T(8,128)S(1)} collective-permute-done((f32[8,128]{1,0:T(8,128)S(1)}, f32[8,128]{1,0:T(8,128)S(1)}, u32[]{:S(2)}, u32[]{:S(2)}) %collective-permute-start.2) | collective-permute-done | bytes 4128 | tf_op jit(solution)/shard_map/ppermute | solution.py:381
  31.9 1.1 %collective-permute-start.3 = (f32[8,128]{1,0:T(8,128)S(1)}, f32[8,128]{1,0:T(8,128)S(1)}, u32[]{:S(2)}, u32[]{:S(2)}) collective-permute-start(f32[8,128]{1,0:T(8,128)S(1)} %add.14), channel_id=1, source_target_pairs={{0,8},{4,12},{8,0},{12,4},{1,9},{5,13},{9,1},{13,5},{2,10},{6,14},... | collective-permute-start | bytes 12296 | tf_op jit(solution)/shard_map/ppermute | solution.py:381
  33.0 3.4 %collective-permute-done.3 = f32[8,128]{1,0:T(8,128)S(1)} collective-permute-done((f32[8,128]{1,0:T(8,128)S(1)}, f32[8,128]{1,0:T(8,128)S(1)}, u32[]{:S(2)}, u32[]{:S(2)}) %collective-permute-start.3) | collective-permute-done | bytes 4128 | tf_op jit(solution)/shard_map/ppermute | solution.py:381
  36.4 1.8 %first.1 = (f32[8,128]{1,0:T(8,128)S(1)}, f32[8,128]{1,0:T(8,128)S(1)}) custom-call(f32[8,128]{1,0:T(8,128)S(1)} %add.15.recv_ref, s32[128,128]{1,0:T(8,128)S(1)} %get-tuple-element.22.refs_0_, s32[128,128]{1,0:T(8,128)S(1)} %get-tuple-element.23.refs_1_, s32[128,128]{1,0:T(8,128)S(1)} %get-tuple-element.24.refs_2_, ...), custom_call_target="tpu_custom_call" | custom-call | tf_op jit(solution)/shard_map/first/pallas_call | solution.py:440
  38.2 6.2 %all_to_all.21 = f32[4,8,128]{2,1,0:T(8,128)S(1)} all-to-all(f32[4,8,128]{2,1,0:T(8,128)S(1)} %broadcast_in_dim.4), channel_id=1, replica_groups=mesh['groups'=2,'det'=4,'sky'=4] {'sky'}, dimensions={0} | all-to-all | bytes 32768 | tf_op jit(solution)/shard_map/all_to_all | solution.py:389
  44.4 8.0 %all_to_all.22 = f32[4,8,128]{2,1,0:T(8,128)S(1)} all-to-all(f32[4,8,128]{2,1,0:T(8,128)S(1)} %broadcast_in_dim.5), channel_id=1, replica_groups=mesh['groups'=2,'det'=4,'sky'=4] {'det'}, dimensions={0} | all-to-all | bytes 32768 | tf_op jit(solution)/shard_map/all_to_all | solution.py:389
  52.4 2.0 %second.1 = (f32[8,128]{1,0:T(8,128)S(1)}, f32[16,1,128]{2,1,0:T(1,128)S(1)}) custom-call(f32[8,128]{1,0:T(8,128)S(1)} %reduce_sum.19.recv_ref, f32[8,128]{1,0:T(8,128)S(1)} %get-tuple-element.36.right_ref, f32[8,128]{1,0:T(8,128)S(1)} %get-tuple-element.37.rank_ref, s32[128,128]{1,0:T(8,128)S(1)} %get-tuple-element.22.refs_0_, ...), custom_call_target="tpu_custom_call" | custom-call | tf_op jit(solution)/shard_map/second/pallas_call | solution.py:448
  54.4 9.0 %all_to_all.23.recv_ref = f32[16,1,128]{2,1,0:T(1,128)S(1)} all-to-all(f32[16,1,128]{2,1,0:T(1,128)S(1)} %get-tuple-element.39), channel_id=1, replica_groups=mesh['groups'=2,'det'=4,'sky'=4] {'det','sky'}, dimensions={0} | all-to-all | bytes 16384 | tf_op jit(solution)/shard_map/all_to_all | solution.py:373
  63.4 0.7 %finish.1 = (f32[2,32]{1,0:T(2,128)}, f32[2,32]{1,0:T(2,128)}) custom-call(f32[8,128]{1,0:T(8,128)S(1)} %get-tuple-element.38.own_ref, f32[16,1,128]{2,1,0:T(1,128)S(1)} %all_to_all.23.recv_ref), custom_call_target="tpu_custom_call" | custom-call | tf_op jit(solution)/shard_map/finish/pallas_call | solution.py:457
  (8 shorter events, 0.0 us)
Async XLA Ops:
  23.5 1.2 %collective-permute-start = (f32[8,128]{1,0:T(8,128)S(1)}, f32[8,128]{1,0:T(8,128)S(1)}, u32[]{:S(2)}, u32[]{:S(2)}) collective-permute-start(f32[8,128]{1,0:T(8,128)S(1)} %get-tuple-element.21), channel_id=1, source_target_pairs={{0,1},{1,0},{2,3},{3,2},{4,5},{5,4},{6,7},{7,6},{8,9},{9,8},{10,11... | collective-permute-start | bytes 12296 | tf_op jit(solution)/shard_map/ppermute | solution.py:381
  24.7 3.6 %collective-permute-start.1 = (f32[8,128]{1,0:T(8,128)S(1)}, f32[8,128]{1,0:T(8,128)S(1)}, u32[]{:S(2)}, u32[]{:S(2)}) collective-permute-start(f32[8,128]{1,0:T(8,128)S(1)} %add.12), channel_id=1, source_target_pairs={{0,2},{1,3},{2,0},{3,1},{4,6},{5,7},{6,4},{7,5},{8,10},{9,11},{10,... | collective-permute-start | bytes 12296 | tf_op jit(solution)/shard_map/ppermute | solution.py:381
  28.3 3.6 %collective-permute-start.2 = (f32[8,128]{1,0:T(8,128)S(1)}, f32[8,128]{1,0:T(8,128)S(1)}, u32[]{:S(2)}, u32[]{:S(2)}) collective-permute-start(f32[8,128]{1,0:T(8,128)S(1)} %add.13), channel_id=1, source_target_pairs={{0,4},{4,0},{8,12},{12,8},{1,5},{5,1},{9,13},{13,9},{2,6},{6,2},{1... | collective-permute-start | bytes 12296 | tf_op jit(solution)/shard_map/ppermute | solution.py:381
  31.9 4.5 %collective-permute-start.3 = (f32[8,128]{1,0:T(8,128)S(1)}, f32[8,128]{1,0:T(8,128)S(1)}, u32[]{:S(2)}, u32[]{:S(2)}) collective-permute-start(f32[8,128]{1,0:T(8,128)S(1)} %add.14), channel_id=1, source_target_pairs={{0,8},{4,12},{8,0},{12,4},{1,9},{5,13},{9,1},{13,5},{2,10},{6,14},... | collective-permute-start | bytes 12296 | tf_op jit(solution)/shard_map/ppermute | solution.py:381

commit v6 on v4

--- a/solution.py
+++ b/solution.py
@@ -369,8 +369,15 @@
 PARAMS = pltpu.CompilerParams(vmem_limit_bytes=48 * 1024 * 1024)
 
 
+def places(owners, inner):
+    lines = owners // inner
+    order = sorted(range(lines), key=lambda line: (abs(2 * line + 1 - lines), line))
+    return [line * inner + other for line in order for other in range(inner)]
+
+
 def send_out(rows):
-    return lax.all_to_all(rows, AXES, split_axis=0, concat_axis=0, tiled=True)
+    group = places(lax.axis_size(AXES), lax.axis_size(AXES[1]))
+    return lax.all_to_all(rows, AXES, split_axis=0, concat_axis=0, tiled=True, axis_index_groups=[group])
 
 
 def on_device(tod, angle, pixel, baseline_id, det_weight, tile_owner, tile_slot):

time: 56.5 us -> 53.4 us (0.945)
  blocking collectives: 45.6 us -> 42.4 us
    all_to_all x4, blocking collectives: 45.6 us -> 42.4 us  [send_out(): lax.all_to_all(rows, AXES, split_axis=0, concat_axis=0, tiled=True, axis_...]
where the time goes in v6:
time: 53.4 us; the launch traced here: 53 us
  blocking collectives  42.4 us (79%)
  Pallas kernels  9.95 us (19%)
  between operations  0.64 us (1%)
    all_to_all x4, blocking collectives, send_out(): lax.all_to_all(rows, AXES, split_axis=0, concat_axis=0, tiled=True, axis_...  42.4 us
    pallas_call x1, Pallas kernels, on_device(): pl.pallas_call(functools.partial(setup_kernel, owners, capacity, tiles),...  2.79 us
    pallas_call x1, Pallas kernels, on_device(): pl.pallas_call(functools.partial(pack_kernel, owners, capacity), out_shap...  2.64 us
    pallas_call x1, Pallas kernels, on_device(): pl.pallas_call(functools.partial(second_kernel, capacity, tiles), out_sha...  2.03 us
    pallas_call x1, Pallas kernels, on_device(): pl.pallas_call(functools.partial(first_kernel, capacity, tiles), out_shap...  1.77 us

profile of v6, /device:TPU:0, one launch (start us, length us, event | category | flops | bytes accessed | tf_op | source)
XLA Modules:
  0.0 53.0 jit_solution(5803404872271502536)
XLA Ops:
  0.6 2.6 %pack.1 = f32[16,32,128]{2,1,0:T(8,128)} custom-call(f32[2,6400]{1,0:T(2,128)} %tod_hbm.1, f32[2,6400]{1,0:T(2,128)} %angle_hbm.1, s32[2,6400]{1,0:T(2,128)} %pixel_hbm.1, s32[2,6400]{1,0:T(2,128)} %base_hbm.1, s32[2,50]{1,0:T(2,128)} %bitcast.1, s32[2,50]{1,0:T(2,128)} %tile_hbm.1, f32[2]{0:T(128)} %weight_hbm.1), custom_call_target="tpu_custom_call" | custom-call | tf_op jit(solution)/shard_map/pack/pallas_call | solution.py:395
  3.3 17.0 %all_to_all.20.recv_ref = f32[16,32,128]{2,1,0:T(8,128)S(1)} all-to-all(f32[16,32,128]{2,1,0:T(8,128)} %pack.1), channel_id=1, replica_groups={{4,5,6,7,8,9,10,11,0,1,2,3,12,13,14,15},{20,21,22,23,24,25,26,27,16,17,..., dimensions={0} | all-to-all | bytes 524288 | tf_op jit(solution)/shard_map/all_to_all | solution.py:380
  20.3 2.8 %setup.1 = (f32[16,8,128]{2,1,0:T(8,128)S(1)}, s32[128,128]{1,0:T(8,128)S(1)}, s32[128,128]{1,0:T(8,128)S(1)}, s32[128,128]{1,0:T(8,128)S(1)}, f32[128,128]{1,0:...) custom-call(f32[16,32,128]{2,1,0:T(8,128)S(1)} %all_to_all.20.recv_ref), custom_call_target="tpu_custom_call" | custom-call | tf_op jit(solution)/shard_map/setup/pallas_call | solution.py:421
  23.1 8.3 %all_to_all.21.recv_ref = f32[16,8,128]{2,1,0:T(8,128)S(1)} all-to-all(f32[16,8,128]{2,1,0:T(8,128)S(1)} %get-tuple-element.21), channel_id=1, replica_groups={{4,5,6,7,8,9,10,11,0,1,2,3,12,13,14,15},{20,21,22,23,24,25,26,27,16,17,..., dimensions={0} | all-to-all | bytes 131072 | tf_op jit(solution)/shard_map/all_to_all | solution.py:380
  31.4 1.8 %first.1 = (f32[8,128]{1,0:T(8,128)S(1)}, f32[16,8,128]{2,1,0:T(8,128)S(1)}) custom-call(f32[16,8,128]{2,1,0:T(8,128)S(1)} %all_to_all.21.recv_ref, s32[128,128]{1,0:T(8,128)S(1)} %get-tuple-element.22.refs_0_, s32[128,128]{1,0:T(8,128)S(1)} %get-tuple-element.23.refs_1_, s32[128,128]{1,0:T(8,128)S(1)} %get-tuple-element.24.refs_2_, ...), custom_call_target="tpu_custom_call" | custom-call | tf_op jit(solution)/shard_map/first/pallas_call | solution.py:431
  33.1 8.6 %all_to_all.22.recv_ref = f32[16,8,128]{2,1,0:T(8,128)S(1)} all-to-all(f32[16,8,128]{2,1,0:T(8,128)S(1)} %get-tuple-element.35), channel_id=1, replica_groups={{4,5,6,7,8,9,10,11,0,1,2,3,12,13,14,15},{20,21,22,23,24,25,26,27,16,17,..., dimensions={0} | all-to-all | bytes 131072 | tf_op jit(solution)/shard_map/all_to_all | solution.py:380
  41.8 2.0 %second.1 = (f32[8,128]{1,0:T(8,128)S(1)}, f32[16,1,128]{2,1,0:T(1,128)S(1)}) custom-call(f32[16,8,128]{2,1,0:T(8,128)S(1)} %all_to_all.22.recv_ref, f32[8,128]{1,0:T(8,128)S(1)} %get-tuple-element.36.right_ref, f32[8,128]{1,0:T(8,128)S(1)} %get-tuple-element.37.rank_ref, s32[128,128]{1,0:T(8,128)S(1)} %get-tuple-element.22.refs_0_, ...), custom_call_target="tpu_custom_call" | custom-call | tf_op jit(solution)/shard_map/second/pallas_call | solution.py:439
  43.8 8.5 %all_to_all.23.recv_ref = f32[16,1,128]{2,1,0:T(1,128)S(1)} all-to-all(f32[16,1,128]{2,1,0:T(1,128)S(1)} %get-tuple-element.39), channel_id=1, replica_groups={{4,5,6,7,8,9,10,11,0,1,2,3,12,13,14,15},{20,21,22,23,24,25,26,27,16,17,..., dimensions={0} | all-to-all | bytes 16384 | tf_op jit(solution)/shard_map/all_to_all | solution.py:380
  52.3 0.7 %finish.1 = (f32[2,32]{1,0:T(2,128)}, f32[2,32]{1,0:T(2,128)}) custom-call(f32[8,128]{1,0:T(8,128)S(1)} %get-tuple-element.38.own_ref, f32[16,1,128]{2,1,0:T(1,128)S(1)} %all_to_all.23.recv_ref), custom_call_target="tpu_custom_call" | custom-call | tf_op jit(solution)/shard_map/finish/pallas_call | solution.py:448

commit v7 on v6

--- a/solution.py
+++ b/solution.py
@@ -14,10 +14,8 @@
 PACK = 128 // NBASE
 AXES = ("det", "sky")
 
-LANE_TILE = 32
-LANE_WEIGHT = 33
-LANE_DET = 34
-LANE_RANK = 35
+LANE_TILE = 2 * NBASE
+
 
 f32 = jnp.float32
 bf16 = jnp.bfloat16
@@ -76,6 +74,12 @@
     return sin_out, cos_out
 
 
+def fact_lanes(capacity):
+    block = LANE_TILE + capacity
+    weight = block + capacity
+    return LANE_TILE, block, weight, weight + 2
+
+
 def pack_kernel(owners, capacity, tod_hbm, angle_hbm, pixel_hbm, base_hbm, owner_hbm, tile_hbm, weight_hbm,
                 out_ref, tod_ref, angle_ref, pixel_ref, base_ref, owner_ref, tile_ref, weight_ref, rows, small, arrived):
     pairs = ((base_hbm, base_ref), (owner_hbm, owner_ref), (tile_hbm, tile_ref), (weight_hbm, weight_ref),
@@ -83,33 +87,21 @@
     copies = [pltpu.make_async_copy(source, into, arrived.at[n]) for n, (source, into) in enumerate(pairs)]
     for copy in copies:
         copy.start()
-    for copy in copies:
-        copy.wait()
     detectors, samples = tod_ref.shape
     blocks = samples // SB
     count = detectors * blocks
     slots = owners * capacity
-    for channel, ref in enumerate((tod_ref, angle_ref, pixel_ref, base_ref)):
-        rows[channel, pl.ds(96, 32), :] = jnp.zeros((32, 128), f32)
+    pair_rows = 3 * capacity + 1
+    lane_tile, lane_block, lane_weight, lane_rank = fact_lanes(capacity)
+
+    def by_block(number, ref):
+        rows[number, pl.ds(96, 32), :] = jnp.zeros((32, 128), f32)
         for k in range(blocks):
-            piece = ref[:, k * SB:(k + 1) * SB]
-            rows[channel, detectors * k:detectors * (k + 1), :] = piece.astype(f32)
-    small[...] = jnp.zeros((8, 128), i32)
-    small[0:detectors, 0:blocks] = owner_ref[...]
-    small[detectors:2 * detectors, 0:blocks] = tile_ref[...]
-    lane8 = iota((8, 128), 1)
-    spread = lanes_at(small[...], lane8 >> 1)
-    odd = (iota((1, 128), 1) & 1) == 1
-    owner = jnp.where(odd, spread[1:2], spread[0:1])
-    tile = jnp.where(odd, spread[3:4], spread[2:3])
-    lane = iota((1, 128), 1)
-    match = ((iota((owners, 128), 0) == owner) & (lane < count)).astype(f32)
-    running = mm(match.astype(bf16), upper())
-    rank = jnp.sum(match * running, axis=0, keepdims=True).astype(i32) - 1
-    target = jnp.where(lane < count, owner * capacity + rank, -1)
-    route = (iota((slots, 128), 0) == target).astype(f32).astype(bf16)
-
-    base = rows[3]
+            rows[number, detectors * k:detectors * (k + 1), :] = ref[:, k * SB:(k + 1) * SB].astype(f32)
+        return rows[number]
+
+    copies[0].wait()
+    base = by_block(3, base_ref)
     wide = iota((128, 128), 1)
     level = wide.astype(f32)
     bound = jnp.zeros((128, 128), i32)
@@ -117,23 +109,49 @@
         below = lanes_at(base, bound + (step - 1)) <= level
         bound = bound + jnp.where(below, step, 0)
     bound = bound + jnp.where(lanes_at(base, bound) <= level, 1, 0)
-    parity = iota((128, 128), 0) & 1
-    weight = jnp.where(parity == 1, weight_ref[1], weight_ref[0])
-    meta = jnp.where(wide < NBASE, bound.astype(f32), 0.0)
-    meta = meta + jnp.where(wide == LANE_WEIGHT, weight, 0.0)
-    meta = meta + jnp.where(wide == LANE_DET, parity.astype(f32), 0.0)
-    turned = jnp.where(iota((128, 128), 0) == LANE_TILE, (tile + 1).astype(f32), 0.0).astype(bf16)
-    meta_out = left_exact(route, meta) + lax.dot_general(
-        route, turned, (((1,), (1,)), ((), ())), preferred_element_type=f32)
-    meta_out = meta_out + jnp.where(
-        iota((slots, 128), 1) == LANE_RANK, (iota((slots, 128), 0) // capacity).astype(f32), 0.0)
-
-    outs = (left_exact(route, rows[0]), left_exact(route, rows[1]), mm(route, rows[2].astype(bf16)), meta_out)
-    for channel, values in enumerate(outs):
-        if capacity % 8 == 0:
-            out_ref[:, channel * capacity:(channel + 1) * capacity, :] = values.reshape(owners, capacity, 128)
-        else:
-            out_ref[channel] = values
+    member = (iota((8, 128), 1) & 1) == iota((8, 128), 0)
+    member = (member & (iota((8, 128), 1) < count)).astype(f32).astype(bf16)
+    bounds = mm(member, bound.astype(f32).astype(bf16))
+
+    copies[1].wait()
+    copies[2].wait()
+    copies[3].wait()
+    small[...] = jnp.zeros((8, 128), i32)
+    small[0:detectors, 0:blocks] = owner_ref[...]
+    small[detectors:2 * detectors, 0:blocks] = tile_ref[...]
+    spread = lanes_at(small[...], iota((8, 128), 1) >> 1)
+    lane = iota((1, 128), 1)
+    odd = (lane & 1) == 1
+    owner = jnp.where(odd, spread[1:2], spread[0:1])
+    tile = jnp.where(odd, spread[3:4], spread[2:3])
+    match = ((iota((owners, 128), 0) == owner) & (lane < count)).astype(f32)
+    running = mm(match.astype(bf16), upper())
+    rank = jnp.sum(match * running, axis=0, keepdims=True).astype(i32) - 1
+    target = jnp.where(lane < count, owner * capacity + rank, -1)
+    route = (iota((slots, 128), 0) == target).astype(f32).astype(bf16)
+
+    line = iota((128, 128), 0)
+    facts = jnp.zeros((owners, 128), f32)
+    for values, first in ((tile + 1, lane_tile), (lane, lane_block)):
+        place = (line - first == rank).astype(f32).astype(bf16)
+        facts = facts + lax.dot_general(
+            (match * values.astype(f32)).astype(bf16), place, (((1,), (1,)), ((), ())), preferred_element_type=f32)
+    lane16 = iota((owners, 128), 1)
+    facts = jnp.where(lane16 < NBASE, bounds[0:1], facts)
+    facts = jnp.where((lane16 >= NBASE) & (lane16 < 2 * NBASE), pltpu.roll(bounds, NBASE, 1)[1:2], facts)
+    facts = jnp.where(lane16 == lane_weight, weight_ref[0], facts)
+    facts = jnp.where(lane16 == lane_weight + 1, weight_ref[1], facts)
+    facts = jnp.where(lane16 == lane_rank, iota((owners, 128), 0).astype(f32), facts)
+    for other in range(owners):
+        out_ref[(other + 1) * pair_rows - 1:(other + 1) * pair_rows, :] = facts[other:other + 1]
+
+    for number, ref in enumerate((tod_ref, angle_ref, pixel_ref)):
+        copies[4 + number].wait()
+        values = by_block(number, ref)
+        values = mm(route, values.astype(bf16)) if number == 2 else left_exact(route, values)
+        for other in range(owners):
+            start = other * pair_rows + number * capacity
+            out_ref[start:start + capacity, :] = values[other * capacity:(other + 1) * capacity]
 
 
 def sort_lanes(keys):
@@ -224,15 +242,19 @@
 
 
 def setup_kernel(owners, capacity, tiles, recv_ref, part_ref, base_ref, sbase_ref, pixel_ref, cos_ref, sin_ref,
-                 wcos_ref, wsin_ref, weight_ref, ends_ref, bounds_ref, tile_slot_ref, slot_tile_ref, inv_ref, rank_ref):
+                 wcos_ref, wsin_ref, weight_ref, ends_ref, bounds_ref, tile_slot_ref, slot_tile_ref, inv_ref, rank_ref,
+                 rows):
     slots = owners * capacity
-
-    def channel(number):
-        if capacity % 8 == 0:
-            return recv_ref[:, number * capacity:(number + 1) * capacity, :].reshape(slots, 128)
-        return recv_ref[number]
-
-    tod, angle, pixel_f, meta = channel(0), channel(1), channel(2), channel(3)
+    pair_rows = 3 * capacity + 1
+    lane_tile, lane_block, lane_weight, lane_rank = fact_lanes(capacity)
+    for other in range(owners):
+        start = other * pair_rows
+        mine = slice(other * capacity, (other + 1) * capacity)
+        for number in range(3):
+            rows[number, mine, :] = recv_ref[start + number * capacity:start + (number + 1) * capacity, :]
+        fact = recv_ref[start + pair_rows - 1:start + pair_rows, :]
+        rows[3, mine, :] = jnp.broadcast_to(fact, (capacity, 128))
+    tod, angle, pixel_f, facts = rows[0], rows[1], rows[2], rows[3].astype(i32)
     lane = iota((slots, 128), 1)
     slot = iota((slots, 128), 0)
     pixel = pixel_f.astype(i32)
@@ -241,25 +263,28 @@
     sin_ref[...] = sine
     cos_ref[...] = cosine
 
-    def meta_lane(number):
-        return lanes_at(meta, jnp.full((slots, 128), number, i32))
-
-    weight = meta_lane(LANE_WEIGHT)
+    within = slot % capacity
+    tile = lanes_at(facts, lane_tile + within) - 1
+    block = lanes_at(facts, lane_block + within)
+    odd = block & 1
+    start = (block >> 1) * SB
+    weight = lanes_at(rows[3], lane_weight + odd)
     weight_ref[...] = weight
-    tile = meta_lane(LANE_TILE).astype(i32) - 1
     slot_tile = (tile == lane).astype(f32)
     slot_tile_ref[...] = slot_tile
     tile_slot = slot_tile.T
     tile_slot_ref[...] = tile_slot
-    rank_ref[...] = meta_lane(LANE_RANK)[0:8]
-    group = (((slot // capacity) & 1) << 1) + meta_lane(LANE_DET).astype(i32)
-    bounds = jnp.where((lane >> 5) == group, lanes_at(meta, lane & 31).astype(i32), 0)
+    rank_ref[...] = jnp.broadcast_to(facts[0:1, lane_rank:lane_rank + 1].astype(f32), (8, 128))
+    group = (((slot // capacity) & 1) << 1) + odd
+    first = odd << 5
+    bounds = jnp.clip(lanes_at(facts, (lane & 31) + first) - start, 0, SB)
+    bounds = jnp.where(((lane >> 5) == group) & (tile >= 0), bounds, 0)
     bounds_ref[...] = bounds
 
-    meta_i = meta.astype(i32)
     base = jnp.zeros((slots, 128), i32)
+    moment = start + lane
     for step in (16, 8, 4, 2, 1):
-        base = base + jnp.where(lanes_at(meta_i, base + (step - 1)) <= lane, step, 0)
+        base = base + jnp.where(lanes_at(facts, base + (first + (step - 1))) <= moment, step, 0)
     base = base + (group << 5)
     base_ref[...] = base
 
@@ -389,12 +414,11 @@
     tiles = -(-tiles_own // 8) * 8
     slots = owners * capacity
     vec_rows = owners * detectors * NBASE // 128
-    direct = capacity % 8 == 0
-
-    packed_shape = (owners, 4 * capacity, 128) if direct else (4, slots, 128)
+
+    pair_rows = 3 * capacity + 1
     send = pl.pallas_call(
         functools.partial(pack_kernel, owners, capacity),
-        out_shape=jax.ShapeDtypeStruct(packed_shape, f32),
+        out_shape=jax.ShapeDtypeStruct((owners * pair_rows, 128), f32),
         in_specs=[pl.BlockSpec(memory_space=pltpu.HBM)] * 7,
         out_specs=whole(1)[0],
         scratch_shapes=[
@@ -407,11 +431,7 @@
         compiler_params=pltpu.CompilerParams(vmem_limit_bytes=PACK_VMEM),
         name="pack",
     )(tod, angle, pixel, baseline_id, tile_owner.reshape(detectors, blocks), tile_slot, det_weight)
-    if not direct:
-        send = send.reshape(4, owners, capacity, 128).transpose(1, 0, 2, 3)
-    recv = send_out(send)
-    if not direct:
-        recv = recv.transpose(1, 0, 2, 3).reshape(4, slots, 128)
+    recv = send_out(send.reshape(owners, pair_rows, 1, 128)).reshape(owners * pair_rows, 128)
 
     def lanes(dtype):
         return jax.ShapeDtypeStruct((slots, 128), dtype)
@@ -425,6 +445,7 @@
                    jax.ShapeDtypeStruct((6, tiles, 128), f32), jax.ShapeDtypeStruct((8, 128), f32)),
         in_specs=whole(1),
         out_specs=tuple(whole(15)),
+        scratch_shapes=[pltpu.VMEM((4, slots, 128), f32)],
         compiler_params=PARAMS,
         name="setup",
     )(recv)

time: 53.4 us -> 52.9 us (level)
  blocking collectives: 42.4 us -> 41.2 us
  Pallas kernels: 9.95 us -> 10.7 us
    all_to_all x4, blocking collectives: 42.4 us -> 41.2 us  [send_out(): lax.all_to_all(rows, AXES, split_axis=0, concat_axis=0, tiled=True, axis_...]
    pallas_call x1, Pallas kernels: 2.64 us -> 3.32 us  [on_device(): pl.pallas_call(functools.partial(pack_kernel, owners, capacity), out_shap...]
where the time goes in v7:
time: 52.9 us; the launch traced here: 52.5 us
  blocking collectives  41.2 us (78%)
  Pallas kernels  10.7 us (20%)
  between operations  0.64 us (1%)
    all_to_all x4, blocking collectives, send_out(): lax.all_to_all(rows, AXES, split_axis=0, concat_axis=0, tiled=True, axis_...  41.2 us
    pallas_call x1, Pallas kernels, on_device(): pl.pallas_call(functools.partial(pack_kernel, owners, capacity), out_shap...  3.32 us
    pallas_call x1, Pallas kernels, on_device(): pl.pallas_call(functools.partial(setup_kernel, owners, capacity, tiles),...  2.83 us
    pallas_call x1, Pallas kernels, on_device(): pl.pallas_call(functools.partial(second_kernel, capacity, tiles), out_sha...  2.03 us
    pallas_call x1, Pallas kernels, on_device(): pl.pallas_call(functools.partial(first_kernel, capacity, tiles), out_shap...  1.77 us

profile of v7, /device:TPU:0, one launch (start us, length us, event | category | flops | bytes accessed | tf_op | source)
XLA Modules:
  0.0 52.5 jit_solution(417617093171425760)
XLA Ops:
  0.6 3.3 %pack.1 = f32[400,128]{1,0:T(8,128)} custom-call(f32[2,6400]{1,0:T(2,128)} %tod_hbm.1, f32[2,6400]{1,0:T(2,128)} %angle_hbm.1, s32[2,6400]{1,0:T(2,128)} %pixel_hbm.1, s32[2,6400]{1,0:T(2,128)} %base_hbm.1, s32[2,50]{1,0:T(2,128)} %bitcast.5, s32[2,50]{1,0:T(2,128)} %tile_hbm.1, f32[2]{0:T(128)} %weight_hbm.1), custom_call_target="tpu_custom_call" | custom-call | tf_op jit(solution)/shard_map/pack/pallas_call | solution.py:419
  4.0 15.8 %all_to_all.20 = f32[16,25,1,128]{3,2,1,0:T(1,128)S(1)} all-to-all(f32[16,25,1,128]{3,2,1,0:T(1,128)} %bitcast.4), channel_id=1, replica_groups={{4,5,6,7,8,9,10,11,0,1,2,3,12,13,14,15},{20,21,22,23,24,25,26,27,16,17,..., dimensions={0} | all-to-all | bytes 409600 | tf_op jit(solution)/shard_map/all_to_all | solution.py:405
  19.7 2.8 %setup.1 = (f32[16,8,128]{2,1,0:T(8,128)S(1)}, s32[128,128]{1,0:T(8,128)S(1)}, s32[128,128]{1,0:T(8,128)S(1)}, s32[128,128]{1,0:T(8,128)S(1)}, f32[128,128]{1,0:...) custom-call(f32[400,128]{1,0:T(8,128)S(1)} %bitcast.3), custom_call_target="tpu_custom_call" | custom-call | tf_op jit(solution)/shard_map/setup/pallas_call | solution.py:441
  22.6 8.3 %all_to_all.21.recv_ref = f32[16,8,128]{2,1,0:T(8,128)S(1)} all-to-all(f32[16,8,128]{2,1,0:T(8,128)S(1)} %get-tuple-element.21), channel_id=1, replica_groups={{4,5,6,7,8,9,10,11,0,1,2,3,12,13,14,15},{20,21,22,23,24,25,26,27,16,17,..., dimensions={0} | all-to-all | bytes 131072 | tf_op jit(solution)/shard_map/all_to_all | solution.py:405
  30.9 1.8 %first.1 = (f32[8,128]{1,0:T(8,128)S(1)}, f32[16,8,128]{2,1,0:T(8,128)S(1)}) custom-call(f32[16,8,128]{2,1,0:T(8,128)S(1)} %all_to_all.21.recv_ref, s32[128,128]{1,0:T(8,128)S(1)} %get-tuple-element.22.refs_0_, s32[128,128]{1,0:T(8,128)S(1)} %get-tuple-element.23.refs_1_, s32[128,128]{1,0:T(8,128)S(1)} %get-tuple-element.24.refs_2_, ...), custom_call_target="tpu_custom_call" | custom-call | tf_op jit(solution)/shard_map/first/pallas_call | solution.py:452
  32.6 8.6 %all_to_all.22.recv_ref = f32[16,8,128]{2,1,0:T(8,128)S(1)} all-to-all(f32[16,8,128]{2,1,0:T(8,128)S(1)} %get-tuple-element.35), channel_id=1, replica_groups={{4,5,6,7,8,9,10,11,0,1,2,3,12,13,14,15},{20,21,22,23,24,25,26,27,16,17,..., dimensions={0} | all-to-all | bytes 131072 | tf_op jit(solution)/shard_map/all_to_all | solution.py:405
  41.3 2.0 %second.1 = (f32[8,128]{1,0:T(8,128)S(1)}, f32[16,1,128]{2,1,0:T(1,128)S(1)}) custom-call(f32[16,8,128]{2,1,0:T(8,128)S(1)} %all_to_all.22.recv_ref, f32[8,128]{1,0:T(8,128)S(1)} %get-tuple-element.36.right_ref, f32[8,128]{1,0:T(8,128)S(1)} %get-tuple-element.37.rank_ref, s32[128,128]{1,0:T(8,128)S(1)} %get-tuple-element.22.refs_0_, ...), custom_call_target="tpu_custom_call" | custom-call | tf_op jit(solution)/shard_map/second/pallas_call | solution.py:460
  43.3 8.5 %all_to_all.23.recv_ref = f32[16,1,128]{2,1,0:T(1,128)S(1)} all-to-all(f32[16,1,128]{2,1,0:T(1,128)S(1)} %get-tuple-element.39), channel_id=1, replica_groups={{4,5,6,7,8,9,10,11,0,1,2,3,12,13,14,15},{20,21,22,23,24,25,26,27,16,17,..., dimensions={0} | all-to-all | bytes 16384 | tf_op jit(solution)/shard_map/all_to_all | solution.py:405
  51.8 0.7 %finish.1 = (f32[2,32]{1,0:T(2,128)}, f32[2,32]{1,0:T(2,128)}) custom-call(f32[8,128]{1,0:T(8,128)S(1)} %get-tuple-element.38.own_ref, f32[16,1,128]{2,1,0:T(1,128)S(1)} %all_to_all.23.recv_ref), custom_call_target="tpu_custom_call" | custom-call | tf_op jit(solution)/shard_map/finish/pallas_call | solution.py:469

commit v8 on v7

--- a/solution.py
+++ b/solution.py
@@ -30,26 +30,24 @@
     return jnp.take_along_axis(values, index, axis=1, mode="promise_in_bounds")
 
 
-def split3(values):
-    first = values.astype(bf16)
-    rest = values - first.astype(f32)
-    second = rest.astype(bf16)
-    third = (rest - second.astype(f32)).astype(bf16)
-    return first, second, third
+def split(values, terms):
+    parts = []
+    for _ in range(terms - 1):
+        parts.append(values.astype(bf16))
+        values = values - parts[-1].astype(f32)
+    return parts + [values.astype(bf16)]
 
 
 def mm(left, right):
     return jnp.dot(left, right, preferred_element_type=f32)
 
 
-def left_exact(left, right):
-    one, two, three = split3(right)
-    return (mm(left, three) + mm(left, two)) + mm(left, one)
-
-
-def right_exact(left, right):
-    one, two, three = split3(left)
-    return (mm(three, right) + mm(two, right)) + mm(one, right)
+def left_hot(left, right, terms=2):
+    return sum(mm(left, term) for term in reversed(split(right, terms)))
+
+
+def right_hot(left, right, terms=2):
+    return sum(mm(term, right) for term in reversed(split(left, terms)))
 
 
 def upper():
@@ -87,6 +85,8 @@
     copies = [pltpu.make_async_copy(source, into, arrived.at[n]) for n, (source, into) in enumerate(pairs)]
     for copy in copies:
         copy.start()
+    for copy in copies:
+        copy.wait()
     detectors, samples = tod_ref.shape
     blocks = samples // SB
     count = detectors * blocks
@@ -100,7 +100,6 @@
             rows[number, detectors * k:detectors * (k + 1), :] = ref[:, k * SB:(k + 1) * SB].astype(f32)
         return rows[number]
 
-    copies[0].wait()
     base = by_block(3, base_ref)
     wide = iota((128, 128), 1)
     level = wide.astype(f32)
@@ -113,9 +112,6 @@
     member = (member & (iota((8, 128), 1) < count)).astype(f32).astype(bf16)
     bounds = mm(member, bound.astype(f32).astype(bf16))
 
-    copies[1].wait()
-    copies[2].wait()
-    copies[3].wait()
     small[...] = jnp.zeros((8, 128), i32)
     small[0:detectors, 0:blocks] = owner_ref[...]
     small[detectors:2 * detectors, 0:blocks] = tile_ref[...]
@@ -146,9 +142,8 @@
         out_ref[(other + 1) * pair_rows - 1:(other + 1) * pair_rows, :] = facts[other:other + 1]
 
     for number, ref in enumerate((tod_ref, angle_ref, pixel_ref)):
-        copies[4 + number].wait()
         values = by_block(number, ref)
-        values = mm(route, values.astype(bf16)) if number == 2 else left_exact(route, values)
+        values = left_hot(route, values, 1 if number == 2 else 3)
         for other in range(owners):
             start = other * pair_rows + number * capacity
             out_ref[start:start + capacity, :] = values[other * capacity:(other + 1) * capacity]
@@ -191,11 +186,13 @@
     return lanes_at(mixed, ((lane & 15) << 3) + (lane >> 4))
 
 
-def ends_to_sums(prefix, ends):
-    filled = ends > 0
-    at_end = jnp.where(filled, lanes_at(prefix, jnp.maximum(ends - 1, 0)), 0.0)
-    before = jnp.where(iota(ends.shape, 1) == 0, 0.0, pltpu.roll(at_end, 1, 1))
-    return jnp.where(filled, at_end - before, 0.0)
+def at_ends(prefix, ends):
+    return jnp.where(ends > 0, lanes_at(prefix, jnp.maximum(ends - 1, 0)), 0.0)
+
+
+def between(values, period):
+    first = (iota(values.shape, 1) & (period - 1)) == 0
+    return values - jnp.where(first, 0.0, pltpu.roll(values, 1, 1))
 
 
 def cofactors(hit_sums):
@@ -222,27 +219,42 @@
     return [first, second, third]
 
 
-def vector_rows(slots, capacity, turned):
-    rows = slots * 2 * NBASE // capacity // 128
+def rows_of_slots(slots, rows, turned):
     per_row = slots // rows
     if turned:
         return (iota((rows, slots), 0) == iota((rows, slots), 1) // per_row).astype(f32).astype(bf16)
     return (iota((slots, rows), 1) == iota((slots, rows), 0) // per_row).astype(f32).astype(bf16)
 
 
+def to_slots(vector, slots):
+    rows = vector.shape[0]
+    per_row = slots // rows
+    if per_row % 8:
+        return left_hot(rows_of_slots(slots, rows, False), vector, 3)
+    return jnp.broadcast_to(vector[:, None, :], (rows, per_row, 128)).reshape(slots, 128)
+
+
+def from_slots(values, rows):
+    slots = values.shape[0]
+    per_row = slots // rows
+    if per_row % 8:
+        return left_hot(rows_of_slots(slots, rows, True), values, 3)
+    return jnp.sum(values.reshape(rows, per_row, 128), axis=1)
+
+
 def map_to_baselines(capacity, map_sums, inverse, signal, slot_tile, pixel, cosine, sine, weight, bounds):
     slots = pixel.shape[0]
     sky = solve_map(inverse, map_sums)
-    near = left_exact(slot_tile, jnp.concatenate(sky, axis=1))
+    near = left_hot(slot_tile, jnp.concatenate(sky, axis=1))
     rest = signal - lanes_at(near[:, 0:128], pixel)
     rest = rest - cosine * lanes_at(near[:, 128:256], pixel)
     rest = rest - sine * lanes_at(near[:, 256:384], pixel)
-    totals = ends_to_sums(right_exact(rest, upper()), bounds) * weight
-    return left_exact(vector_rows(slots, capacity, True), totals)
+    ended = at_ends(right_hot(weight * rest, upper()), bounds)
+    return between(from_slots(ended, slots * 2 * NBASE // capacity // 128), NBASE)
 
 
 def setup_kernel(owners, capacity, tiles, recv_ref, part_ref, base_ref, sbase_ref, pixel_ref, cos_ref, sin_ref,
-                 wcos_ref, wsin_ref, weight_ref, ends_ref, bounds_ref, tile_slot_ref, slot_tile_ref, inv_ref, rank_ref,
+                 scos_ref, ssin_ref, weight_ref, ends_ref, bounds_ref, tile_slot_ref, slot_tile_ref, inv_ref, rank_ref,
                  rows):
     slots = owners * capacity
     pair_rows = 3 * capacity + 1
@@ -299,19 +311,17 @@
     sbase_ref[...] = lanes_at(base, order)
     scos = lanes_at(cosine, order)
     ssin = lanes_at(sine, order)
-    stod = lanes_at(tod, order)
-    wcos_ref[...] = scos
-    wsin_ref[...] = ssin
-
-    tri = upper()
+    wtod = weight * lanes_at(tod, order)
+    wcos = weight * scos
+    scos_ref[...] = scos
+    ssin_ref[...] = ssin
+
     stacked = jnp.concatenate(
-        [stod, scos * stod, ssin * stod, scos, ssin, scos * scos, scos * ssin], axis=0)
-    prefix = right_exact(stacked, tri)
-    binned = [ends_to_sums(prefix[n * slots:(n + 1) * slots], ends) for n in range(7)]
-    before = pltpu.roll(ends, 1, 1)
-    hits = (ends - jnp.where(lane == 0, 0, before)).astype(f32)
-    all_binned = jnp.concatenate([weight * values for values in binned + [hits]], axis=1)
-    sums = left_exact(tile_slot.astype(bf16)[0:tiles], all_binned)
+        [wtod, scos * wtod, ssin * wtod, wcos, weight * ssin, wcos * scos, wcos * ssin], axis=0)
+    prefix = right_hot(stacked, upper())
+    binned = [between(at_ends(prefix[n * slots:(n + 1) * slots], ends), 128) for n in range(7)]
+    binned.append(weight * between(ends.astype(f32), 128))
+    sums = left_hot(tile_slot.astype(bf16)[0:tiles], jnp.concatenate(binned, axis=1))
     sums = [sums[:, 128 * n:128 * (n + 1)] for n in range(8)]
     inverse = cofactors([sums[7], sums[3], sums[4], sums[5], sums[6], sums[7] - sums[5]])
     for number, values in enumerate(inverse):
@@ -321,20 +331,19 @@
     part_ref[...] = jnp.broadcast_to(part[None], part_ref.shape)
 
 
-def apply(capacity, tiles, vector, base_ref, sbase_ref, pixel_ref, cos_ref, sin_ref, wcos_ref, wsin_ref,
+def apply(capacity, tiles, vector, base_ref, sbase_ref, pixel_ref, cos_ref, sin_ref, scos_ref, ssin_ref,
           weight_ref, ends_ref, bounds_ref, tile_slot_ref, slot_tile_ref, inv_ref):
     slots = pixel_ref.shape[0]
-    levels = left_exact(vector_rows(slots, capacity, False), vector)
+    levels = to_slots(vector, slots)
     signal = lanes_at(levels, base_ref[...])
-    sorted_signal = lanes_at(levels, sbase_ref[...])
-    stacked = jnp.concatenate(
-        [sorted_signal, wcos_ref[...] * sorted_signal, wsin_ref[...] * sorted_signal], axis=0)
-    prefix = right_exact(stacked, upper())
+    weight = weight_ref[...]
+    weighted = weight * lanes_at(levels, sbase_ref[...])
+    stacked = jnp.concatenate([weighted, scos_ref[...] * weighted, ssin_ref[...] * weighted], axis=0)
+    prefix = right_hot(stacked, upper())
     ends = ends_ref[...]
-    weight = weight_ref[...]
     binned = jnp.concatenate(
-        [weight * ends_to_sums(prefix[n * slots:(n + 1) * slots], ends) for n in range(3)], axis=1)
-    sums = left_exact(tile_slot_ref[0:tiles, :].astype(bf16), binned)
+        [between(at_ends(prefix[n * slots:(n + 1) * slots], ends), 128) for n in range(3)], axis=1)
+    sums = left_hot(tile_slot_ref[0:tiles, :].astype(bf16), binned)
     return map_to_baselines(
         capacity, [sums[:, 128 * n:128 * (n + 1)] for n in range(3)], [inv_ref[n] for n in range(6)], signal,
         slot_tile_ref[:, 0:tiles].astype(bf16), pixel_ref[...], cos_ref[...], sin_ref[...], weight, bounds_ref[...])
@@ -368,17 +377,18 @@
         own_ref[number:number + 1, :] = jnp.where((rank & 1) == 1, pltpu.roll(row, 64, 1), row)
     own_ref[3:4, :] = jnp.broadcast_to(norm_next, (1, 128))
     part = apply(capacity, tiles, direction, *state)
-    curve = total(direction * part)
-    lane = iota((1, 128), 1)
-    turned = pltpu.roll(part, 64, 1)
+    curve = jnp.sum(direction * part, axis=0, keepdims=True)
+    curve = curve + pltpu.roll(curve, 64, 1)
+    own = iota(part.shape, 1) < 64
+    halves = jnp.where(own, part, curve), jnp.where(own, pltpu.roll(part, 64, 1), curve)
     for owner in range(out_ref.shape[0]):
-        source = part if owner % 2 == 0 else turned
-        out_ref[owner] = jnp.where(lane < 64, source[owner // 2:owner // 2 + 1], jnp.where(lane == 64, curve, 0.0))
+        out_ref[owner] = halves[owner % 2][owner // 2:owner // 2 + 1]
 
 
 def final_kernel(own_ref, recv_ref, levels_ref, misfit_ref):
     image = jnp.sum(recv_ref[...], axis=0)
-    scale = own_ref[3:4, :] / lanes_at(jnp.broadcast_to(image, (8, 128)), jnp.full((8, 128), 64, i32))[0:1]
+    curve = jnp.sum(jnp.where(iota((1, 128), 1) < 64, 0.0, image), axis=1, keepdims=True)
+    scale = own_ref[3:4, :] / curve
     levels = own_ref[0:1, :] + scale * own_ref[1:2, :]
     misfit = own_ref[2:3, :] - scale * image
     for values, ref in ((levels, levels_ref), (misfit, misfit_ref)):

time: 52.9 us -> 50.9 us (0.962)
  Pallas kernels: 10.7 us -> 8.76 us
    pallas_call x1, Pallas kernels: 3.32 us -> 2.62 us  [on_device(): pl.pallas_call(functools.partial(pack_kernel, owners, capacity), out_shap...]
where the time goes in v8:
time: 50.9 us; the launch traced here: 50.6 us
  blocking collectives  41.2 us (81%)
  Pallas kernels  8.76 us (17%)
  between operations  0.64 us (1%)
    all_to_all x4, blocking collectives, send_out(): lax.all_to_all(rows, AXES, split_axis=0, concat_axis=0, tiled=True, axis_...  41.2 us
    pallas_call x1, Pallas kernels, on_device(): pl.pallas_call(functools.partial(pack_kernel, owners, capacity), out_shap...  2.62 us
    pallas_call x1, Pallas kernels, on_device(): pl.pallas_call(functools.partial(setup_kernel, owners, capacity, tiles),...  2.38 us
    pallas_call x1, Pallas kernels, on_device(): pl.pallas_call(functools.partial(second_kernel, capacity, tiles), out_sha...  1.64 us
    pallas_call x1, Pallas kernels, on_device(): pl.pallas_call(functools.partial(first_kernel, capacity, tiles), out_shap...  1.38 us

profile of v8, /device:TPU:0, one launch (start us, length us, event | category | flops | bytes accessed | tf_op | source)
XLA Modules:
  0.0 50.6 jit_solution(9629431114314650562)
XLA Ops:
  0.6 2.6 %pack.1 = f32[400,128]{1,0:T(8,128)} custom-call(f32[2,6400]{1,0:T(2,128)} %tod_hbm.1, f32[2,6400]{1,0:T(2,128)} %angle_hbm.1, s32[2,6400]{1,0:T(2,128)} %pixel_hbm.1, s32[2,6400]{1,0:T(2,128)} %base_hbm.1, s32[2,50]{1,0:T(2,128)} %bitcast.5, s32[2,50]{1,0:T(2,128)} %tile_hbm.1, f32[2]{0:T(128)} %weight_hbm.1), custom_call_target="tpu_custom_call" | custom-call | tf_op jit(solution)/shard_map/pack/pallas_call | solution.py:429
  3.3 15.8 %all_to_all.20 = f32[16,25,1,128]{3,2,1,0:T(1,128)S(1)} all-to-all(f32[16,25,1,128]{3,2,1,0:T(1,128)} %bitcast.4), channel_id=1, replica_groups={{4,5,6,7,8,9,10,11,0,1,2,3,12,13,14,15},{20,21,22,23,24,25,26,27,16,17,..., dimensions={0} | all-to-all | bytes 409600 | tf_op jit(solution)/shard_map/all_to_all | solution.py:415
  19.0 2.4 %setup.1 = (f32[16,8,128]{2,1,0:T(8,128)S(1)}, s32[128,128]{1,0:T(8,128)S(1)}, s32[128,128]{1,0:T(8,128)S(1)}, s32[128,128]{1,0:T(8,128)S(1)}, f32[128,128]{1,0:...) custom-call(f32[400,128]{1,0:T(8,128)S(1)} %bitcast.3), custom_call_target="tpu_custom_call" | custom-call | tf_op jit(solution)/shard_map/setup/pallas_call | solution.py:451
  21.4 8.3 %all_to_all.21.recv_ref = f32[16,8,128]{2,1,0:T(8,128)S(1)} all-to-all(f32[16,8,128]{2,1,0:T(8,128)S(1)} %get-tuple-element.21), channel_id=1, replica_groups={{4,5,6,7,8,9,10,11,0,1,2,3,12,13,14,15},{20,21,22,23,24,25,26,27,16,17,..., dimensions={0} | all-to-all | bytes 131072 | tf_op jit(solution)/shard_map/all_to_all | solution.py:415
  29.7 1.4 %first.1 = (f32[8,128]{1,0:T(8,128)S(1)}, f32[16,8,128]{2,1,0:T(8,128)S(1)}) custom-call(f32[16,8,128]{2,1,0:T(8,128)S(1)} %all_to_all.21.recv_ref, s32[128,128]{1,0:T(8,128)S(1)} %get-tuple-element.22.refs_0_, s32[128,128]{1,0:T(8,128)S(1)} %get-tuple-element.23.refs_1_, s32[128,128]{1,0:T(8,128)S(1)} %get-tuple-element.24.refs_2_, ...), custom_call_target="tpu_custom_call" | custom-call | tf_op jit(solution)/shard_map/first/pallas_call | solution.py:462
  31.1 8.6 %all_to_all.22.recv_ref = f32[16,8,128]{2,1,0:T(8,128)S(1)} all-to-all(f32[16,8,128]{2,1,0:T(8,128)S(1)} %get-tuple-element.35), channel_id=1, replica_groups={{4,5,6,7,8,9,10,11,0,1,2,3,12,13,14,15},{20,21,22,23,24,25,26,27,16,17,..., dimensions={0} | all-to-all | bytes 131072 | tf_op jit(solution)/shard_map/all_to_all | solution.py:415
  39.7 1.6 %second.1 = (f32[8,128]{1,0:T(8,128)S(1)}, f32[16,1,128]{2,1,0:T(1,128)S(1)}) custom-call(f32[16,8,128]{2,1,0:T(8,128)S(1)} %all_to_all.22.recv_ref, f32[8,128]{1,0:T(8,128)S(1)} %get-tuple-element.36.right_ref, f32[8,128]{1,0:T(8,128)S(1)} %get-tuple-element.37.rank_ref, s32[128,128]{1,0:T(8,128)S(1)} %get-tuple-element.22.refs_0_, ...), custom_call_target="tpu_custom_call" | custom-call | tf_op jit(solution)/shard_map/second/pallas_call | solution.py:470
  41.4 8.5 %all_to_all.23.recv_ref = f32[16,1,128]{2,1,0:T(1,128)S(1)} all-to-all(f32[16,1,128]{2,1,0:T(1,128)S(1)} %get-tuple-element.39), channel_id=1, replica_groups={{4,5,6,7,8,9,10,11,0,1,2,3,12,13,14,15},{20,21,22,23,24,25,26,27,16,17,..., dimensions={0} | all-to-all | bytes 16384 | tf_op jit(solution)/shard_map/all_to_all | solution.py:415
  49.8 0.7 %finish.1 = (f32[2,32]{1,0:T(2,128)}, f32[2,32]{1,0:T(2,128)}) custom-call(f32[8,128]{1,0:T(8,128)S(1)} %get-tuple-element.38.own_ref, f32[16,1,128]{2,1,0:T(1,128)S(1)} %all_to_all.23.recv_ref), custom_call_target="tpu_custom_call" | custom-call | tf_op jit(solution)/shard_map/finish/pallas_call | solution.py:479

commit v9 on v8

--- a/solution.py
+++ b/solution.py
@@ -400,13 +400,12 @@
     return [pl.BlockSpec(memory_space=pltpu.VMEM)] * count
 
 
-PACK_VMEM = 64 * 1024 * 1024
 PARAMS = pltpu.CompilerParams(vmem_limit_bytes=48 * 1024 * 1024)
 
 
 def places(owners, inner):
     lines = owners // inner
-    order = sorted(range(lines), key=lambda line: (abs(2 * line + 1 - lines), line))
+    order = list(range((lines - 1) // 2, -1, -1)) + list(range((lines - 1) // 2 + 1, lines))
     return [line * inner + other for line in order for other in range(inner)]
 
 
@@ -438,9 +437,10 @@
             pltpu.SMEM((detectors,), f32),
             pltpu.VMEM((4, 128, 128), f32), pltpu.VMEM((8, 128), i32), pltpu.SemaphoreType.DMA((7,)),
         ],
-        compiler_params=pltpu.CompilerParams(vmem_limit_bytes=PACK_VMEM),
+        compiler_params=PARAMS,
         name="pack",
-    )(tod, angle, pixel, baseline_id, tile_owner.reshape(detectors, blocks), tile_slot, det_weight)
+    )(*[pltpu.with_memory_space_constraint(operand, pltpu.HBM) for operand in (
+        tod, angle, pixel, baseline_id, tile_owner.reshape(detectors, blocks), tile_slot, det_weight)])
     recv = send_out(send.reshape(owners, pair_rows, 1, 128)).reshape(owners * pair_rows, 128)
 
     def lanes(dtype):

time: 50.9 us -> 49.6 us (0.974)
  Pallas kernels: 8.76 us -> 8.11 us
  blocking collectives: 41.2 us -> 40.6 us
    pallas_call x1, Pallas kernels: 2.62 us -> 1.96 us  [on_device(): pl.pallas_call(functools.partial(pack_kernel, owners, capacity), out_shap...]
    all_to_all x4, blocking collectives: 41.2 us -> 40.6 us  [send_out(): lax.all_to_all(rows, AXES, split_axis=0, concat_axis=0, tiled=True, axis_...]
where the time goes in v9:
time: 49.6 us; the launch traced here: 49.3 us
  blocking collectives  40.6 us (82%)
  Pallas kernels  8.11 us (16%)
  between operations  0.64 us (1%)
    all_to_all x4, blocking collectives, send_out(): lax.all_to_all(rows, AXES, split_axis=0, concat_axis=0, tiled=True, axis_...  40.6 us
    pallas_call x1, Pallas kernels, on_device(): pl.pallas_call(functools.partial(setup_kernel, owners, capacity, tiles),...  2.39 us
    pallas_call x1, Pallas kernels, on_device(): pl.pallas_call(functools.partial(pack_kernel, owners, capacity), out_shap...  1.96 us
    pallas_call x1, Pallas kernels, on_device(): pl.pallas_call(functools.partial(second_kernel, capacity, tiles), out_sha...  1.64 us
    pallas_call x1, Pallas kernels, on_device(): pl.pallas_call(functools.partial(first_kernel, capacity, tiles), out_shap...  1.38 us

profile of v9, /device:TPU:0, one launch (start us, length us, event | category | flops | bytes accessed | tf_op | source)
XLA Modules:
  0.0 49.3 jit_solution(8361672942483271352)
XLA Ops:
  0.6 2.0 %pack.1 = f32[400,128]{1,0:T(8,128)S(1)} custom-call(f32[2,6400]{1,0:T(2,128)} %tod_hbm.1, f32[2,6400]{1,0:T(2,128)} %angle_hbm.1, s32[2,6400]{1,0:T(2,128)} %pixel_hbm.1, s32[2,6400]{1,0:T(2,128)} %base_hbm.1, s32[2,50]{1,0:T(2,128)} %bitcast.5, s32[2,50]{1,0:T(2,128)} %tile_hbm.1, f32[2]{0:T(128)} %weight_hbm.1), custom_call_target="tpu_custom_call" | custom-call | tf_op jit(solution)/shard_map/pack/pallas_call | solution.py:428
  2.6 13.9 %all_to_all.20 = f32[16,25,1,128]{3,2,1,0:T(1,128)S(1)} all-to-all(f32[16,25,1,128]{3,2,1,0:T(1,128)S(1)} %bitcast.4), channel_id=1, replica_groups={{4,5,6,7,0,1,2,3,8,9,10,11,12,13,14,15},{20,21,22,23,16,17,18,19,24,25,..., dimensions={0} | all-to-all | bytes 409600 | tf_op jit(solution)/shard_map/all_to_all | solution.py:414
  16.5 2.4 %setup.1 = (f32[16,8,128]{2,1,0:T(8,128)S(1)}, s32[128,128]{1,0:T(8,128)S(1)}, s32[128,128]{1,0:T(8,128)S(1)}, s32[128,128]{1,0:T(8,128)S(1)}, f32[128,128]{1,0:...) custom-call(f32[400,128]{1,0:T(8,128)S(1)} %bitcast.3), custom_call_target="tpu_custom_call" | custom-call | tf_op jit(solution)/shard_map/setup/pallas_call | solution.py:451
  18.9 9.6 %all_to_all.21.recv_ref = f32[16,8,128]{2,1,0:T(8,128)S(1)} all-to-all(f32[16,8,128]{2,1,0:T(8,128)S(1)} %get-tuple-element.21), channel_id=1, replica_groups={{4,5,6,7,0,1,2,3,8,9,10,11,12,13,14,15},{20,21,22,23,16,17,18,19,24,25,..., dimensions={0} | all-to-all | bytes 131072 | tf_op jit(solution)/shard_map/all_to_all | solution.py:414
  28.5 1.4 %first.1 = (f32[8,128]{1,0:T(8,128)S(1)}, f32[16,8,128]{2,1,0:T(8,128)S(1)}) custom-call(f32[16,8,128]{2,1,0:T(8,128)S(1)} %all_to_all.21.recv_ref, s32[128,128]{1,0:T(8,128)S(1)} %get-tuple-element.22.refs_0_, s32[128,128]{1,0:T(8,128)S(1)} %get-tuple-element.23.refs_1_, s32[128,128]{1,0:T(8,128)S(1)} %get-tuple-element.24.refs_2_, ...), custom_call_target="tpu_custom_call" | custom-call | tf_op jit(solution)/shard_map/first/pallas_call | solution.py:462
  29.9 8.6 %all_to_all.22.recv_ref = f32[16,8,128]{2,1,0:T(8,128)S(1)} all-to-all(f32[16,8,128]{2,1,0:T(8,128)S(1)} %get-tuple-element.35), channel_id=1, replica_groups={{4,5,6,7,0,1,2,3,8,9,10,11,12,13,14,15},{20,21,22,23,16,17,18,19,24,25,..., dimensions={0} | all-to-all | bytes 131072 | tf_op jit(solution)/shard_map/all_to_all | solution.py:414
  38.5 1.6 %second.1 = (f32[8,128]{1,0:T(8,128)S(1)}, f32[16,1,128]{2,1,0:T(1,128)S(1)}) custom-call(f32[16,8,128]{2,1,0:T(8,128)S(1)} %all_to_all.22.recv_ref, f32[8,128]{1,0:T(8,128)S(1)} %get-tuple-element.36.right_ref, f32[8,128]{1,0:T(8,128)S(1)} %get-tuple-element.37.rank_ref, s32[128,128]{1,0:T(8,128)S(1)} %get-tuple-element.22.refs_0_, ...), custom_call_target="tpu_custom_call" | custom-call | tf_op jit(solution)/shard_map/second/pallas_call | solution.py:470
  40.1 8.5 %all_to_all.23.recv_ref = f32[16,1,128]{2,1,0:T(1,128)S(1)} all-to-all(f32[16,1,128]{2,1,0:T(1,128)S(1)} %get-tuple-element.39), channel_id=1, replica_groups={{4,5,6,7,0,1,2,3,8,9,10,11,12,13,14,15},{20,21,22,23,16,17,18,19,24,25,..., dimensions={0} | all-to-all | bytes 16384 | tf_op jit(solution)/shard_map/all_to_all | solution.py:414
  48.6 0.7 %finish.1 = (f32[2,32]{1,0:T(2,128)}, f32[2,32]{1,0:T(2,128)}) custom-call(f32[8,128]{1,0:T(8,128)S(1)} %get-tuple-element.38.own_ref, f32[16,1,128]{2,1,0:T(1,128)S(1)} %all_to_all.23.recv_ref), custom_call_target="tpu_custom_call" | custom-call | tf_op jit(solution)/shard_map/finish/pallas_call | solution.py:479

commit v10 on v9

--- a/solution.py
+++ b/solution.py
@@ -209,7 +209,8 @@
     minor_qu = entry_iq * entry_iu - entry_ii * entry_qu
     minor_uu = entry_ii * entry_qq - entry_iq * entry_iq
     determinant = entry_ii * minor_ii + entry_iq * minor_iq + entry_iu * minor_iu
-    return [minor / determinant for minor in (minor_ii, minor_iq, minor_iu, minor_qq, minor_qu, minor_uu)]
+    scale = 1.0 / determinant
+    return [minor * scale for minor in (minor_ii, minor_iq, minor_iu, minor_qq, minor_qu, minor_uu)]
 
 
 def solve_map(inverse, map_sums):
@@ -242,20 +243,18 @@
     return jnp.sum(values.reshape(rows, per_row, 128), axis=1)
 
 
-def map_to_baselines(capacity, map_sums, inverse, signal, slot_tile, pixel, cosine, sine, weight, bounds):
+def map_to_baselines(capacity, map_sums, inverse, signal, pixel, cosine, sine, weight, bounds):
     slots = pixel.shape[0]
     sky = solve_map(inverse, map_sums)
-    near = left_hot(slot_tile, jnp.concatenate(sky, axis=1))
-    rest = signal - lanes_at(near[:, 0:128], pixel)
-    rest = rest - cosine * lanes_at(near[:, 128:256], pixel)
-    rest = rest - sine * lanes_at(near[:, 256:384], pixel)
+    rest = signal - lanes_at(sky[0], pixel)
+    rest = rest - cosine * lanes_at(sky[1], pixel)
+    rest = rest - sine * lanes_at(sky[2], pixel)
     ended = at_ends(right_hot(weight * rest, upper()), bounds)
     return between(from_slots(ended, slots * 2 * NBASE // capacity // 128), NBASE)
 
 
-def setup_kernel(owners, capacity, tiles, recv_ref, part_ref, base_ref, sbase_ref, pixel_ref, cos_ref, sin_ref,
-                 scos_ref, ssin_ref, weight_ref, ends_ref, bounds_ref, tile_slot_ref, slot_tile_ref, inv_ref, rank_ref,
-                 rows):
+def setup_kernel(owners, capacity, recv_ref, part_ref, base_ref, sbase_ref, pixel_ref, cos_ref, sin_ref,
+                 scos_ref, ssin_ref, weight_ref, ends_ref, bounds_ref, same_ref, inv_ref, rank_ref, rows):
     slots = owners * capacity
     pair_rows = 3 * capacity + 1
     lane_tile, lane_block, lane_weight, lane_rank = fact_lanes(capacity)
@@ -282,10 +281,10 @@
     start = (block >> 1) * SB
     weight = lanes_at(rows[3], lane_weight + odd)
     weight_ref[...] = weight
-    slot_tile = (tile == lane).astype(f32)
-    slot_tile_ref[...] = slot_tile
-    tile_slot = slot_tile.T
-    tile_slot_ref[...] = tile_slot
+    tile_row = tile.astype(f32).T[0:1]
+    tile_column = jnp.concatenate([tile.astype(f32)] * (slots // 128), axis=1)
+    same = (tile_column == jnp.where(tile_row < 0.0, -2.0, tile_row)).astype(f32).astype(bf16)
+    same_ref[...] = same
     rank_ref[...] = jnp.broadcast_to(facts[0:1, lane_rank:lane_rank + 1].astype(f32), (8, 128))
     group = (((slot // capacity) & 1) << 1) + odd
     first = odd << 5
@@ -321,18 +320,17 @@
     prefix = right_hot(stacked, upper())
     binned = [between(at_ends(prefix[n * slots:(n + 1) * slots], ends), 128) for n in range(7)]
     binned.append(weight * between(ends.astype(f32), 128))
-    sums = left_hot(tile_slot.astype(bf16)[0:tiles], jnp.concatenate(binned, axis=1))
+    sums = left_hot(same, jnp.concatenate(binned, axis=1))
     sums = [sums[:, 128 * n:128 * (n + 1)] for n in range(8)]
     inverse = cofactors([sums[7], sums[3], sums[4], sums[5], sums[6], sums[7] - sums[5]])
     for number, values in enumerate(inverse):
         inv_ref[number] = values
-    part = map_to_baselines(capacity, sums[0:3], inverse, tod, slot_tile.astype(bf16)[:, 0:tiles], pixel, cosine, sine,
-                            weight, bounds)
+    part = map_to_baselines(capacity, sums[0:3], inverse, tod, pixel, cosine, sine, weight, bounds)
     part_ref[...] = jnp.broadcast_to(part[None], part_ref.shape)
 
 
-def apply(capacity, tiles, vector, base_ref, sbase_ref, pixel_ref, cos_ref, sin_ref, scos_ref, ssin_ref,
-          weight_ref, ends_ref, bounds_ref, tile_slot_ref, slot_tile_ref, inv_ref):
+def apply(capacity, vector, base_ref, sbase_ref, pixel_ref, cos_ref, sin_ref, scos_ref, ssin_ref,
+          weight_ref, ends_ref, bounds_ref, same_ref, inv_ref):
     slots = pixel_ref.shape[0]
     levels = to_slots(vector, slots)
     signal = lanes_at(levels, base_ref[...])
@@ -343,40 +341,44 @@
     ends = ends_ref[...]
     binned = jnp.concatenate(
         [between(at_ends(prefix[n * slots:(n + 1) * slots], ends), 128) for n in range(3)], axis=1)
-    sums = left_hot(tile_slot_ref[0:tiles, :].astype(bf16), binned)
+    sums = left_hot(same_ref[...], binned)
     return map_to_baselines(
         capacity, [sums[:, 128 * n:128 * (n + 1)] for n in range(3)], [inv_ref[n] for n in range(6)], signal,
-        slot_tile_ref[:, 0:tiles].astype(bf16), pixel_ref[...], cos_ref[...], sin_ref[...], weight, bounds_ref[...])
+        pixel_ref[...], cos_ref[...], sin_ref[...], weight, bounds_ref[...])
 
 
 def total(values):
     return jnp.sum(jnp.sum(values, axis=0, keepdims=True), axis=1, keepdims=True)
 
 
-def first_kernel(capacity, tiles, recv_ref, *refs):
-    *state, right_ref, part_ref = refs
+def first_kernel(capacity, recv_ref, *refs):
+    *state, right_ref, share_ref, part_ref = refs
     right = jnp.sum(recv_ref[...], axis=0)
     right_ref[...] = right
-    part = apply(capacity, tiles, right, *state)
+    part = apply(capacity, right, *state)
+    share_ref[...] = part
     part_ref[...] = jnp.broadcast_to(part[None], part_ref.shape)
 
 
-def second_kernel(capacity, tiles, recv_ref, right_ref, rank_ref, *refs):
+def second_kernel(capacity, recv_ref, right_ref, share_ref, rank_ref, *refs):
     *state, own_ref, out_ref = refs
     right = right_ref[...]
     image = jnp.sum(recv_ref[...], axis=0)
+    twice = apply(capacity, image, *state)
     norm_now = total(right * right)
     scale = norm_now / total(right * image)
     misfit = right - scale * image
     norm_next = total(misfit * misfit)
-    direction = misfit + (norm_next / norm_now) * right
+    ratio = norm_next / norm_now
+    direction = misfit + ratio * right
     rank = rank_ref[0:1, :].astype(i32)
     mine = iota(right.shape, 0) == (rank >> 1)
     for number, values in enumerate((scale * right, direction, misfit)):
         row = jnp.sum(jnp.where(mine, values, 0.0), axis=0, keepdims=True)
         own_ref[number:number + 1, :] = jnp.where((rank & 1) == 1, pltpu.roll(row, 64, 1), row)
     own_ref[3:4, :] = jnp.broadcast_to(norm_next, (1, 128))
-    part = apply(capacity, tiles, direction, *state)
+    share = share_ref[...]
+    part = (share - scale * twice) + ratio * share
     curve = jnp.sum(direction * part, axis=0, keepdims=True)
     curve = curve + pltpu.roll(curve, 64, 1)
     own = iota(part.shape, 1) < 64
@@ -419,8 +421,6 @@
     blocks = tile_slot.shape[1]
     owners = lax.axis_size(AXES)
     capacity = detectors * blocks // owners + 2
-    tiles_own = 6 * capacity
-    tiles = -(-tiles_own // 8) * 8
     slots = owners * capacity
     vec_rows = owners * detectors * NBASE // 128
 
@@ -449,32 +449,32 @@
     vector_shape = jax.ShapeDtypeStruct((vec_rows, 128), f32)
     parts_shape = jax.ShapeDtypeStruct((owners, vec_rows, 128), f32)
     part, *state, rank = pl.pallas_call(
-        functools.partial(setup_kernel, owners, capacity, tiles),
+        functools.partial(setup_kernel, owners, capacity),
         out_shape=(parts_shape, lanes(i32), lanes(i32), lanes(i32), lanes(f32), lanes(f32), lanes(f32), lanes(f32),
-                   lanes(f32), lanes(i32), lanes(i32), jax.ShapeDtypeStruct((128, slots), f32), lanes(f32),
-                   jax.ShapeDtypeStruct((6, tiles, 128), f32), jax.ShapeDtypeStruct((8, 128), f32)),
+                   lanes(f32), lanes(i32), lanes(i32), jax.ShapeDtypeStruct((slots, slots), bf16),
+                   jax.ShapeDtypeStruct((6, slots, 128), f32), jax.ShapeDtypeStruct((8, 128), f32)),
         in_specs=whole(1),
-        out_specs=tuple(whole(15)),
+        out_specs=tuple(whole(14)),
         scratch_shapes=[pltpu.VMEM((4, slots, 128), f32)],
         compiler_params=PARAMS,
         name="setup",
     )(recv)
-    right, part = pl.pallas_call(
-        functools.partial(first_kernel, capacity, tiles),
-        out_shape=(vector_shape, parts_shape),
+    right, share, part = pl.pallas_call(
+        functools.partial(first_kernel, capacity),
+        out_shape=(vector_shape, vector_shape, parts_shape),
         in_specs=whole(1 + len(state)),
-        out_specs=tuple(whole(2)),
+        out_specs=tuple(whole(3)),
         compiler_params=PARAMS,
         name="first",
     )(send_out(part), *state)
     own, part = pl.pallas_call(
-        functools.partial(second_kernel, capacity, tiles),
+        functools.partial(second_kernel, capacity),
         out_shape=(jax.ShapeDtypeStruct((8, 128), f32), jax.ShapeDtypeStruct((owners, 1, 128), f32)),
-        in_specs=whole(3 + len(state)),
+        in_specs=whole(4 + len(state)),
         out_specs=tuple(whole(2)),
         compiler_params=PARAMS,
         name="second",
-    )(send_out(part), right, rank, *state)
+    )(send_out(part), right, share, rank, *state)
     out = jax.ShapeDtypeStruct((detectors, NBASE), f32)
     return pl.pallas_call(
         final_kernel,

time: 49.6 us -> 49 us (0.988)
  Pallas kernels: 8.11 us -> 7.51 us
    pallas_call x3, Pallas kernels: 5.41 us -> 4.82 us  [the longest x1 2.32 us: on_device(): pl.pallas_call(functools.partial(setup_kernel, owners, capacity), out_sha...]
where the time goes in v10:
time: 49 us; the launch traced here: 48.7 us
  blocking collectives  40.6 us (83%)
  Pallas kernels  7.51 us (15%)
  between operations  0.64 us (1%)
    all_to_all x4, blocking collectives, send_out(): lax.all_to_all(rows, AXES, split_axis=0, concat_axis=0, tiled=True, axis_...  40.6 us
    pallas_call x1, Pallas kernels, on_device(): pl.pallas_call(functools.partial(setup_kernel, owners, capacity), out_sha...  2.32 us
    pallas_call x1, Pallas kernels, on_device(): pl.pallas_call(functools.partial(pack_kernel, owners, capacity), out_shap...  1.96 us
    pallas_call x1, Pallas kernels, on_device(): pl.pallas_call(functools.partial(second_kernel, capacity), out_shape=(jax...  1.29 us
    pallas_call x1, Pallas kernels, on_device(): pl.pallas_call(functools.partial(first_kernel, capacity), out_shape=(vect...  1.2 us

profile of v10, /device:TPU:0, one launch (start us, length us, event | category | flops | bytes accessed | tf_op | source)
XLA Modules:
  0.0 48.7 jit_solution(10781512367898297109)
XLA Ops:
  0.6 2.0 %pack.1 = f32[400,128]{1,0:T(8,128)S(1)} custom-call(f32[2,6400]{1,0:T(2,128)} %tod_hbm.1, f32[2,6400]{1,0:T(2,128)} %angle_hbm.1, s32[2,6400]{1,0:T(2,128)} %pixel_hbm.1, s32[2,6400]{1,0:T(2,128)} %base_hbm.1, s32[2,50]{1,0:T(2,128)} %bitcast.5, s32[2,50]{1,0:T(2,128)} %tile_hbm.1, f32[2]{0:T(128)} %weight_hbm.1), custom_call_target="tpu_custom_call" | custom-call | tf_op jit(solution)/shard_map/pack/pallas_call | solution.py:428
  2.6 13.9 %all_to_all.20 = f32[16,25,1,128]{3,2,1,0:T(1,128)S(1)} all-to-all(f32[16,25,1,128]{3,2,1,0:T(1,128)S(1)} %bitcast.4), channel_id=1, replica_groups={{4,5,6,7,0,1,2,3,8,9,10,11,12,13,14,15},{20,21,22,23,16,17,18,19,24,25,..., dimensions={0} | all-to-all | bytes 409600 | tf_op jit(solution)/shard_map/all_to_all | solution.py:416
  16.5 2.3 %setup.1 = (f32[16,8,128]{2,1,0:T(8,128)S(1)}, s32[128,128]{1,0:T(8,128)S(1)}, s32[128,128]{1,0:T(8,128)S(1)}, s32[128,128]{1,0:T(8,128)S(1)}, f32[128,128]{1,0:...) custom-call(f32[400,128]{1,0:T(8,128)S(1)} %bitcast.3), custom_call_target="tpu_custom_call" | custom-call | tf_op jit(solution)/shard_map/setup/pallas_call | solution.py:451
  18.8 9.6 %all_to_all.21.recv_ref = f32[16,8,128]{2,1,0:T(8,128)S(1)} all-to-all(f32[16,8,128]{2,1,0:T(8,128)S(1)} %get-tuple-element.21), channel_id=1, replica_groups={{4,5,6,7,0,1,2,3,8,9,10,11,12,13,14,15},{20,21,22,23,16,17,18,19,24,25,..., dimensions={0} | all-to-all | bytes 131072 | tf_op jit(solution)/shard_map/all_to_all | solution.py:416
  28.4 1.2 %first.1 = (f32[8,128]{1,0:T(8,128)S(1)}, f32[8,128]{1,0:T(8,128)S(1)}, f32[16,8,128]{2,1,0:T(8,128)S(1)}) custom-call(f32[16,8,128]{2,1,0:T(8,128)S(1)} %all_to_all.21.recv_ref, s32[128,128]{1,0:T(8,128)S(1)} %get-tuple-element.22.refs_0_, s32[128,128]{1,0:T(8,128)S(1)} %get-tuple-element.23.refs_1_, s32[128,128]{1,0:T(8,128)S(1)} %get-tuple-element.24.refs_2_, ...), custom_call_target="tpu_custom_call" | custom-call | tf_op jit(solution)/shard_map/first/pallas_call | solution.py:462
  29.6 8.6 %all_to_all.22.recv_ref = f32[16,8,128]{2,1,0:T(8,128)S(1)} all-to-all(f32[16,8,128]{2,1,0:T(8,128)S(1)} %get-tuple-element.34), channel_id=1, replica_groups={{4,5,6,7,0,1,2,3,8,9,10,11,12,13,14,15},{20,21,22,23,16,17,18,19,24,25,..., dimensions={0} | all-to-all | bytes 131072 | tf_op jit(solution)/shard_map/all_to_all | solution.py:416
  38.2 1.3 %second.1 = (f32[8,128]{1,0:T(8,128)S(1)}, f32[16,1,128]{2,1,0:T(1,128)S(1)}) custom-call(f32[16,8,128]{2,1,0:T(8,128)S(1)} %all_to_all.22.recv_ref, f32[8,128]{1,0:T(8,128)S(1)} %get-tuple-element.35.right_ref, f32[8,128]{1,0:T(8,128)S(1)} %get-tuple-element.36.share_ref, f32[8,128]{1,0:T(8,128)S(1)} %get-tuple-element.37.rank_ref, ...), custom_call_target="tpu_custom_call" | custom-call | tf_op jit(solution)/shard_map/second/pallas_call | solution.py:470
  39.5 8.5 %all_to_all.23.recv_ref = f32[16,1,128]{2,1,0:T(1,128)S(1)} all-to-all(f32[16,1,128]{2,1,0:T(1,128)S(1)} %get-tuple-element.39), channel_id=1, replica_groups={{4,5,6,7,0,1,2,3,8,9,10,11,12,13,14,15},{20,21,22,23,16,17,18,19,24,25,..., dimensions={0} | all-to-all | bytes 16384 | tf_op jit(solution)/shard_map/all_to_all | solution.py:416
  48.0 0.7 %finish.1 = (f32[2,32]{1,0:T(2,128)}, f32[2,32]{1,0:T(2,128)}) custom-call(f32[8,128]{1,0:T(8,128)S(1)} %get-tuple-element.38.own_ref, f32[16,1,128]{2,1,0:T(1,128)S(1)} %all_to_all.23.recv_ref), custom_call_target="tpu_custom_call" | custom-call | tf_op jit(solution)/shard_map/finish/pallas_call | solution.py:479

commit v11 on v10

--- a/solution.py
+++ b/solution.py
@@ -38,16 +38,24 @@
     return parts + [values.astype(bf16)]
 
 
+def count_up_to(ascending, level):
+    found = jnp.zeros(ascending.shape, i32)
+    for probes, step in (((31, 63, 95), 32), ((7, 15, 23), 8), ((1, 3, 5), 2), ((0, 1), 1)):
+        met = [jnp.where(lanes_at(ascending, found + probe) <= level, step, 0) for probe in probes]
+        found = found + sum(met[1:], met[0])
+    return found
+
+
 def mm(left, right):
     return jnp.dot(left, right, preferred_element_type=f32)
 
 
 def left_hot(left, right, terms=2):
-    return sum(mm(left, term) for term in reversed(split(right, terms)))
+    return mm(jnp.concatenate([left] * terms, axis=1), jnp.concatenate(split(right, terms), axis=0))
 
 
 def right_hot(left, right, terms=2):
-    return sum(mm(term, right) for term in reversed(split(left, terms)))
+    return mm(jnp.concatenate(split(left, terms), axis=1), jnp.concatenate([right] * terms, axis=0))
 
 
 def upper():
@@ -102,12 +110,7 @@
 
     base = by_block(3, base_ref)
     wide = iota((128, 128), 1)
-    level = wide.astype(f32)
-    bound = jnp.zeros((128, 128), i32)
-    for step in (64, 32, 16, 8, 4, 2, 1):
-        below = lanes_at(base, bound + (step - 1)) <= level
-        bound = bound + jnp.where(below, step, 0)
-    bound = bound + jnp.where(lanes_at(base, bound) <= level, 1, 0)
+    bound = count_up_to(base, wide.astype(f32))
     member = (iota((8, 128), 1) & 1) == iota((8, 128), 0)
     member = (member & (iota((8, 128), 1) < count)).astype(f32).astype(bf16)
     bounds = mm(member, bound.astype(f32).astype(bf16))
@@ -301,11 +304,7 @@
 
     keys = sort_lanes(pixel_f * 128.0 + lane.astype(f32))
     order = keys.astype(i32) & 127
-    limit = (lane.astype(f32) + 1.0) * 128.0
-    ends = jnp.zeros((slots, 128), i32)
-    for step in (64, 32, 16, 8, 4, 2, 1):
-        ends = ends + jnp.where(lanes_at(keys, ends + (step - 1)) < limit, step, 0)
-    ends = ends + jnp.where(lanes_at(keys, ends) < limit, 1, 0)
+    ends = count_up_to(keys, lane.astype(f32) * 128.0 + 127.0)
     ends_ref[...] = ends
     sbase_ref[...] = lanes_at(base, order)
     scos = lanes_at(cosine, order)

time: 49 us -> 48.9 us (level)
  no operation moved by 1% of the time
where the time goes in v11:
time: 48.9 us; the launch traced here: 48.6 us
  blocking collectives  40.6 us (83%)
  Pallas kernels  7.37 us (15%)
  between operations  0.64 us (1%)
    all_to_all x4, blocking collectives, send_out(): lax.all_to_all(rows, AXES, split_axis=0, concat_axis=0, tiled=True, axis_...  40.6 us
    pallas_call x1, Pallas kernels, on_device(): pl.pallas_call(functools.partial(setup_kernel, owners, capacity), out_sha...  2.62 us
    pallas_call x1, Pallas kernels, on_device(): pl.pallas_call(functools.partial(pack_kernel, owners, capacity), out_shap...  1.74 us
    pallas_call x1, Pallas kernels, on_device(): pl.pallas_call(functools.partial(second_kernel, capacity), out_shape=(jax...  1.17 us
    pallas_call x1, Pallas kernels, on_device(): pl.pallas_call(functools.partial(first_kernel, capacity), out_shape=(vect...  1.09 us

profile of v11, /device:TPU:0, one launch (start us, length us, event | category | flops | bytes accessed | tf_op | source)
XLA Modules:
  0.0 48.6 jit_solution(5845266785440242087)
XLA Ops:
  0.6 1.7 %pack.1 = f32[400,128]{1,0:T(8,128)S(1)} custom-call(f32[2,6400]{1,0:T(2,128)} %tod_hbm.1, f32[2,6400]{1,0:T(2,128)} %angle_hbm.1, s32[2,6400]{1,0:T(2,128)} %pixel_hbm.1, s32[2,6400]{1,0:T(2,128)} %base_hbm.1, s32[2,50]{1,0:T(2,128)} %bitcast.5, s32[2,50]{1,0:T(2,128)} %tile_hbm.1, f32[2]{0:T(128)} %weight_hbm.1), custom_call_target="tpu_custom_call" | custom-call | tf_op jit(solution)/shard_map/pack/pallas_call | solution.py:427
  2.4 13.9 %all_to_all.20 = f32[16,25,1,128]{3,2,1,0:T(1,128)S(1)} all-to-all(f32[16,25,1,128]{3,2,1,0:T(1,128)S(1)} %bitcast.4), channel_id=1, replica_groups={{4,5,6,7,0,1,2,3,8,9,10,11,12,13,14,15},{20,21,22,23,16,17,18,19,24,25,..., dimensions={0} | all-to-all | bytes 409600 | tf_op jit(solution)/shard_map/all_to_all | solution.py:415
  16.3 2.6 %setup.1 = (f32[16,8,128]{2,1,0:T(8,128)S(1)}, s32[128,128]{1,0:T(8,128)S(1)}, s32[128,128]{1,0:T(8,128)S(1)}, s32[128,128]{1,0:T(8,128)S(1)}, f32[128,128]{1,0:...) custom-call(f32[400,128]{1,0:T(8,128)S(1)} %bitcast.3), custom_call_target="tpu_custom_call" | custom-call | tf_op jit(solution)/shard_map/setup/pallas_call | solution.py:450
  18.9 9.6 %all_to_all.21.recv_ref = f32[16,8,128]{2,1,0:T(8,128)S(1)} all-to-all(f32[16,8,128]{2,1,0:T(8,128)S(1)} %get-tuple-element.21), channel_id=1, replica_groups={{4,5,6,7,0,1,2,3,8,9,10,11,12,13,14,15},{20,21,22,23,16,17,18,19,24,25,..., dimensions={0} | all-to-all | bytes 131072 | tf_op jit(solution)/shard_map/all_to_all | solution.py:415
  28.5 1.1 %first.1 = (f32[8,128]{1,0:T(8,128)S(1)}, f32[8,128]{1,0:T(8,128)S(1)}, f32[16,8,128]{2,1,0:T(8,128)S(1)}) custom-call(f32[16,8,128]{2,1,0:T(8,128)S(1)} %all_to_all.21.recv_ref, s32[128,128]{1,0:T(8,128)S(1)} %get-tuple-element.22.refs_0_, s32[128,128]{1,0:T(8,128)S(1)} %get-tuple-element.23.refs_1_, s32[128,128]{1,0:T(8,128)S(1)} %get-tuple-element.24.refs_2_, ...), custom_call_target="tpu_custom_call" | custom-call | tf_op jit(solution)/shard_map/first/pallas_call | solution.py:461
  29.6 8.6 %all_to_all.22.recv_ref = f32[16,8,128]{2,1,0:T(8,128)S(1)} all-to-all(f32[16,8,128]{2,1,0:T(8,128)S(1)} %get-tuple-element.34), channel_id=1, replica_groups={{4,5,6,7,0,1,2,3,8,9,10,11,12,13,14,15},{20,21,22,23,16,17,18,19,24,25,..., dimensions={0} | all-to-all | bytes 131072 | tf_op jit(solution)/shard_map/all_to_all | solution.py:415
  38.2 1.2 %second.1 = (f32[8,128]{1,0:T(8,128)S(1)}, f32[16,1,128]{2,1,0:T(1,128)S(1)}) custom-call(f32[16,8,128]{2,1,0:T(8,128)S(1)} %all_to_all.22.recv_ref, f32[8,128]{1,0:T(8,128)S(1)} %get-tuple-element.35.right_ref, f32[8,128]{1,0:T(8,128)S(1)} %get-tuple-element.36.share_ref, f32[8,128]{1,0:T(8,128)S(1)} %get-tuple-element.37.rank_ref, ...), custom_call_target="tpu_custom_call" | custom-call | tf_op jit(solution)/shard_map/second/pallas_call | solution.py:469
  39.4 8.5 %all_to_all.23.recv_ref = f32[16,1,128]{2,1,0:T(1,128)S(1)} all-to-all(f32[16,1,128]{2,1,0:T(1,128)S(1)} %get-tuple-element.39), channel_id=1, replica_groups={{4,5,6,7,0,1,2,3,8,9,10,11,12,13,14,15},{20,21,22,23,16,17,18,19,24,25,..., dimensions={0} | all-to-all | bytes 16384 | tf_op jit(solution)/shard_map/all_to_all | solution.py:415
  47.8 0.7 %finish.1 = (f32[2,32]{1,0:T(2,128)}, f32[2,32]{1,0:T(2,128)}) custom-call(f32[8,128]{1,0:T(8,128)S(1)} %get-tuple-element.38.own_ref, f32[16,1,128]{2,1,0:T(1,128)S(1)} %all_to_all.23.recv_ref), custom_call_target="tpu_custom_call" | custom-call | tf_op jit(solution)/shard_map/finish/pallas_call | solution.py:478

commit v12 on v11

--- a/solution.py
+++ b/solution.py
@@ -256,8 +256,8 @@
     return between(from_slots(ended, slots * 2 * NBASE // capacity // 128), NBASE)
 
 
-def setup_kernel(owners, capacity, recv_ref, part_ref, base_ref, sbase_ref, pixel_ref, cos_ref, sin_ref,
-                 scos_ref, ssin_ref, weight_ref, ends_ref, bounds_ref, same_ref, inv_ref, rank_ref, rows):
+def setup_kernel(owners, capacity, recv_ref, part_ref, pixel_ref, cos_ref, sin_ref, scos_ref, ssin_ref, weight_ref,
+                 ends_ref, bounds_ref, same_ref, inv_ref, near_ref, group_ref, order_ref, rank_ref, rows):
     slots = owners * capacity
     pair_rows = 3 * capacity + 1
     lane_tile, lane_block, lane_weight, lane_rank = fact_lanes(capacity)
@@ -266,47 +266,56 @@
         mine = slice(other * capacity, (other + 1) * capacity)
         for number in range(3):
             rows[number, mine, :] = recv_ref[start + number * capacity:start + (number + 1) * capacity, :]
-        fact = recv_ref[start + pair_rows - 1:start + pair_rows, :]
-        rows[3, mine, :] = jnp.broadcast_to(fact, (capacity, 128))
-    tod, angle, pixel_f, facts = rows[0], rows[1], rows[2], rows[3].astype(i32)
+        rows[3, other:other + 1, :] = recv_ref[start + pair_rows - 1:start + pair_rows, :]
+    tod, angle, pixel_f = rows[0], rows[1], rows[2]
     lane = iota((slots, 128), 1)
     slot = iota((slots, 128), 0)
+    keys = sort_lanes(pixel_f * 128.0 + lane.astype(f32))
+    order = keys.astype(i32) & 127
+    order_ref[...] = order
     pixel = pixel_f.astype(i32)
     pixel_ref[...] = pixel
     sine, cosine = sin_cos_double(angle)
     sin_ref[...] = sine
     cos_ref[...] = cosine
 
-    within = slot % capacity
-    tile = lanes_at(facts, lane_tile + within) - 1
-    block = lanes_at(facts, lane_block + within)
+    facts = rows[3, 0:owners, :]
+    few = iota(facts.shape, 1)
+    rank_ref[...] = jnp.broadcast_to(facts[0:1, lane_rank:lane_rank + 1], (8, 128))
+
+    def from_facts(index):
+        return to_slots(lanes_at(facts, index), slots)
+
+    spread = to_slots(facts, slots)
+    ones = jnp.ones((128, 128), bf16)
+
+    def own_lane(first):
+        mine = jnp.where(lane == first + slot % capacity, spread, 0.0)
+        return mm(mine.astype(bf16), ones).astype(i32)
+
+    tile = own_lane(lane_tile) - 1
+    block = own_lane(lane_block)
     odd = block & 1
-    start = (block >> 1) * SB
-    weight = lanes_at(rows[3], lane_weight + odd)
+    weight = jnp.where(odd == 1, from_facts(jnp.full(few.shape, lane_weight + 1, i32)),
+                       from_facts(jnp.full(few.shape, lane_weight, i32)))
     weight_ref[...] = weight
-    tile_row = tile.astype(f32).T[0:1]
-    tile_column = jnp.concatenate([tile.astype(f32)] * (slots // 128), axis=1)
-    same = (tile_column == jnp.where(tile_row < 0.0, -2.0, tile_row)).astype(f32).astype(bf16)
+    hot = (tile == lane).astype(f32).astype(bf16)
+    same = lax.dot_general(hot, hot, (((1,), (1,)), ((), ())), preferred_element_type=f32).astype(bf16)
     same_ref[...] = same
-    rank_ref[...] = jnp.broadcast_to(facts[0:1, lane_rank:lane_rank + 1].astype(f32), (8, 128))
     group = (((slot // capacity) & 1) << 1) + odd
-    first = odd << 5
-    bounds = jnp.clip(lanes_at(facts, (lane & 31) + first) - start, 0, SB)
-    bounds = jnp.where(((lane >> 5) == group) & (tile >= 0), bounds, 0)
+    group_ref[...] = group
+    near = jnp.where(odd == 1, from_facts((few & 31) + NBASE), from_facts(few & 31)).astype(i32)
+    near = jnp.clip(near - (block >> 1) * SB, 0, SB)
+    near_ref[...] = near
+    bounds = jnp.where(((lane >> 5) == group) & (tile >= 0), near, 0)
     bounds_ref[...] = bounds
 
-    base = jnp.zeros((slots, 128), i32)
-    moment = start + lane
-    for step in (16, 8, 4, 2, 1):
-        base = base + jnp.where(lanes_at(facts, base + (first + (step - 1))) <= moment, step, 0)
-    base = base + (group << 5)
-    base_ref[...] = base
-
-    keys = sort_lanes(pixel_f * 128.0 + lane.astype(f32))
-    order = keys.astype(i32) & 127
-    ends = count_up_to(keys, lane.astype(f32) * 128.0 + 127.0)
+    limit = lane.astype(f32) * 128.0 + 127.0
+    ends = jnp.zeros((slots, 128), i32)
+    for step in (64, 32, 16, 8, 4, 2, 1):
+        ends = ends + jnp.where(lanes_at(keys, ends + (step - 1)) <= limit, step, 0)
+    ends = ends + jnp.where(lanes_at(keys, ends) <= limit, 1, 0)
     ends_ref[...] = ends
-    sbase_ref[...] = lanes_at(base, order)
     scos = lanes_at(cosine, order)
     ssin = lanes_at(sine, order)
     wtod = weight * lanes_at(tod, order)
@@ -326,6 +335,17 @@
         inv_ref[number] = values
     part = map_to_baselines(capacity, sums[0:3], inverse, tod, pixel, cosine, sine, weight, bounds)
     part_ref[...] = jnp.broadcast_to(part[None], part_ref.shape)
+
+
+def bases_kernel(near_ref, group_ref, order_ref, base_ref, sbase_ref):
+    near = near_ref[...]
+    lane = iota(near.shape, 1)
+    base = jnp.zeros(near.shape, i32)
+    for step in (16, 8, 4, 2, 1):
+        base = base + jnp.where(lanes_at(near, base + (step - 1)) <= lane, step, 0)
+    base = base + (group_ref[...] << 5)
+    base_ref[...] = base
+    sbase_ref[...] = lanes_at(base, order_ref[...])
 
 
 def apply(capacity, vector, base_ref, sbase_ref, pixel_ref, cos_ref, sin_ref, scos_ref, ssin_ref,
@@ -447,17 +467,28 @@
 
     vector_shape = jax.ShapeDtypeStruct((vec_rows, 128), f32)
     parts_shape = jax.ShapeDtypeStruct((owners, vec_rows, 128), f32)
-    part, *state, rank = pl.pallas_call(
+    part, *state, near, group, order, rank = pl.pallas_call(
         functools.partial(setup_kernel, owners, capacity),
-        out_shape=(parts_shape, lanes(i32), lanes(i32), lanes(i32), lanes(f32), lanes(f32), lanes(f32), lanes(f32),
-                   lanes(f32), lanes(i32), lanes(i32), jax.ShapeDtypeStruct((slots, slots), bf16),
-                   jax.ShapeDtypeStruct((6, slots, 128), f32), jax.ShapeDtypeStruct((8, 128), f32)),
+        out_shape=(parts_shape, lanes(i32), lanes(f32), lanes(f32), lanes(f32), lanes(f32), lanes(f32), lanes(i32),
+                   lanes(i32), jax.ShapeDtypeStruct((slots, slots), bf16),
+                   jax.ShapeDtypeStruct((6, slots, 128), f32), lanes(i32), lanes(i32), lanes(i32),
+                   jax.ShapeDtypeStruct((8, 128), f32)),
         in_specs=whole(1),
-        out_specs=tuple(whole(14)),
+        out_specs=tuple(whole(15)),
         scratch_shapes=[pltpu.VMEM((4, slots, 128), f32)],
         compiler_params=PARAMS,
         name="setup",
     )(recv)
+    bases = pl.pallas_call(
+        bases_kernel,
+        out_shape=(lanes(i32), lanes(i32)),
+        in_specs=whole(3),
+        out_specs=tuple(whole(2)),
+        compiler_params=PARAMS,
+        cost_estimate=pl.CostEstimate(flops=100_000_000, bytes_accessed=5 * slots * 512, transcendentals=0),
+        name="bases",
+    )(near, group, order)
+    state = list(bases) + state
     right, share, part = pl.pallas_call(
         functools.partial(first_kernel, capacity),
         out_shape=(vector_shape, vector_shape, parts_shape),

time: 48.9 us -> 49.9 us (1.020)
  blocking collectives: 40.6 us -> 30.9 us
  starting transfers between devices: 0 us -> 5.34 us
  waiting for transfers between devices: 0 us -> 4.68 us
  Pallas kernels: 7.37 us -> 7.92 us
    all_to_all x4 -> x3, blocking collectives: 40.6 us -> 30.9 us  [send_out(): lax.all_to_all(rows, AXES, split_axis=0, concat_axis=0, tiled=True, axis_...]
    all_to_all x0 -> x1, starting transfers between devices: none -> 5.34 us  [send_out(): lax.all_to_all(rows, AXES, split_axis=0, concat_axis=0, tiled=True, axis_...]
    all_to_all x0 -> x1, waiting for transfers between devices: none -> 4.68 us  [send_out(): lax.all_to_all(rows, AXES, split_axis=0, concat_axis=0, tiled=True, axis_...]
  transfers between devices with their start and end apart: 0 -> 1, of which waited for: 0 -> 1; matrix products, arithmetic and copies ran while one was open for 0% -> 0% of each run, Pallas kernels for 0% -> 1%
where the time goes in v12:
time: 49.9 us; the launch traced here: 49.5 us
  blocking collectives  30.9 us (62%)
  Pallas kernels  7.92 us (16%)
  starting transfers between devices  5.34 us (11%)
  waiting for transfers between devices  4.68 us (9%)
  between operations  0.64 us (1%)
    all_to_all x3, blocking collectives, send_out(): lax.all_to_all(rows, AXES, split_axis=0, concat_axis=0, tiled=True, axis_...  30.9 us
    all_to_all x1, starting transfers between devices, send_out(): lax.all_to_all(rows, AXES, split_axis=0, concat_axis=0, tiled=True, axis_...  5.34 us
    all_to_all x1, waiting for transfers between devices, send_out(): lax.all_to_all(rows, AXES, split_axis=0, concat_axis=0, tiled=True, axis_...  4.68 us
    pallas_call x1, Pallas kernels, on_device(): pl.pallas_call(functools.partial(setup_kernel, owners, capacity), out_sha...  2.7 us
    pallas_call x1, Pallas kernels, on_device(): pl.pallas_call(functools.partial(pack_kernel, owners, capacity), out_shap...  1.74 us
    pallas_call x1, Pallas kernels, on_device(): pl.pallas_call(functools.partial(second_kernel, capacity), out_shape=(jax...  1.17 us
    pallas_call x1, Pallas kernels, on_device(): pl.pallas_call(functools.partial(first_kernel, capacity), out_shape=(vect...  1.09 us
  transfers between devices with their start and end apart: 1, of which 1 were waited for; matrix products, arithmetic and copies ran while one was open for 0% of the time, Pallas kernels for 1%

profile of v12, /device:TPU:0, one launch (start us, length us, event | category | flops | bytes accessed | tf_op | source)
XLA Modules:
  0.0 49.5 jit_solution(11931287135935822146)
XLA Ops:
  0.6 1.7 %pack.1 = f32[400,128]{1,0:T(8,128)S(1)} custom-call(f32[2,6400]{1,0:T(2,128)} %tod_hbm.1, f32[2,6400]{1,0:T(2,128)} %angle_hbm.1, s32[2,6400]{1,0:T(2,128)} %pixel_hbm.1, s32[2,6400]{1,0:T(2,128)} %base_hbm.1, s32[2,50]{1,0:T(2,128)} %bitcast.5, s32[2,50]{1,0:T(2,128)} %tile_hbm.1, f32[2]{0:T(128)} %weight_hbm.1), custom_call_target="tpu_custom_call" | custom-call | tf_op jit(solution)/shard_map/pack/pallas_call | solution.py:447
  2.4 13.9 %all_to_all.20 = f32[16,25,1,128]{3,2,1,0:T(1,128)S(1)} all-to-all(f32[16,25,1,128]{3,2,1,0:T(1,128)S(1)} %bitcast.4), channel_id=1, replica_groups={{4,5,6,7,0,1,2,3,8,9,10,11,12,13,14,15},{20,21,22,23,16,17,18,19,24,25,..., dimensions={0} | all-to-all | bytes 409600 | tf_op jit(solution)/shard_map/all_to_all | solution.py:435
  16.3 2.7 %setup.1 = (f32[16,8,128]{2,1,0:T(8,128)}, s32[128,128]{1,0:T(8,128)S(1)}, f32[128,128]{1,0:T(8,128)S(1)}, f32[128,128]{1,0:T(8,128)S(1)}, f32[128,128]{1,0:T(8,...) custom-call(f32[400,128]{1,0:T(8,128)S(1)} %bitcast.3), custom_call_target="tpu_custom_call" | custom-call | tf_op jit(solution)/shard_map/setup/pallas_call | solution.py:470
  19.0 5.3 %all-to-all-start.1 = ((f32[16,8,128]{2,1,0:T(8,128)}), f32[16,8,128]{2,1,0:T(8,128)S(1)}, u32[]{:S(2)}, u32[]{:S(2)}) async-start(f32[16,8,128]{2,1,0:T(8,128)} %get-tuple-element.24), calls=%async_computation.1 | async-start | bytes 131072 | tf_op jit(solution)/shard_map/all_to_all | solution.py:435
  24.3 0.5 bases.1
  24.8 4.7 %all-to-all-done.1.recv_ref = f32[16,8,128]{2,1,0:T(8,128)S(1)} async-done(((f32[16,8,128]{2,1,0:T(8,128)}), f32[16,8,128]{2,1,0:T(8,128)S(1)}, u32[]{:S(2)}, u32[]{:S(2)}) %all-to-all-start.1) | async-done | bytes 65568 | tf_op jit(solution)/shard_map/all_to_all | solution.py:435
  29.5 1.1 %first.1 = (f32[8,128]{1,0:T(8,128)S(1)}, f32[8,128]{1,0:T(8,128)S(1)}, f32[16,8,128]{2,1,0:T(8,128)S(1)}) custom-call(f32[16,8,128]{2,1,0:T(8,128)S(1)} %all-to-all-done.1.recv_ref, s32[128,128]{1,0:T(8,128)S(1)} %get-tuple-element.28.refs_0_, s32[128,128]{1,0:T(8,128)S(1)} %get-tuple-element.29.refs_1_, s32[128,128]{1,0:T(8,128)S(1)} %get-tuple-element.30.refs_2_, ...), custom_call_target="tpu_custom_call" | custom-call | tf_op jit(solution)/shard_map/first/pallas_call | solution.py:492
  30.6 8.6 %all_to_all.21.recv_ref = f32[16,8,128]{2,1,0:T(8,128)S(1)} all-to-all(f32[16,8,128]{2,1,0:T(8,128)S(1)} %get-tuple-element.40), channel_id=1, replica_groups={{4,5,6,7,0,1,2,3,8,9,10,11,12,13,14,15},{20,21,22,23,16,17,18,19,24,25,..., dimensions={0} | all-to-all | bytes 131072 | tf_op jit(solution)/shard_map/all_to_all | solution.py:435
  39.2 1.2 %second.1 = (f32[8,128]{1,0:T(8,128)S(1)}, f32[16,1,128]{2,1,0:T(1,128)S(1)}) custom-call(f32[16,8,128]{2,1,0:T(8,128)S(1)} %all_to_all.21.recv_ref, f32[8,128]{1,0:T(8,128)S(1)} %get-tuple-element.41.right_ref, f32[8,128]{1,0:T(8,128)S(1)} %get-tuple-element.42.share_ref, f32[8,128]{1,0:T(8,128)S(1)} %get-tuple-element.43.rank_ref, ...), custom_call_target="tpu_custom_call" | custom-call | tf_op jit(solution)/shard_map/second/pallas_call | solution.py:500
  40.3 8.5 %all_to_all.22.recv_ref = f32[16,1,128]{2,1,0:T(1,128)S(1)} all-to-all(f32[16,1,128]{2,1,0:T(1,128)S(1)} %get-tuple-element.45), channel_id=1, replica_groups={{4,5,6,7,0,1,2,3,8,9,10,11,12,13,14,15},{20,21,22,23,16,17,18,19,24,25,..., dimensions={0} | all-to-all | bytes 16384 | tf_op jit(solution)/shard_map/all_to_all | solution.py:435
  48.8 0.7 %finish.1 = (f32[2,32]{1,0:T(2,128)}, f32[2,32]{1,0:T(2,128)}) custom-call(f32[8,128]{1,0:T(8,128)S(1)} %get-tuple-element.44.own_ref, f32[16,1,128]{2,1,0:T(1,128)S(1)} %all_to_all.22.recv_ref), custom_call_target="tpu_custom_call" | custom-call | tf_op jit(solution)/shard_map/finish/pallas_call | solution.py:509
Async XLA Ops:
  19.0 10.5 %all-to-all-start.1 = ((f32[16,8,128]{2,1,0:T(8,128)}), f32[16,8,128]{2,1,0:T(8,128)S(1)}, u32[]{:S(2)}, u32[]{:S(2)}) async-start(f32[16,8,128]{2,1,0:T(8,128)} %get-tuple-element.24), calls=%async_computation.1 | async-start | bytes 131072 | tf_op jit(solution)/shard_map/all_to_all | solution.py:435

commit v13 on v11

--- a/solution.py
+++ b/solution.py
@@ -50,11 +50,15 @@
     return jnp.dot(left, right, preferred_element_type=f32)
 
 
-def left_hot(left, right, terms=2):
+def left_hot(left, right, terms=2, apart=False):
+    if apart:
+        return sum(mm(left, term) for term in reversed(split(right, terms)))
     return mm(jnp.concatenate([left] * terms, axis=1), jnp.concatenate(split(right, terms), axis=0))
 
 
-def right_hot(left, right, terms=2):
+def right_hot(left, right, terms=2, apart=False):
+    if apart:
+        return sum(mm(term, right) for term in reversed(split(left, terms)))
     return mm(jnp.concatenate(split(left, terms), axis=1), jnp.concatenate([right] * terms, axis=0))
 
 
@@ -304,7 +308,11 @@
 
     keys = sort_lanes(pixel_f * 128.0 + lane.astype(f32))
     order = keys.astype(i32) & 127
-    ends = count_up_to(keys, lane.astype(f32) * 128.0 + 127.0)
+    limit = lane.astype(f32) * 128.0 + 127.0
+    ends = jnp.zeros((slots, 128), i32)
+    for step in (64, 32, 16, 8, 4, 2, 1):
+        ends = ends + jnp.where(lanes_at(keys, ends + (step - 1)) <= limit, step, 0)
+    ends = ends + jnp.where(lanes_at(keys, ends) <= limit, 1, 0)
     ends_ref[...] = ends
     sbase_ref[...] = lanes_at(base, order)
     scos = lanes_at(cosine, order)
@@ -316,10 +324,10 @@
 
     stacked = jnp.concatenate(
         [wtod, scos * wtod, ssin * wtod, wcos, weight * ssin, wcos * scos, wcos * ssin], axis=0)
-    prefix = right_hot(stacked, upper())
+    prefix = right_hot(stacked, upper(), apart=True)
     binned = [between(at_ends(prefix[n * slots:(n + 1) * slots], ends), 128) for n in range(7)]
     binned.append(weight * between(ends.astype(f32), 128))
-    sums = left_hot(same, jnp.concatenate(binned, axis=1))
+    sums = left_hot(same, jnp.concatenate(binned, axis=1), apart=True)
     sums = [sums[:, 128 * n:128 * (n + 1)] for n in range(8)]
     inverse = cofactors([sums[7], sums[3], sums[4], sums[5], sums[6], sums[7] - sums[5]])
     for number, values in enumerate(inverse):

time: 48.9 us -> 48.6 us (level)
  no operation moved by 1% of the time
where the time goes in v13:
time: 48.6 us; the launch traced here: 48.3 us
  blocking collectives  40.6 us (84%)
  Pallas kernels  7.12 us (15%)
  between operations  0.64 us (1%)
    all_to_all x4, blocking collectives, send_out(): lax.all_to_all(rows, AXES, split_axis=0, concat_axis=0, tiled=True, axis_...  40.6 us
    pallas_call x1, Pallas kernels, on_device(): pl.pallas_call(functools.partial(setup_kernel, owners, capacity), out_sha...  2.37 us
    pallas_call x1, Pallas kernels, on_device(): pl.pallas_call(functools.partial(pack_kernel, owners, capacity), out_shap...  1.74 us
    pallas_call x1, Pallas kernels, on_device(): pl.pallas_call(functools.partial(second_kernel, capacity), out_shape=(jax...  1.17 us
    pallas_call x1, Pallas kernels, on_device(): pl.pallas_call(functools.partial(first_kernel, capacity), out_shape=(vect...  1.09 us

profile of v13, /device:TPU:0, one launch (start us, length us, event | category | flops | bytes accessed | tf_op | source)
XLA Modules:
  0.0 48.3 jit_solution(15405617432301397874)
XLA Ops:
  0.6 1.7 %pack.1 = f32[400,128]{1,0:T(8,128)S(1)} custom-call(f32[2,6400]{1,0:T(2,128)} %tod_hbm.1, f32[2,6400]{1,0:T(2,128)} %angle_hbm.1, s32[2,6400]{1,0:T(2,128)} %pixel_hbm.1, s32[2,6400]{1,0:T(2,128)} %base_hbm.1, s32[2,50]{1,0:T(2,128)} %bitcast.5, s32[2,50]{1,0:T(2,128)} %tile_hbm.1, f32[2]{0:T(128)} %weight_hbm.1), custom_call_target="tpu_custom_call" | custom-call | tf_op jit(solution)/shard_map/pack/pallas_call | solution.py:435
  2.4 13.9 %all_to_all.20 = f32[16,25,1,128]{3,2,1,0:T(1,128)S(1)} all-to-all(f32[16,25,1,128]{3,2,1,0:T(1,128)S(1)} %bitcast.4), channel_id=1, replica_groups={{4,5,6,7,0,1,2,3,8,9,10,11,12,13,14,15},{20,21,22,23,16,17,18,19,24,25,..., dimensions={0} | all-to-all | bytes 409600 | tf_op jit(solution)/shard_map/all_to_all | solution.py:423
  16.3 2.4 %setup.1 = (f32[16,8,128]{2,1,0:T(8,128)S(1)}, s32[128,128]{1,0:T(8,128)S(1)}, s32[128,128]{1,0:T(8,128)S(1)}, s32[128,128]{1,0:T(8,128)S(1)}, f32[128,128]{1,0:...) custom-call(f32[400,128]{1,0:T(8,128)S(1)} %bitcast.3), custom_call_target="tpu_custom_call" | custom-call | tf_op jit(solution)/shard_map/setup/pallas_call | solution.py:458
  18.7 9.6 %all_to_all.21.recv_ref = f32[16,8,128]{2,1,0:T(8,128)S(1)} all-to-all(f32[16,8,128]{2,1,0:T(8,128)S(1)} %get-tuple-element.21), channel_id=1, replica_groups={{4,5,6,7,0,1,2,3,8,9,10,11,12,13,14,15},{20,21,22,23,16,17,18,19,24,25,..., dimensions={0} | all-to-all | bytes 131072 | tf_op jit(solution)/shard_map/all_to_all | solution.py:423
  28.3 1.1 %first.1 = (f32[8,128]{1,0:T(8,128)S(1)}, f32[8,128]{1,0:T(8,128)S(1)}, f32[16,8,128]{2,1,0:T(8,128)S(1)}) custom-call(f32[16,8,128]{2,1,0:T(8,128)S(1)} %all_to_all.21.recv_ref, s32[128,128]{1,0:T(8,128)S(1)} %get-tuple-element.22.refs_0_, s32[128,128]{1,0:T(8,128)S(1)} %get-tuple-element.23.refs_1_, s32[128,128]{1,0:T(8,128)S(1)} %get-tuple-element.24.refs_2_, ...), custom_call_target="tpu_custom_call" | custom-call | tf_op jit(solution)/shard_map/first/pallas_call | solution.py:469
  29.4 8.6 %all_to_all.22.recv_ref = f32[16,8,128]{2,1,0:T(8,128)S(1)} all-to-all(f32[16,8,128]{2,1,0:T(8,128)S(1)} %get-tuple-element.34), channel_id=1, replica_groups={{4,5,6,7,0,1,2,3,8,9,10,11,12,13,14,15},{20,21,22,23,16,17,18,19,24,25,..., dimensions={0} | all-to-all | bytes 131072 | tf_op jit(solution)/shard_map/all_to_all | solution.py:423
  37.9 1.2 %second.1 = (f32[8,128]{1,0:T(8,128)S(1)}, f32[16,1,128]{2,1,0:T(1,128)S(1)}) custom-call(f32[16,8,128]{2,1,0:T(8,128)S(1)} %all_to_all.22.recv_ref, f32[8,128]{1,0:T(8,128)S(1)} %get-tuple-element.35.right_ref, f32[8,128]{1,0:T(8,128)S(1)} %get-tuple-element.36.share_ref, f32[8,128]{1,0:T(8,128)S(1)} %get-tuple-element.37.rank_ref, ...), custom_call_target="tpu_custom_call" | custom-call | tf_op jit(solution)/shard_map/second/pallas_call | solution.py:477
  39.1 8.5 %all_to_all.23.recv_ref = f32[16,1,128]{2,1,0:T(1,128)S(1)} all-to-all(f32[16,1,128]{2,1,0:T(1,128)S(1)} %get-tuple-element.39), channel_id=1, replica_groups={{4,5,6,7,0,1,2,3,8,9,10,11,12,13,14,15},{20,21,22,23,16,17,18,19,24,25,..., dimensions={0} | all-to-all | bytes 16384 | tf_op jit(solution)/shard_map/all_to_all | solution.py:423
  47.6 0.7 %finish.1 = (f32[2,32]{1,0:T(2,128)}, f32[2,32]{1,0:T(2,128)}) custom-call(f32[8,128]{1,0:T(8,128)S(1)} %get-tuple-element.38.own_ref, f32[16,1,128]{2,1,0:T(1,128)S(1)} %all_to_all.23.recv_ref), custom_call_target="tpu_custom_call" | custom-call | tf_op jit(solution)/shard_map/finish/pallas_call | solution.py:486

commit v14 on v13

--- a/solution.py
+++ b/solution.py
@@ -193,13 +193,15 @@
     return lanes_at(mixed, ((lane & 15) << 3) + (lane >> 4))
 
 
-def at_ends(prefix, ends):
-    return jnp.where(ends > 0, lanes_at(prefix, jnp.maximum(ends - 1, 0)), 0.0)
-
-
-def between(values, period):
-    first = (iota(values.shape, 1) & (period - 1)) == 0
-    return values - jnp.where(first, 0.0, pltpu.roll(values, 1, 1))
+def at_ends(ends):
+    filled = ends > 0
+    last = jnp.maximum(ends - 1, 0)
+    return lambda prefix: jnp.where(filled, lanes_at(prefix, last), 0.0)
+
+
+def between(period, shape):
+    first = (iota(shape, 1) & (period - 1)) == 0
+    return lambda values: values - jnp.where(first, 0.0, pltpu.roll(values, 1, 1))
 
 
 def cofactors(hit_sums):
@@ -256,8 +258,9 @@
     rest = signal - lanes_at(sky[0], pixel)
     rest = rest - cosine * lanes_at(sky[1], pixel)
     rest = rest - sine * lanes_at(sky[2], pixel)
-    ended = at_ends(right_hot(weight * rest, upper()), bounds)
-    return between(from_slots(ended, slots * 2 * NBASE // capacity // 128), NBASE)
+    ended = at_ends(bounds)(right_hot(weight * rest, upper()))
+    part = from_slots(ended, slots * 2 * NBASE // capacity // 128)
+    return between(NBASE, part.shape)(part)
 
 
 def setup_kernel(owners, capacity, recv_ref, part_ref, base_ref, sbase_ref, pixel_ref, cos_ref, sin_ref,
@@ -308,11 +311,7 @@
 
     keys = sort_lanes(pixel_f * 128.0 + lane.astype(f32))
     order = keys.astype(i32) & 127
-    limit = lane.astype(f32) * 128.0 + 127.0
-    ends = jnp.zeros((slots, 128), i32)
-    for step in (64, 32, 16, 8, 4, 2, 1):
-        ends = ends + jnp.where(lanes_at(keys, ends + (step - 1)) <= limit, step, 0)
-    ends = ends + jnp.where(lanes_at(keys, ends) <= limit, 1, 0)
+    ends = count_up_to(keys, lane.astype(f32) * 128.0 + 127.0)
     ends_ref[...] = ends
     sbase_ref[...] = lanes_at(base, order)
     scos = lanes_at(cosine, order)
@@ -325,8 +324,9 @@
     stacked = jnp.concatenate(
         [wtod, scos * wtod, ssin * wtod, wcos, weight * ssin, wcos * scos, wcos * ssin], axis=0)
     prefix = right_hot(stacked, upper(), apart=True)
-    binned = [between(at_ends(prefix[n * slots:(n + 1) * slots], ends), 128) for n in range(7)]
-    binned.append(weight * between(ends.astype(f32), 128))
+    read, differ = at_ends(ends), between(128, ends.shape)
+    binned = [differ(read(prefix[n * slots:(n + 1) * slots])) for n in range(7)]
+    binned.append(weight * differ(ends.astype(f32)))
     sums = left_hot(same, jnp.concatenate(binned, axis=1), apart=True)
     sums = [sums[:, 128 * n:128 * (n + 1)] for n in range(8)]
     inverse = cofactors([sums[7], sums[3], sums[4], sums[5], sums[6], sums[7] - sums[5]])
@@ -345,9 +345,8 @@
     weighted = weight * lanes_at(levels, sbase_ref[...])
     stacked = jnp.concatenate([weighted, scos_ref[...] * weighted, ssin_ref[...] * weighted], axis=0)
     prefix = right_hot(stacked, upper())
-    ends = ends_ref[...]
-    binned = jnp.concatenate(
-        [between(at_ends(prefix[n * slots:(n + 1) * slots], ends), 128) for n in range(3)], axis=1)
+    read, differ = at_ends(ends_ref[...]), between(128, pixel_ref.shape)
+    binned = jnp.concatenate([differ(read(prefix[n * slots:(n + 1) * slots])) for n in range(3)], axis=1)
     sums = left_hot(same_ref[...], binned)
     return map_to_baselines(
         capacity, [sums[:, 128 * n:128 * (n + 1)] for n in range(3)], [inv_ref[n] for n in range(6)], signal,

time: 48.6 us -> 49 us (level)
  no operation moved by 1% of the time
where the time goes in v14:
time: 49 us; the launch traced here: 48.7 us
  blocking collectives  40.6 us (83%)
  Pallas kernels  7.45 us (15%)
  between operations  0.64 us (1%)
    all_to_all x4, blocking collectives, send_out(): lax.all_to_all(rows, AXES, split_axis=0, concat_axis=0, tiled=True, axis_...  40.6 us
    pallas_call x1, Pallas kernels, on_device(): pl.pallas_call(functools.partial(setup_kernel, owners, capacity), out_sha...  2.71 us
    pallas_call x1, Pallas kernels, on_device(): pl.pallas_call(functools.partial(pack_kernel, owners, capacity), out_shap...  1.74 us
    pallas_call x1, Pallas kernels, on_device(): pl.pallas_call(functools.partial(second_kernel, capacity), out_shape=(jax...  1.17 us
    pallas_call x1, Pallas kernels, on_device(): pl.pallas_call(functools.partial(first_kernel, capacity), out_shape=(vect...  1.09 us

profile of v14, /device:TPU:0, one launch (start us, length us, event | category | flops | bytes accessed | tf_op | source)
XLA Modules:
  0.0 48.7 jit_solution(8968619014245338406)
XLA Ops:
  0.6 1.7 %pack.1 = f32[400,128]{1,0:T(8,128)S(1)} custom-call(f32[2,6400]{1,0:T(2,128)} %tod_hbm.1, f32[2,6400]{1,0:T(2,128)} %angle_hbm.1, s32[2,6400]{1,0:T(2,128)} %pixel_hbm.1, s32[2,6400]{1,0:T(2,128)} %base_hbm.1, s32[2,50]{1,0:T(2,128)} %bitcast.5, s32[2,50]{1,0:T(2,128)} %tile_hbm.1, f32[2]{0:T(128)} %weight_hbm.1), custom_call_target="tpu_custom_call" | custom-call | tf_op jit(solution)/shard_map/pack/pallas_call | solution.py:434
  2.4 13.9 %all_to_all.20 = f32[16,25,1,128]{3,2,1,0:T(1,128)S(1)} all-to-all(f32[16,25,1,128]{3,2,1,0:T(1,128)S(1)} %bitcast.4), channel_id=1, replica_groups={{4,5,6,7,0,1,2,3,8,9,10,11,12,13,14,15},{20,21,22,23,16,17,18,19,24,25,..., dimensions={0} | all-to-all | bytes 409600 | tf_op jit(solution)/shard_map/all_to_all | solution.py:422
  16.3 2.7 %setup.1 = (f32[16,8,128]{2,1,0:T(8,128)S(1)}, s32[128,128]{1,0:T(8,128)S(1)}, s32[128,128]{1,0:T(8,128)S(1)}, s32[128,128]{1,0:T(8,128)S(1)}, f32[128,128]{1,0:...) custom-call(f32[400,128]{1,0:T(8,128)S(1)} %bitcast.3), custom_call_target="tpu_custom_call" | custom-call | tf_op jit(solution)/shard_map/setup/pallas_call | solution.py:457
  19.0 9.6 %all_to_all.21.recv_ref = f32[16,8,128]{2,1,0:T(8,128)S(1)} all-to-all(f32[16,8,128]{2,1,0:T(8,128)S(1)} %get-tuple-element.21), channel_id=1, replica_groups={{4,5,6,7,0,1,2,3,8,9,10,11,12,13,14,15},{20,21,22,23,16,17,18,19,24,25,..., dimensions={0} | all-to-all | bytes 131072 | tf_op jit(solution)/shard_map/all_to_all | solution.py:422
  28.6 1.1 %first.1 = (f32[8,128]{1,0:T(8,128)S(1)}, f32[8,128]{1,0:T(8,128)S(1)}, f32[16,8,128]{2,1,0:T(8,128)S(1)}) custom-call(f32[16,8,128]{2,1,0:T(8,128)S(1)} %all_to_all.21.recv_ref, s32[128,128]{1,0:T(8,128)S(1)} %get-tuple-element.22.refs_0_, s32[128,128]{1,0:T(8,128)S(1)} %get-tuple-element.23.refs_1_, s32[128,128]{1,0:T(8,128)S(1)} %get-tuple-element.24.refs_2_, ...), custom_call_target="tpu_custom_call" | custom-call | tf_op jit(solution)/shard_map/first/pallas_call | solution.py:468
  29.7 8.6 %all_to_all.22.recv_ref = f32[16,8,128]{2,1,0:T(8,128)S(1)} all-to-all(f32[16,8,128]{2,1,0:T(8,128)S(1)} %get-tuple-element.34), channel_id=1, replica_groups={{4,5,6,7,0,1,2,3,8,9,10,11,12,13,14,15},{20,21,22,23,16,17,18,19,24,25,..., dimensions={0} | all-to-all | bytes 131072 | tf_op jit(solution)/shard_map/all_to_all | solution.py:422
  38.3 1.2 %second.1 = (f32[8,128]{1,0:T(8,128)S(1)}, f32[16,1,128]{2,1,0:T(1,128)S(1)}) custom-call(f32[16,8,128]{2,1,0:T(8,128)S(1)} %all_to_all.22.recv_ref, f32[8,128]{1,0:T(8,128)S(1)} %get-tuple-element.35.right_ref, f32[8,128]{1,0:T(8,128)S(1)} %get-tuple-element.36.share_ref, f32[8,128]{1,0:T(8,128)S(1)} %get-tuple-element.37.rank_ref, ...), custom_call_target="tpu_custom_call" | custom-call | tf_op jit(solution)/shard_map/second/pallas_call | solution.py:476
  39.5 8.5 %all_to_all.23.recv_ref = f32[16,1,128]{2,1,0:T(1,128)S(1)} all-to-all(f32[16,1,128]{2,1,0:T(1,128)S(1)} %get-tuple-element.39), channel_id=1, replica_groups={{4,5,6,7,0,1,2,3,8,9,10,11,12,13,14,15},{20,21,22,23,16,17,18,19,24,25,..., dimensions={0} | all-to-all | bytes 16384 | tf_op jit(solution)/shard_map/all_to_all | solution.py:422
  47.9 0.7 %finish.1 = (f32[2,32]{1,0:T(2,128)}, f32[2,32]{1,0:T(2,128)}) custom-call(f32[8,128]{1,0:T(8,128)S(1)} %get-tuple-element.38.own_ref, f32[16,1,128]{2,1,0:T(1,128)S(1)} %all_to_all.23.recv_ref), custom_call_target="tpu_custom_call" | custom-call | tf_op jit(solution)/shard_map/finish/pallas_call | solution.py:485

commit v15 on v14

--- a/solution.py
+++ b/solution.py
@@ -40,25 +40,20 @@
 
 def count_up_to(ascending, level):
     found = jnp.zeros(ascending.shape, i32)
-    for probes, step in (((31, 63, 95), 32), ((7, 15, 23), 8), ((1, 3, 5), 2), ((0, 1), 1)):
-        met = [jnp.where(lanes_at(ascending, found + probe) <= level, step, 0) for probe in probes]
-        found = found + sum(met[1:], met[0])
-    return found
+    for step in (64, 32, 16, 8, 4, 2, 1):
+        found = found + jnp.where(lanes_at(ascending, found + (step - 1)) <= level, step, 0)
+    return found + jnp.where(lanes_at(ascending, found) <= level, 1, 0)
 
 
 def mm(left, right):
     return jnp.dot(left, right, preferred_element_type=f32)
 
 
-def left_hot(left, right, terms=2, apart=False):
-    if apart:
-        return sum(mm(left, term) for term in reversed(split(right, terms)))
+def left_hot(left, right, terms=2):
     return mm(jnp.concatenate([left] * terms, axis=1), jnp.concatenate(split(right, terms), axis=0))
 
 
-def right_hot(left, right, terms=2, apart=False):
-    if apart:
-        return sum(mm(term, right) for term in reversed(split(left, terms)))
+def right_hot(left, right, terms=2):
     return mm(jnp.concatenate(split(left, terms), axis=1), jnp.concatenate([right] * terms, axis=0))
 
 
@@ -323,11 +318,11 @@
 
     stacked = jnp.concatenate(
         [wtod, scos * wtod, ssin * wtod, wcos, weight * ssin, wcos * scos, wcos * ssin], axis=0)
-    prefix = right_hot(stacked, upper(), apart=True)
+    prefix = right_hot(stacked, upper())
     read, differ = at_ends(ends), between(128, ends.shape)
     binned = [differ(read(prefix[n * slots:(n + 1) * slots])) for n in range(7)]
     binned.append(weight * differ(ends.astype(f32)))
-    sums = left_hot(same, jnp.concatenate(binned, axis=1), apart=True)
+    sums = left_hot(same, jnp.concatenate(binned, axis=1))
     sums = [sums[:, 128 * n:128 * (n + 1)] for n in range(8)]
     inverse = cofactors([sums[7], sums[3], sums[4], sums[5], sums[6], sums[7] - sums[5]])
     for number, values in enumerate(inverse):

time: 49 us -> 49 us (level)
  no operation moved by 1% of the time
where the time goes in v15:
time: 49 us; the launch traced here: 48.6 us
  blocking collectives  40.6 us (83%)
  Pallas kernels  7.43 us (15%)
  between operations  0.64 us (1%)
    all_to_all x4, blocking collectives, send_out(): lax.all_to_all(rows, AXES, split_axis=0, concat_axis=0, tiled=True, axis_...  40.6 us
    pallas_call x1, Pallas kernels, on_device(): pl.pallas_call(functools.partial(setup_kernel, owners, capacity), out_sha...  2.46 us
    pallas_call x1, Pallas kernels, on_device(): pl.pallas_call(functools.partial(pack_kernel, owners, capacity), out_shap...  1.97 us
    pallas_call x1, Pallas kernels, on_device(): pl.pallas_call(functools.partial(second_kernel, capacity), out_shape=(jax...  1.17 us
    pallas_call x1, Pallas kernels, on_device(): pl.pallas_call(functools.partial(first_kernel, capacity), out_shape=(vect...  1.09 us

profile of v15, /device:TPU:0, one launch (start us, length us, event | category | flops | bytes accessed | tf_op | source)
XLA Modules:
  0.0 48.6 jit_solution(1362525667712521072)
XLA Ops:
  0.6 2.0 %pack.1 = f32[400,128]{1,0:T(8,128)S(1)} custom-call(f32[2,6400]{1,0:T(2,128)} %tod_hbm.1, f32[2,6400]{1,0:T(2,128)} %angle_hbm.1, s32[2,6400]{1,0:T(2,128)} %pixel_hbm.1, s32[2,6400]{1,0:T(2,128)} %base_hbm.1, s32[2,50]{1,0:T(2,128)} %bitcast.5, s32[2,50]{1,0:T(2,128)} %tile_hbm.1, f32[2]{0:T(128)} %weight_hbm.1), custom_call_target="tpu_custom_call" | custom-call | tf_op jit(solution)/shard_map/pack/pallas_call | solution.py:429
  2.6 13.9 %all_to_all.20 = f32[16,25,1,128]{3,2,1,0:T(1,128)S(1)} all-to-all(f32[16,25,1,128]{3,2,1,0:T(1,128)S(1)} %bitcast.4), channel_id=1, replica_groups={{4,5,6,7,0,1,2,3,8,9,10,11,12,13,14,15},{20,21,22,23,16,17,18,19,24,25,..., dimensions={0} | all-to-all | bytes 409600 | tf_op jit(solution)/shard_map/all_to_all | solution.py:417
  16.5 2.5 %setup.1 = (f32[16,8,128]{2,1,0:T(8,128)S(1)}, s32[128,128]{1,0:T(8,128)S(1)}, s32[128,128]{1,0:T(8,128)S(1)}, s32[128,128]{1,0:T(8,128)S(1)}, f32[128,128]{1,0:...) custom-call(f32[400,128]{1,0:T(8,128)S(1)} %bitcast.3), custom_call_target="tpu_custom_call" | custom-call | tf_op jit(solution)/shard_map/setup/pallas_call | solution.py:452
  19.0 9.6 %all_to_all.21.recv_ref = f32[16,8,128]{2,1,0:T(8,128)S(1)} all-to-all(f32[16,8,128]{2,1,0:T(8,128)S(1)} %get-tuple-element.21), channel_id=1, replica_groups={{4,5,6,7,0,1,2,3,8,9,10,11,12,13,14,15},{20,21,22,23,16,17,18,19,24,25,..., dimensions={0} | all-to-all | bytes 131072 | tf_op jit(solution)/shard_map/all_to_all | solution.py:417
  28.6 1.1 %first.1 = (f32[8,128]{1,0:T(8,128)S(1)}, f32[8,128]{1,0:T(8,128)S(1)}, f32[16,8,128]{2,1,0:T(8,128)S(1)}) custom-call(f32[16,8,128]{2,1,0:T(8,128)S(1)} %all_to_all.21.recv_ref, s32[128,128]{1,0:T(8,128)S(1)} %get-tuple-element.22.refs_0_, s32[128,128]{1,0:T(8,128)S(1)} %get-tuple-element.23.refs_1_, s32[128,128]{1,0:T(8,128)S(1)} %get-tuple-element.24.refs_2_, ...), custom_call_target="tpu_custom_call" | custom-call | tf_op jit(solution)/shard_map/first/pallas_call | solution.py:463
  29.7 8.6 %all_to_all.22.recv_ref = f32[16,8,128]{2,1,0:T(8,128)S(1)} all-to-all(f32[16,8,128]{2,1,0:T(8,128)S(1)} %get-tuple-element.34), channel_id=1, replica_groups={{4,5,6,7,0,1,2,3,8,9,10,11,12,13,14,15},{20,21,22,23,16,17,18,19,24,25,..., dimensions={0} | all-to-all | bytes 131072 | tf_op jit(solution)/shard_map/all_to_all | solution.py:417
  38.3 1.2 %second.1 = (f32[8,128]{1,0:T(8,128)S(1)}, f32[16,1,128]{2,1,0:T(1,128)S(1)}) custom-call(f32[16,8,128]{2,1,0:T(8,128)S(1)} %all_to_all.22.recv_ref, f32[8,128]{1,0:T(8,128)S(1)} %get-tuple-element.35.right_ref, f32[8,128]{1,0:T(8,128)S(1)} %get-tuple-element.36.share_ref, f32[8,128]{1,0:T(8,128)S(1)} %get-tuple-element.37.rank_ref, ...), custom_call_target="tpu_custom_call" | custom-call | tf_op jit(solution)/shard_map/second/pallas_call | solution.py:471
  39.4 8.5 %all_to_all.23.recv_ref = f32[16,1,128]{2,1,0:T(1,128)S(1)} all-to-all(f32[16,1,128]{2,1,0:T(1,128)S(1)} %get-tuple-element.39), channel_id=1, replica_groups={{4,5,6,7,0,1,2,3,8,9,10,11,12,13,14,15},{20,21,22,23,16,17,18,19,24,25,..., dimensions={0} | all-to-all | bytes 16384 | tf_op jit(solution)/shard_map/all_to_all | solution.py:417
  47.9 0.7 %finish.1 = (f32[2,32]{1,0:T(2,128)}, f32[2,32]{1,0:T(2,128)}) custom-call(f32[8,128]{1,0:T(8,128)S(1)} %get-tuple-element.38.own_ref, f32[16,1,128]{2,1,0:T(1,128)S(1)} %all_to_all.23.recv_ref), custom_call_target="tpu_custom_call" | custom-call | tf_op jit(solution)/shard_map/finish/pallas_call | solution.py:480

commit v16 on v13

--- a/solution.py
+++ b/solution.py
@@ -50,9 +50,7 @@
     return jnp.dot(left, right, preferred_element_type=f32)
 
 
-def left_hot(left, right, terms=2, apart=False):
-    if apart:
-        return sum(mm(left, term) for term in reversed(split(right, terms)))
+def left_hot(left, right, terms=2):
     return mm(jnp.concatenate([left] * terms, axis=1), jnp.concatenate(split(right, terms), axis=0))
 
 
@@ -112,9 +110,10 @@
             rows[number, detectors * k:detectors * (k + 1), :] = ref[:, k * SB:(k + 1) * SB].astype(f32)
         return rows[number]
 
-    base = by_block(3, base_ref)
-    wide = iota((128, 128), 1)
-    bound = count_up_to(base, wide.astype(f32))
+    by_block(3, base_ref)
+    filled = -(-count // 8) * 8
+    bound = count_up_to(rows[3, 0:filled, :], iota((filled, 128), 1).astype(f32))
+    bound = jnp.concatenate([bound, jnp.zeros((128 - filled, 128), i32)], axis=0)
     member = (iota((8, 128), 1) & 1) == iota((8, 128), 0)
     member = (member & (iota((8, 128), 1) < count)).astype(f32).astype(bf16)
     bounds = mm(member, bound.astype(f32).astype(bf16))
@@ -327,7 +326,7 @@
     prefix = right_hot(stacked, upper(), apart=True)
     binned = [between(at_ends(prefix[n * slots:(n + 1) * slots], ends), 128) for n in range(7)]
     binned.append(weight * between(ends.astype(f32), 128))
-    sums = left_hot(same, jnp.concatenate(binned, axis=1), apart=True)
+    sums = left_hot(same, jnp.concatenate(binned, axis=1))
     sums = [sums[:, 128 * n:128 * (n + 1)] for n in range(8)]
     inverse = cofactors([sums[7], sums[3], sums[4], sums[5], sums[6], sums[7] - sums[5]])
     for number, values in enumerate(inverse):

time: 48.6 us -> 48.7 us (level)
  no operation moved by 1% of the time
where the time goes in v16:
time: 48.7 us; the launch traced here: 48.4 us
  blocking collectives  40.6 us (83%)
  Pallas kernels  7.16 us (15%)
  between operations  0.64 us (1%)
    all_to_all x4, blocking collectives, send_out(): lax.all_to_all(rows, AXES, split_axis=0, concat_axis=0, tiled=True, axis_...  40.6 us
    pallas_call x1, Pallas kernels, on_device(): pl.pallas_call(functools.partial(setup_kernel, owners, capacity), out_sha...  2.46 us
    pallas_call x1, Pallas kernels, on_device(): pl.pallas_call(functools.partial(pack_kernel, owners, capacity), out_shap...  1.7 us
    pallas_call x1, Pallas kernels, on_device(): pl.pallas_call(functools.partial(second_kernel, capacity), out_shape=(jax...  1.17 us
    pallas_call x1, Pallas kernels, on_device(): pl.pallas_call(functools.partial(first_kernel, capacity), out_shape=(vect...  1.09 us

profile of v16, /device:TPU:0, one launch (start us, length us, event | category | flops | bytes accessed | tf_op | source)
XLA Modules:
  0.0 48.4 jit_solution(3806240916131218340)
XLA Ops:
  0.6 1.7 %pack.1 = f32[400,128]{1,0:T(8,128)S(1)} custom-call(f32[2,6400]{1,0:T(2,128)} %tod_hbm.1, f32[2,6400]{1,0:T(2,128)} %angle_hbm.1, s32[2,6400]{1,0:T(2,128)} %pixel_hbm.1, s32[2,6400]{1,0:T(2,128)} %base_hbm.1, s32[2,50]{1,0:T(2,128)} %bitcast.5, s32[2,50]{1,0:T(2,128)} %tile_hbm.1, f32[2]{0:T(128)} %weight_hbm.1), custom_call_target="tpu_custom_call" | custom-call | tf_op jit(solution)/shard_map/pack/pallas_call | solution.py:434
  2.3 13.9 %all_to_all.20 = f32[16,25,1,128]{3,2,1,0:T(1,128)S(1)} all-to-all(f32[16,25,1,128]{3,2,1,0:T(1,128)S(1)} %bitcast.4), channel_id=1, replica_groups={{4,5,6,7,0,1,2,3,8,9,10,11,12,13,14,15},{20,21,22,23,16,17,18,19,24,25,..., dimensions={0} | all-to-all | bytes 409600 | tf_op jit(solution)/shard_map/all_to_all | solution.py:422
  16.3 2.5 %setup.1 = (f32[16,8,128]{2,1,0:T(8,128)S(1)}, s32[128,128]{1,0:T(8,128)S(1)}, s32[128,128]{1,0:T(8,128)S(1)}, s32[128,128]{1,0:T(8,128)S(1)}, f32[128,128]{1,0:...) custom-call(f32[400,128]{1,0:T(8,128)S(1)} %bitcast.3), custom_call_target="tpu_custom_call" | custom-call | tf_op jit(solution)/shard_map/setup/pallas_call | solution.py:457
  18.7 9.6 %all_to_all.21.recv_ref = f32[16,8,128]{2,1,0:T(8,128)S(1)} all-to-all(f32[16,8,128]{2,1,0:T(8,128)S(1)} %get-tuple-element.21), channel_id=1, replica_groups={{4,5,6,7,0,1,2,3,8,9,10,11,12,13,14,15},{20,21,22,23,16,17,18,19,24,25,..., dimensions={0} | all-to-all | bytes 131072 | tf_op jit(solution)/shard_map/all_to_all | solution.py:422
  28.3 1.1 %first.1 = (f32[8,128]{1,0:T(8,128)S(1)}, f32[8,128]{1,0:T(8,128)S(1)}, f32[16,8,128]{2,1,0:T(8,128)S(1)}) custom-call(f32[16,8,128]{2,1,0:T(8,128)S(1)} %all_to_all.21.recv_ref, s32[128,128]{1,0:T(8,128)S(1)} %get-tuple-element.22.refs_0_, s32[128,128]{1,0:T(8,128)S(1)} %get-tuple-element.23.refs_1_, s32[128,128]{1,0:T(8,128)S(1)} %get-tuple-element.24.refs_2_, ...), custom_call_target="tpu_custom_call" | custom-call | tf_op jit(solution)/shard_map/first/pallas_call | solution.py:468
  29.4 8.6 %all_to_all.22.recv_ref = f32[16,8,128]{2,1,0:T(8,128)S(1)} all-to-all(f32[16,8,128]{2,1,0:T(8,128)S(1)} %get-tuple-element.34), channel_id=1, replica_groups={{4,5,6,7,0,1,2,3,8,9,10,11,12,13,14,15},{20,21,22,23,16,17,18,19,24,25,..., dimensions={0} | all-to-all | bytes 131072 | tf_op jit(solution)/shard_map/all_to_all | solution.py:422
  38.0 1.2 %second.1 = (f32[8,128]{1,0:T(8,128)S(1)}, f32[16,1,128]{2,1,0:T(1,128)S(1)}) custom-call(f32[16,8,128]{2,1,0:T(8,128)S(1)} %all_to_all.22.recv_ref, f32[8,128]{1,0:T(8,128)S(1)} %get-tuple-element.35.right_ref, f32[8,128]{1,0:T(8,128)S(1)} %get-tuple-element.36.share_ref, f32[8,128]{1,0:T(8,128)S(1)} %get-tuple-element.37.rank_ref, ...), custom_call_target="tpu_custom_call" | custom-call | tf_op jit(solution)/shard_map/second/pallas_call | solution.py:476
  39.2 8.5 %all_to_all.23.recv_ref = f32[16,1,128]{2,1,0:T(1,128)S(1)} all-to-all(f32[16,1,128]{2,1,0:T(1,128)S(1)} %get-tuple-element.39), channel_id=1, replica_groups={{4,5,6,7,0,1,2,3,8,9,10,11,12,13,14,15},{20,21,22,23,16,17,18,19,24,25,..., dimensions={0} | all-to-all | bytes 16384 | tf_op jit(solution)/shard_map/all_to_all | solution.py:422
  47.6 0.7 %finish.1 = (f32[2,32]{1,0:T(2,128)}, f32[2,32]{1,0:T(2,128)}) custom-call(f32[8,128]{1,0:T(8,128)S(1)} %get-tuple-element.38.own_ref, f32[16,1,128]{2,1,0:T(1,128)S(1)} %all_to_all.23.recv_ref), custom_call_target="tpu_custom_call" | custom-call | tf_op jit(solution)/shard_map/finish/pallas_call | solution.py:485

commit v17 on v16

--- a/solution.py
+++ b/solution.py
@@ -50,7 +50,9 @@
     return jnp.dot(left, right, preferred_element_type=f32)
 
 
-def left_hot(left, right, terms=2):
+def left_hot(left, right, terms=2, apart=False):
+    if apart:
+        return sum(mm(left, term) for term in reversed(split(right, terms)))
     return mm(jnp.concatenate([left] * terms, axis=1), jnp.concatenate(split(right, terms), axis=0))
 
 
@@ -326,7 +328,7 @@
     prefix = right_hot(stacked, upper(), apart=True)
     binned = [between(at_ends(prefix[n * slots:(n + 1) * slots], ends), 128) for n in range(7)]
     binned.append(weight * between(ends.astype(f32), 128))
-    sums = left_hot(same, jnp.concatenate(binned, axis=1))
+    sums = left_hot(same, jnp.concatenate(binned, axis=1), apart=True)
     sums = [sums[:, 128 * n:128 * (n + 1)] for n in range(8)]
     inverse = cofactors([sums[7], sums[3], sums[4], sums[5], sums[6], sums[7] - sums[5]])
     for number, values in enumerate(inverse):

time: 48.7 us -> 48.6 us (level)
  no operation moved by 1% of the time
where the time goes in v17:
time: 48.6 us; the launch traced here: 48.3 us
  blocking collectives  40.6 us (84%)
  Pallas kernels  7.07 us (15%)
  between operations  0.64 us (1%)
    all_to_all x4, blocking collectives, send_out(): lax.all_to_all(rows, AXES, split_axis=0, concat_axis=0, tiled=True, axis_...  40.6 us
    pallas_call x1, Pallas kernels, on_device(): pl.pallas_call(functools.partial(setup_kernel, owners, capacity), out_sha...  2.37 us
    pallas_call x1, Pallas kernels, on_device(): pl.pallas_call(functools.partial(pack_kernel, owners, capacity), out_shap...  1.7 us
    pallas_call x1, Pallas kernels, on_device(): pl.pallas_call(functools.partial(second_kernel, capacity), out_shape=(jax...  1.17 us
    pallas_call x1, Pallas kernels, on_device(): pl.pallas_call(functools.partial(first_kernel, capacity), out_shape=(vect...  1.09 us

profile of v17, /device:TPU:0, one launch (start us, length us, event | category | flops | bytes accessed | tf_op | source)
XLA Modules:
  0.0 48.3 jit_solution(804243273073507014)
XLA Ops:
  0.6 1.7 %pack.1 = f32[400,128]{1,0:T(8,128)S(1)} custom-call(f32[2,6400]{1,0:T(2,128)} %tod_hbm.1, f32[2,6400]{1,0:T(2,128)} %angle_hbm.1, s32[2,6400]{1,0:T(2,128)} %pixel_hbm.1, s32[2,6400]{1,0:T(2,128)} %base_hbm.1, s32[2,50]{1,0:T(2,128)} %bitcast.5, s32[2,50]{1,0:T(2,128)} %tile_hbm.1, f32[2]{0:T(128)} %weight_hbm.1), custom_call_target="tpu_custom_call" | custom-call | tf_op jit(solution)/shard_map/pack/pallas_call | solution.py:436
  2.3 13.9 %all_to_all.20 = f32[16,25,1,128]{3,2,1,0:T(1,128)S(1)} all-to-all(f32[16,25,1,128]{3,2,1,0:T(1,128)S(1)} %bitcast.4), channel_id=1, replica_groups={{4,5,6,7,0,1,2,3,8,9,10,11,12,13,14,15},{20,21,22,23,16,17,18,19,24,25,..., dimensions={0} | all-to-all | bytes 409600 | tf_op jit(solution)/shard_map/all_to_all | solution.py:424
  16.3 2.4 %setup.1 = (f32[16,8,128]{2,1,0:T(8,128)S(1)}, s32[128,128]{1,0:T(8,128)S(1)}, s32[128,128]{1,0:T(8,128)S(1)}, s32[128,128]{1,0:T(8,128)S(1)}, f32[128,128]{1,0:...) custom-call(f32[400,128]{1,0:T(8,128)S(1)} %bitcast.3), custom_call_target="tpu_custom_call" | custom-call | tf_op jit(solution)/shard_map/setup/pallas_call | solution.py:459
  18.6 9.6 %all_to_all.21.recv_ref = f32[16,8,128]{2,1,0:T(8,128)S(1)} all-to-all(f32[16,8,128]{2,1,0:T(8,128)S(1)} %get-tuple-element.21), channel_id=1, replica_groups={{4,5,6,7,0,1,2,3,8,9,10,11,12,13,14,15},{20,21,22,23,16,17,18,19,24,25,..., dimensions={0} | all-to-all | bytes 131072 | tf_op jit(solution)/shard_map/all_to_all | solution.py:424
  28.2 1.1 %first.1 = (f32[8,128]{1,0:T(8,128)S(1)}, f32[8,128]{1,0:T(8,128)S(1)}, f32[16,8,128]{2,1,0:T(8,128)S(1)}) custom-call(f32[16,8,128]{2,1,0:T(8,128)S(1)} %all_to_all.21.recv_ref, s32[128,128]{1,0:T(8,128)S(1)} %get-tuple-element.22.refs_0_, s32[128,128]{1,0:T(8,128)S(1)} %get-tuple-element.23.refs_1_, s32[128,128]{1,0:T(8,128)S(1)} %get-tuple-element.24.refs_2_, ...), custom_call_target="tpu_custom_call" | custom-call | tf_op jit(solution)/shard_map/first/pallas_call | solution.py:470
  29.3 8.6 %all_to_all.22.recv_ref = f32[16,8,128]{2,1,0:T(8,128)S(1)} all-to-all(f32[16,8,128]{2,1,0:T(8,128)S(1)} %get-tuple-element.34), channel_id=1, replica_groups={{4,5,6,7,0,1,2,3,8,9,10,11,12,13,14,15},{20,21,22,23,16,17,18,19,24,25,..., dimensions={0} | all-to-all | bytes 131072 | tf_op jit(solution)/shard_map/all_to_all | solution.py:424
  37.9 1.2 %second.1 = (f32[8,128]{1,0:T(8,128)S(1)}, f32[16,1,128]{2,1,0:T(1,128)S(1)}) custom-call(f32[16,8,128]{2,1,0:T(8,128)S(1)} %all_to_all.22.recv_ref, f32[8,128]{1,0:T(8,128)S(1)} %get-tuple-element.35.right_ref, f32[8,128]{1,0:T(8,128)S(1)} %get-tuple-element.36.share_ref, f32[8,128]{1,0:T(8,128)S(1)} %get-tuple-element.37.rank_ref, ...), custom_call_target="tpu_custom_call" | custom-call | tf_op jit(solution)/shard_map/second/pallas_call | solution.py:478
  39.1 8.5 %all_to_all.23.recv_ref = f32[16,1,128]{2,1,0:T(1,128)S(1)} all-to-all(f32[16,1,128]{2,1,0:T(1,128)S(1)} %get-tuple-element.39), channel_id=1, replica_groups={{4,5,6,7,0,1,2,3,8,9,10,11,12,13,14,15},{20,21,22,23,16,17,18,19,24,25,..., dimensions={0} | all-to-all | bytes 16384 | tf_op jit(solution)/shard_map/all_to_all | solution.py:424
  47.5 0.7 %finish.1 = (f32[2,32]{1,0:T(2,128)}, f32[2,32]{1,0:T(2,128)}) custom-call(f32[8,128]{1,0:T(8,128)S(1)} %get-tuple-element.38.own_ref, f32[16,1,128]{2,1,0:T(1,128)S(1)} %all_to_all.23.recv_ref), custom_call_target="tpu_custom_call" | custom-call | tf_op jit(solution)/shard_map/finish/pallas_call | solution.py:487

commit v18 on v16

--- a/solution.py
+++ b/solution.py
@@ -90,12 +90,12 @@
 
 def pack_kernel(owners, capacity, tod_hbm, angle_hbm, pixel_hbm, base_hbm, owner_hbm, tile_hbm, weight_hbm,
                 out_ref, tod_ref, angle_ref, pixel_ref, base_ref, owner_ref, tile_ref, weight_ref, rows, small, arrived):
-    pairs = ((base_hbm, base_ref), (owner_hbm, owner_ref), (tile_hbm, tile_ref), (weight_hbm, weight_ref),
-             (tod_hbm, tod_ref), (angle_hbm, angle_ref), (pixel_hbm, pixel_ref))
+    pairs = ((base_hbm, base_ref), (owner_hbm, owner_ref), (tile_hbm, tile_ref), (tod_hbm, tod_ref),
+             (angle_hbm, angle_ref), (pixel_hbm, pixel_ref), (weight_hbm, weight_ref))
     copies = [pltpu.make_async_copy(source, into, arrived.at[n]) for n, (source, into) in enumerate(pairs)]
     for copy in copies:
         copy.start()
-    for copy in copies:
+    for copy in copies[:-1]:
         copy.wait()
     detectors, samples = tod_ref.shape
     blocks = samples // SB
@@ -141,18 +141,19 @@
     lane16 = iota((owners, 128), 1)
     facts = jnp.where(lane16 < NBASE, bounds[0:1], facts)
     facts = jnp.where((lane16 >= NBASE) & (lane16 < 2 * NBASE), pltpu.roll(bounds, NBASE, 1)[1:2], facts)
-    facts = jnp.where(lane16 == lane_weight, weight_ref[0], facts)
-    facts = jnp.where(lane16 == lane_weight + 1, weight_ref[1], facts)
     facts = jnp.where(lane16 == lane_rank, iota((owners, 128), 0).astype(f32), facts)
-    for other in range(owners):
-        out_ref[(other + 1) * pair_rows - 1:(other + 1) * pair_rows, :] = facts[other:other + 1]
-
     for number, ref in enumerate((tod_ref, angle_ref, pixel_ref)):
         values = by_block(number, ref)
         values = left_hot(route, values, 1 if number == 2 else 3)
         for other in range(owners):
             start = other * pair_rows + number * capacity
             out_ref[start:start + capacity, :] = values[other * capacity:(other + 1) * capacity]
+
+    copies[-1].wait()
+    facts = jnp.where(lane16 == lane_weight, weight_ref[0], facts)
+    facts = jnp.where(lane16 == lane_weight + 1, weight_ref[1], facts)
+    for other in range(owners):
+        out_ref[(other + 1) * pair_rows - 1:(other + 1) * pair_rows, :] = facts[other:other + 1]
 
 
 def sort_lanes(keys):

time: 48.7 us -> 48.7 us (level)
  no operation moved by 1% of the time
where the time goes in v18:
time: 48.7 us; the launch traced here: 48.4 us
  blocking collectives  40.6 us (83%)
  Pallas kernels  7.18 us (15%)
  between operations  0.64 us (1%)
    all_to_all x4, blocking collectives, send_out(): lax.all_to_all(rows, AXES, split_axis=0, concat_axis=0, tiled=True, axis_...  40.6 us
    pallas_call x1, Pallas kernels, on_device(): pl.pallas_call(functools.partial(setup_kernel, owners, capacity), out_sha...  2.46 us
    pallas_call x1, Pallas kernels, on_device(): pl.pallas_call(functools.partial(pack_kernel, owners, capacity), out_shap...  1.71 us
    pallas_call x1, Pallas kernels, on_device(): pl.pallas_call(functools.partial(second_kernel, capacity), out_shape=(jax...  1.17 us
    pallas_call x1, Pallas kernels, on_device(): pl.pallas_call(functools.partial(first_kernel, capacity), out_shape=(vect...  1.09 us

profile of v18, /device:TPU:0, one launch (start us, length us, event | category | flops | bytes accessed | tf_op | source)
XLA Modules:
  0.0 48.4 jit_solution(12637373455956430253)
XLA Ops:
  0.6 1.7 %pack.1 = f32[400,128]{1,0:T(8,128)S(1)} custom-call(f32[2,6400]{1,0:T(2,128)} %tod_hbm.1, f32[2,6400]{1,0:T(2,128)} %angle_hbm.1, s32[2,6400]{1,0:T(2,128)} %pixel_hbm.1, s32[2,6400]{1,0:T(2,128)} %base_hbm.1, s32[2,50]{1,0:T(2,128)} %bitcast.5, s32[2,50]{1,0:T(2,128)} %tile_hbm.1, f32[2]{0:T(128)} %weight_hbm.1), custom_call_target="tpu_custom_call" | custom-call | tf_op jit(solution)/shard_map/pack/pallas_call | solution.py:435
  2.4 13.9 %all_to_all.20 = f32[16,25,1,128]{3,2,1,0:T(1,128)S(1)} all-to-all(f32[16,25,1,128]{3,2,1,0:T(1,128)S(1)} %bitcast.4), channel_id=1, replica_groups={{4,5,6,7,0,1,2,3,8,9,10,11,12,13,14,15},{20,21,22,23,16,17,18,19,24,25,..., dimensions={0} | all-to-all | bytes 409600 | tf_op jit(solution)/shard_map/all_to_all | solution.py:423
  16.3 2.5 %setup.1 = (f32[16,8,128]{2,1,0:T(8,128)S(1)}, s32[128,128]{1,0:T(8,128)S(1)}, s32[128,128]{1,0:T(8,128)S(1)}, s32[128,128]{1,0:T(8,128)S(1)}, f32[128,128]{1,0:...) custom-call(f32[400,128]{1,0:T(8,128)S(1)} %bitcast.3), custom_call_target="tpu_custom_call" | custom-call | tf_op jit(solution)/shard_map/setup/pallas_call | solution.py:458
  18.7 9.6 %all_to_all.21.recv_ref = f32[16,8,128]{2,1,0:T(8,128)S(1)} all-to-all(f32[16,8,128]{2,1,0:T(8,128)S(1)} %get-tuple-element.21), channel_id=1, replica_groups={{4,5,6,7,0,1,2,3,8,9,10,11,12,13,14,15},{20,21,22,23,16,17,18,19,24,25,..., dimensions={0} | all-to-all | bytes 131072 | tf_op jit(solution)/shard_map/all_to_all | solution.py:423
  28.3 1.1 %first.1 = (f32[8,128]{1,0:T(8,128)S(1)}, f32[8,128]{1,0:T(8,128)S(1)}, f32[16,8,128]{2,1,0:T(8,128)S(1)}) custom-call(f32[16,8,128]{2,1,0:T(8,128)S(1)} %all_to_all.21.recv_ref, s32[128,128]{1,0:T(8,128)S(1)} %get-tuple-element.22.refs_0_, s32[128,128]{1,0:T(8,128)S(1)} %get-tuple-element.23.refs_1_, s32[128,128]{1,0:T(8,128)S(1)} %get-tuple-element.24.refs_2_, ...), custom_call_target="tpu_custom_call" | custom-call | tf_op jit(solution)/shard_map/first/pallas_call | solution.py:469
  29.4 8.6 %all_to_all.22.recv_ref = f32[16,8,128]{2,1,0:T(8,128)S(1)} all-to-all(f32[16,8,128]{2,1,0:T(8,128)S(1)} %get-tuple-element.34), channel_id=1, replica_groups={{4,5,6,7,0,1,2,3,8,9,10,11,12,13,14,15},{20,21,22,23,16,17,18,19,24,25,..., dimensions={0} | all-to-all | bytes 131072 | tf_op jit(solution)/shard_map/all_to_all | solution.py:423
  38.0 1.2 %second.1 = (f32[8,128]{1,0:T(8,128)S(1)}, f32[16,1,128]{2,1,0:T(1,128)S(1)}) custom-call(f32[16,8,128]{2,1,0:T(8,128)S(1)} %all_to_all.22.recv_ref, f32[8,128]{1,0:T(8,128)S(1)} %get-tuple-element.35.right_ref, f32[8,128]{1,0:T(8,128)S(1)} %get-tuple-element.36.share_ref, f32[8,128]{1,0:T(8,128)S(1)} %get-tuple-element.37.rank_ref, ...), custom_call_target="tpu_custom_call" | custom-call | tf_op jit(solution)/shard_map/second/pallas_call | solution.py:477
  39.2 8.5 %all_to_all.23.recv_ref = f32[16,1,128]{2,1,0:T(1,128)S(1)} all-to-all(f32[16,1,128]{2,1,0:T(1,128)S(1)} %get-tuple-element.39), channel_id=1, replica_groups={{4,5,6,7,0,1,2,3,8,9,10,11,12,13,14,15},{20,21,22,23,16,17,18,19,24,25,..., dimensions={0} | all-to-all | bytes 16384 | tf_op jit(solution)/shard_map/all_to_all | solution.py:423
  47.6 0.7 %finish.1 = (f32[2,32]{1,0:T(2,128)}, f32[2,32]{1,0:T(2,128)}) custom-call(f32[8,128]{1,0:T(8,128)S(1)} %get-tuple-element.38.own_ref, f32[16,1,128]{2,1,0:T(1,128)S(1)} %all_to_all.23.recv_ref), custom_call_target="tpu_custom_call" | custom-call | tf_op jit(solution)/shard_map/finish/pallas_call | solution.py:486

commit v19 on v18

--- a/solution.py
+++ b/solution.py
@@ -414,8 +414,9 @@
 
 def places(owners, inner):
     lines = owners // inner
-    order = list(range((lines - 1) // 2, -1, -1)) + list(range((lines - 1) // 2 + 1, lines))
-    return [line * inner + other for line in order for other in range(inner)]
+    order = list(range(lines // 2, lines)) + list(range(lines // 2 - 1, -1, -1))
+    across = list(range(inner // 2, inner)) + list(range(inner // 2))
+    return [line * inner + other for line in order for other in across]
 
 
 def send_out(rows):

time: 48.7 us -> 46.9 us (0.963)
  blocking collectives: 40.6 us -> 38.7 us
    all_to_all x4, blocking collectives: 40.6 us -> 38.7 us  [send_out(): lax.all_to_all(rows, AXES, split_axis=0, concat_axis=0, tiled=True, axis_...]
where the time goes in v19:
time: 46.9 us; the launch traced here: 46.5 us
  blocking collectives  38.7 us (83%)
  Pallas kernels  7.18 us (15%)
  between operations  0.64 us (1%)
    all_to_all x4, blocking collectives, send_out(): lax.all_to_all(rows, AXES, split_axis=0, concat_axis=0, tiled=True, axis_...  38.7 us
    pallas_call x1, Pallas kernels, on_device(): pl.pallas_call(functools.partial(setup_kernel, owners, capacity), out_sha...  2.46 us
    pallas_call x1, Pallas kernels, on_device(): pl.pallas_call(functools.partial(pack_kernel, owners, capacity), out_shap...  1.71 us
    pallas_call x1, Pallas kernels, on_device(): pl.pallas_call(functools.partial(second_kernel, capacity), out_shape=(jax...  1.17 us
    pallas_call x1, Pallas kernels, on_device(): pl.pallas_call(functools.partial(first_kernel, capacity), out_shape=(vect...  1.09 us

profile of v19, /device:TPU:0, one launch (start us, length us, event | category | flops | bytes accessed | tf_op | source)
XLA Modules:
  0.0 46.5 jit_solution(3091435173953809189)
XLA Ops:
  0.6 1.7 %pack.1 = f32[400,128]{1,0:T(8,128)S(1)} custom-call(f32[2,6400]{1,0:T(2,128)} %tod_hbm.1, f32[2,6400]{1,0:T(2,128)} %angle_hbm.1, s32[2,6400]{1,0:T(2,128)} %pixel_hbm.1, s32[2,6400]{1,0:T(2,128)} %base_hbm.1, s32[2,50]{1,0:T(2,128)} %bitcast.5, s32[2,50]{1,0:T(2,128)} %tile_hbm.1, f32[2]{0:T(128)} %weight_hbm.1), custom_call_target="tpu_custom_call" | custom-call | tf_op jit(solution)/shard_map/pack/pallas_call | solution.py:436
  2.4 13.4 %all_to_all.20 = f32[16,25,1,128]{3,2,1,0:T(1,128)S(1)} all-to-all(f32[16,25,1,128]{3,2,1,0:T(1,128)S(1)} %bitcast.4), channel_id=1, replica_groups={{10,11,8,9,14,15,12,13,6,7,4,5,2,3,0,1},{26,27,24,25,30,31,28,29,22,23,..., dimensions={0} | all-to-all | bytes 409600 | tf_op jit(solution)/shard_map/all_to_all | solution.py:424
  15.7 2.5 %setup.1 = (f32[16,8,128]{2,1,0:T(8,128)S(1)}, s32[128,128]{1,0:T(8,128)S(1)}, s32[128,128]{1,0:T(8,128)S(1)}, s32[128,128]{1,0:T(8,128)S(1)}, f32[128,128]{1,0:...) custom-call(f32[400,128]{1,0:T(8,128)S(1)} %bitcast.3), custom_call_target="tpu_custom_call" | custom-call | tf_op jit(solution)/shard_map/setup/pallas_call | solution.py:459
  18.2 8.4 %all_to_all.21.recv_ref = f32[16,8,128]{2,1,0:T(8,128)S(1)} all-to-all(f32[16,8,128]{2,1,0:T(8,128)S(1)} %get-tuple-element.21), channel_id=1, replica_groups={{10,11,8,9,14,15,12,13,6,7,4,5,2,3,0,1},{26,27,24,25,30,31,28,29,22,23,..., dimensions={0} | all-to-all | bytes 131072 | tf_op jit(solution)/shard_map/all_to_all | solution.py:424
  26.6 1.1 %first.1 = (f32[8,128]{1,0:T(8,128)S(1)}, f32[8,128]{1,0:T(8,128)S(1)}, f32[16,8,128]{2,1,0:T(8,128)S(1)}) custom-call(f32[16,8,128]{2,1,0:T(8,128)S(1)} %all_to_all.21.recv_ref, s32[128,128]{1,0:T(8,128)S(1)} %get-tuple-element.22.refs_0_, s32[128,128]{1,0:T(8,128)S(1)} %get-tuple-element.23.refs_1_, s32[128,128]{1,0:T(8,128)S(1)} %get-tuple-element.24.refs_2_, ...), custom_call_target="tpu_custom_call" | custom-call | tf_op jit(solution)/shard_map/first/pallas_call | solution.py:470
  27.7 8.6 %all_to_all.22.recv_ref = f32[16,8,128]{2,1,0:T(8,128)S(1)} all-to-all(f32[16,8,128]{2,1,0:T(8,128)S(1)} %get-tuple-element.34), channel_id=1, replica_groups={{10,11,8,9,14,15,12,13,6,7,4,5,2,3,0,1},{26,27,24,25,30,31,28,29,22,23,..., dimensions={0} | all-to-all | bytes 131072 | tf_op jit(solution)/shard_map/all_to_all | solution.py:424
  36.2 1.2 %second.1 = (f32[8,128]{1,0:T(8,128)S(1)}, f32[16,1,128]{2,1,0:T(1,128)S(1)}) custom-call(f32[16,8,128]{2,1,0:T(8,128)S(1)} %all_to_all.22.recv_ref, f32[8,128]{1,0:T(8,128)S(1)} %get-tuple-element.35.right_ref, f32[8,128]{1,0:T(8,128)S(1)} %get-tuple-element.36.share_ref, f32[8,128]{1,0:T(8,128)S(1)} %get-tuple-element.37.rank_ref, ...), custom_call_target="tpu_custom_call" | custom-call | tf_op jit(solution)/shard_map/second/pallas_call | solution.py:478
  37.4 8.4 %all_to_all.23.recv_ref = f32[16,1,128]{2,1,0:T(1,128)S(1)} all-to-all(f32[16,1,128]{2,1,0:T(1,128)S(1)} %get-tuple-element.39), channel_id=1, replica_groups={{10,11,8,9,14,15,12,13,6,7,4,5,2,3,0,1},{26,27,24,25,30,31,28,29,22,23,..., dimensions={0} | all-to-all | bytes 16384 | tf_op jit(solution)/shard_map/all_to_all | solution.py:424
  45.8 0.7 %finish.1 = (f32[2,32]{1,0:T(2,128)}, f32[2,32]{1,0:T(2,128)}) custom-call(f32[8,128]{1,0:T(8,128)S(1)} %get-tuple-element.38.own_ref, f32[16,1,128]{2,1,0:T(1,128)S(1)} %all_to_all.23.recv_ref), custom_call_target="tpu_custom_call" | custom-call | tf_op jit(solution)/shard_map/finish/pallas_call | solution.py:487

commit v20 on v19

--- a/solution.py
+++ b/solution.py
@@ -299,13 +299,6 @@
     bounds = jnp.where(((lane >> 5) == group) & (tile >= 0), bounds, 0)
     bounds_ref[...] = bounds
 
-    base = jnp.zeros((slots, 128), i32)
-    moment = start + lane
-    for step in (16, 8, 4, 2, 1):
-        base = base + jnp.where(lanes_at(facts, base + (first + (step - 1))) <= moment, step, 0)
-    base = base + (group << 5)
-    base_ref[...] = base
-
     keys = sort_lanes(pixel_f * 128.0 + lane.astype(f32))
     order = keys.astype(i32) & 127
     limit = lane.astype(f32) * 128.0 + 127.0
@@ -314,7 +307,6 @@
         ends = ends + jnp.where(lanes_at(keys, ends + (step - 1)) <= limit, step, 0)
     ends = ends + jnp.where(lanes_at(keys, ends) <= limit, 1, 0)
     ends_ref[...] = ends
-    sbase_ref[...] = lanes_at(base, order)
     scos = lanes_at(cosine, order)
     ssin = lanes_at(sine, order)
     wtod = weight * lanes_at(tod, order)
@@ -334,6 +326,14 @@
         inv_ref[number] = values
     part = map_to_baselines(capacity, sums[0:3], inverse, tod, pixel, cosine, sine, weight, bounds)
     part_ref[...] = jnp.broadcast_to(part[None], part_ref.shape)
+
+    base = jnp.zeros((slots, 128), i32)
+    moment = start + lane
+    for step in (16, 8, 4, 2, 1):
+        base = base + jnp.where(lanes_at(facts, base + (first + (step - 1))) <= moment, step, 0)
+    base = base + (group << 5)
+    base_ref[...] = base
+    sbase_ref[...] = lanes_at(base, order)
 
 
 def apply(capacity, vector, base_ref, sbase_ref, pixel_ref, cos_ref, sin_ref, scos_ref, ssin_ref,

time: 46.9 us -> 46.8 us (level)
  no operation moved by 1% of the time
where the time goes in v20:
time: 46.8 us; the launch traced here: 46.5 us
  blocking collectives  38.7 us (83%)
  Pallas kernels  7.12 us (15%)
  between operations  0.64 us (1%)
    all_to_all x4, blocking collectives, send_out(): lax.all_to_all(rows, AXES, split_axis=0, concat_axis=0, tiled=True, axis_...  38.7 us
    pallas_call x1, Pallas kernels, on_device(): pl.pallas_call(functools.partial(setup_kernel, owners, capacity), out_sha...  2.4 us
    pallas_call x1, Pallas kernels, on_device(): pl.pallas_call(functools.partial(pack_kernel, owners, capacity), out_shap...  1.71 us
    pallas_call x1, Pallas kernels, on_device(): pl.pallas_call(functools.partial(second_kernel, capacity), out_shape=(jax...  1.17 us
    pallas_call x1, Pallas kernels, on_device(): pl.pallas_call(functools.partial(first_kernel, capacity), out_shape=(vect...  1.09 us

profile of v20, /device:TPU:0, one launch (start us, length us, event | category | flops | bytes accessed | tf_op | source)
XLA Modules:
  0.0 46.5 jit_solution(15514817540024195453)
XLA Ops:
  0.6 1.7 %pack.1 = f32[400,128]{1,0:T(8,128)S(1)} custom-call(f32[2,6400]{1,0:T(2,128)} %tod_hbm.1, f32[2,6400]{1,0:T(2,128)} %angle_hbm.1, s32[2,6400]{1,0:T(2,128)} %pixel_hbm.1, s32[2,6400]{1,0:T(2,128)} %base_hbm.1, s32[2,50]{1,0:T(2,128)} %bitcast.5, s32[2,50]{1,0:T(2,128)} %tile_hbm.1, f32[2]{0:T(128)} %weight_hbm.1), custom_call_target="tpu_custom_call" | custom-call | tf_op jit(solution)/shard_map/pack/pallas_call | solution.py:436
  2.4 13.4 %all_to_all.20 = f32[16,25,1,128]{3,2,1,0:T(1,128)S(1)} all-to-all(f32[16,25,1,128]{3,2,1,0:T(1,128)S(1)} %bitcast.4), channel_id=1, replica_groups={{10,11,8,9,14,15,12,13,6,7,4,5,2,3,0,1},{26,27,24,25,30,31,28,29,22,23,..., dimensions={0} | all-to-all | bytes 409600 | tf_op jit(solution)/shard_map/all_to_all | solution.py:424
  15.7 2.4 %setup.1 = (f32[16,8,128]{2,1,0:T(8,128)S(1)}, s32[128,128]{1,0:T(8,128)S(1)}, s32[128,128]{1,0:T(8,128)S(1)}, s32[128,128]{1,0:T(8,128)S(1)}, f32[128,128]{1,0:...) custom-call(f32[400,128]{1,0:T(8,128)S(1)} %bitcast.3), custom_call_target="tpu_custom_call" | custom-call | tf_op jit(solution)/shard_map/setup/pallas_call | solution.py:459
  18.1 8.4 %all_to_all.21.recv_ref = f32[16,8,128]{2,1,0:T(8,128)S(1)} all-to-all(f32[16,8,128]{2,1,0:T(8,128)S(1)} %get-tuple-element.21), channel_id=1, replica_groups={{10,11,8,9,14,15,12,13,6,7,4,5,2,3,0,1},{26,27,24,25,30,31,28,29,22,23,..., dimensions={0} | all-to-all | bytes 131072 | tf_op jit(solution)/shard_map/all_to_all | solution.py:424
  26.5 1.1 %first.1 = (f32[8,128]{1,0:T(8,128)S(1)}, f32[8,128]{1,0:T(8,128)S(1)}, f32[16,8,128]{2,1,0:T(8,128)S(1)}) custom-call(f32[16,8,128]{2,1,0:T(8,128)S(1)} %all_to_all.21.recv_ref, s32[128,128]{1,0:T(8,128)S(1)} %get-tuple-element.22.refs_0_, s32[128,128]{1,0:T(8,128)S(1)} %get-tuple-element.23.refs_1_, s32[128,128]{1,0:T(8,128)S(1)} %get-tuple-element.24.refs_2_, ...), custom_call_target="tpu_custom_call" | custom-call | tf_op jit(solution)/shard_map/first/pallas_call | solution.py:470
  27.6 8.6 %all_to_all.22.recv_ref = f32[16,8,128]{2,1,0:T(8,128)S(1)} all-to-all(f32[16,8,128]{2,1,0:T(8,128)S(1)} %get-tuple-element.34), channel_id=1, replica_groups={{10,11,8,9,14,15,12,13,6,7,4,5,2,3,0,1},{26,27,24,25,30,31,28,29,22,23,..., dimensions={0} | all-to-all | bytes 131072 | tf_op jit(solution)/shard_map/all_to_all | solution.py:424
  36.2 1.2 %second.1 = (f32[8,128]{1,0:T(8,128)S(1)}, f32[16,1,128]{2,1,0:T(1,128)S(1)}) custom-call(f32[16,8,128]{2,1,0:T(8,128)S(1)} %all_to_all.22.recv_ref, f32[8,128]{1,0:T(8,128)S(1)} %get-tuple-element.35.right_ref, f32[8,128]{1,0:T(8,128)S(1)} %get-tuple-element.36.share_ref, f32[8,128]{1,0:T(8,128)S(1)} %get-tuple-element.37.rank_ref, ...), custom_call_target="tpu_custom_call" | custom-call | tf_op jit(solution)/shard_map/second/pallas_call | solution.py:478
  37.3 8.4 %all_to_all.23.recv_ref = f32[16,1,128]{2,1,0:T(1,128)S(1)} all-to-all(f32[16,1,128]{2,1,0:T(1,128)S(1)} %get-tuple-element.39), channel_id=1, replica_groups={{10,11,8,9,14,15,12,13,6,7,4,5,2,3,0,1},{26,27,24,25,30,31,28,29,22,23,..., dimensions={0} | all-to-all | bytes 16384 | tf_op jit(solution)/shard_map/all_to_all | solution.py:424
  45.7 0.7 %finish.1 = (f32[2,32]{1,0:T(2,128)}, f32[2,32]{1,0:T(2,128)}) custom-call(f32[8,128]{1,0:T(8,128)S(1)} %get-tuple-element.38.own_ref, f32[16,1,128]{2,1,0:T(1,128)S(1)} %all_to_all.23.recv_ref), custom_call_target="tpu_custom_call" | custom-call | tf_op jit(solution)/shard_map/finish/pallas_call | solution.py:487

commit v21 on v20

--- a/solution.py
+++ b/solution.py
@@ -50,7 +50,9 @@
     return jnp.dot(left, right, preferred_element_type=f32)
 
 
-def left_hot(left, right, terms=2):
+def left_hot(left, right, terms=2, apart=False):
+    if apart:
+        return sum(mm(left, term) for term in reversed(split(right, terms)))
     return mm(jnp.concatenate([left] * terms, axis=1), jnp.concatenate(split(right, terms), axis=0))
 
 
@@ -319,7 +321,7 @@
     prefix = right_hot(stacked, upper(), apart=True)
     binned = [between(at_ends(prefix[n * slots:(n + 1) * slots], ends), 128) for n in range(7)]
     binned.append(weight * between(ends.astype(f32), 128))
-    sums = left_hot(same, jnp.concatenate(binned, axis=1))
+    sums = left_hot(same, jnp.concatenate(binned, axis=1), apart=True)
     sums = [sums[:, 128 * n:128 * (n + 1)] for n in range(8)]
     inverse = cofactors([sums[7], sums[3], sums[4], sums[5], sums[6], sums[7] - sums[5]])
     for number, values in enumerate(inverse):

time: 46.8 us -> 46.8 us (level)
  no operation moved by 1% of the time
where the time goes in v21:
time: 46.8 us; the launch traced here: 46.5 us
  blocking collectives  38.7 us (83%)
  Pallas kernels  7.12 us (15%)
  between operations  0.64 us (1%)
    all_to_all x4, blocking collectives, send_out(): lax.all_to_all(rows, AXES, split_axis=0, concat_axis=0, tiled=True, axis_...  38.7 us
    pallas_call x1, Pallas kernels, on_device(): pl.pallas_call(functools.partial(setup_kernel, owners, capacity), out_sha...  2.4 us
    pallas_call x1, Pallas kernels, on_device(): pl.pallas_call(functools.partial(pack_kernel, owners, capacity), out_shap...  1.71 us
    pallas_call x1, Pallas kernels, on_device(): pl.pallas_call(functools.partial(second_kernel, capacity), out_shape=(jax...  1.17 us
    pallas_call x1, Pallas kernels, on_device(): pl.pallas_call(functools.partial(first_kernel, capacity), out_shape=(vect...  1.09 us

profile of v21, /device:TPU:0, one launch (start us, length us, event | category | flops | bytes accessed | tf_op | source)
XLA Modules:
  0.0 46.5 jit_solution(18162908532584710915)
XLA Ops:
  0.6 1.7 %pack.1 = f32[400,128]{1,0:T(8,128)S(1)} custom-call(f32[2,6400]{1,0:T(2,128)} %tod_hbm.1, f32[2,6400]{1,0:T(2,128)} %angle_hbm.1, s32[2,6400]{1,0:T(2,128)} %pixel_hbm.1, s32[2,6400]{1,0:T(2,128)} %base_hbm.1, s32[2,50]{1,0:T(2,128)} %bitcast.5, s32[2,50]{1,0:T(2,128)} %tile_hbm.1, f32[2]{0:T(128)} %weight_hbm.1), custom_call_target="tpu_custom_call" | custom-call | tf_op jit(solution)/shard_map/pack/pallas_call | solution.py:438
  2.4 13.4 %all_to_all.20 = f32[16,25,1,128]{3,2,1,0:T(1,128)S(1)} all-to-all(f32[16,25,1,128]{3,2,1,0:T(1,128)S(1)} %bitcast.4), channel_id=1, replica_groups={{10,11,8,9,14,15,12,13,6,7,4,5,2,3,0,1},{26,27,24,25,30,31,28,29,22,23,..., dimensions={0} | all-to-all | bytes 409600 | tf_op jit(solution)/shard_map/all_to_all | solution.py:426
  15.7 2.4 %setup.1 = (f32[16,8,128]{2,1,0:T(8,128)S(1)}, s32[128,128]{1,0:T(8,128)S(1)}, s32[128,128]{1,0:T(8,128)S(1)}, s32[128,128]{1,0:T(8,128)S(1)}, f32[128,128]{1,0:...) custom-call(f32[400,128]{1,0:T(8,128)S(1)} %bitcast.3), custom_call_target="tpu_custom_call" | custom-call | tf_op jit(solution)/shard_map/setup/pallas_call | solution.py:461
  18.1 8.4 %all_to_all.21.recv_ref = f32[16,8,128]{2,1,0:T(8,128)S(1)} all-to-all(f32[16,8,128]{2,1,0:T(8,128)S(1)} %get-tuple-element.21), channel_id=1, replica_groups={{10,11,8,9,14,15,12,13,6,7,4,5,2,3,0,1},{26,27,24,25,30,31,28,29,22,23,..., dimensions={0} | all-to-all | bytes 131072 | tf_op jit(solution)/shard_map/all_to_all | solution.py:426
  26.5 1.1 %first.1 = (f32[8,128]{1,0:T(8,128)S(1)}, f32[8,128]{1,0:T(8,128)S(1)}, f32[16,8,128]{2,1,0:T(8,128)S(1)}) custom-call(f32[16,8,128]{2,1,0:T(8,128)S(1)} %all_to_all.21.recv_ref, s32[128,128]{1,0:T(8,128)S(1)} %get-tuple-element.22.refs_0_, s32[128,128]{1,0:T(8,128)S(1)} %get-tuple-element.23.refs_1_, s32[128,128]{1,0:T(8,128)S(1)} %get-tuple-element.24.refs_2_, ...), custom_call_target="tpu_custom_call" | custom-call | tf_op jit(solution)/shard_map/first/pallas_call | solution.py:472
  27.6 8.6 %all_to_all.22.recv_ref = f32[16,8,128]{2,1,0:T(8,128)S(1)} all-to-all(f32[16,8,128]{2,1,0:T(8,128)S(1)} %get-tuple-element.34), channel_id=1, replica_groups={{10,11,8,9,14,15,12,13,6,7,4,5,2,3,0,1},{26,27,24,25,30,31,28,29,22,23,..., dimensions={0} | all-to-all | bytes 131072 | tf_op jit(solution)/shard_map/all_to_all | solution.py:426
  36.2 1.2 %second.1 = (f32[8,128]{1,0:T(8,128)S(1)}, f32[16,1,128]{2,1,0:T(1,128)S(1)}) custom-call(f32[16,8,128]{2,1,0:T(8,128)S(1)} %all_to_all.22.recv_ref, f32[8,128]{1,0:T(8,128)S(1)} %get-tuple-element.35.right_ref, f32[8,128]{1,0:T(8,128)S(1)} %get-tuple-element.36.share_ref, f32[8,128]{1,0:T(8,128)S(1)} %get-tuple-element.37.rank_ref, ...), custom_call_target="tpu_custom_call" | custom-call | tf_op jit(solution)/shard_map/second/pallas_call | solution.py:480
  37.3 8.4 %all_to_all.23.recv_ref = f32[16,1,128]{2,1,0:T(1,128)S(1)} all-to-all(f32[16,1,128]{2,1,0:T(1,128)S(1)} %get-tuple-element.39), channel_id=1, replica_groups={{10,11,8,9,14,15,12,13,6,7,4,5,2,3,0,1},{26,27,24,25,30,31,28,29,22,23,..., dimensions={0} | all-to-all | bytes 16384 | tf_op jit(solution)/shard_map/all_to_all | solution.py:426
  45.7 0.7 %finish.1 = (f32[2,32]{1,0:T(2,128)}, f32[2,32]{1,0:T(2,128)}) custom-call(f32[8,128]{1,0:T(8,128)S(1)} %get-tuple-element.38.own_ref, f32[16,1,128]{2,1,0:T(1,128)S(1)} %all_to_all.23.recv_ref), custom_call_target="tpu_custom_call" | custom-call | tf_op jit(solution)/shard_map/finish/pallas_call | solution.py:489
